TPU v7x, 512 devices: a whole 4x8x8 slice. The times are simulated.
512 devices in a mesh: row: 16 (over y_lo, z), col: 32 (over y_hi, x, core).
Axes of the slice: x: 4, y: 8 (y_hi: 4, y_lo: 2; y = y_hi * 2 + y_lo), z: 8, core: 2. Of those that a mesh axis runs over, the one named last changes fastest.
Arguments:
- features: bfloat16 [131072, 128], P(('row', 'col')), may hold values from -16 to 16
- scales: bfloat16 [131072], P(('row', 'col')), may hold values from 0.29882812 to 3
- vectors: float32 [32, 131072], P(None, ('row', 'col')), may hold values from -4 to 4
- pattern: int32 [16, 32, 2, 128], P('row', 'col'), may hold values from 0 to 511, as said below
- counts: int32 [16, 32], P('row', 'col'), may hold values from 1 to 128
Outputs:
- product: float32 [32, 131072], P(None, ('row', 'col'))
Inputs may be any that keep to these rules, and one draw needn't show every extreme that they name: For s < counts[r, c] the pairs (pattern[r, c, 0, s], pattern[r, c, 1, s]) = (i, j) are distinct, i <= j, i // 32 = r and j % 32 = c; slots s >= counts[r, c] hold block numbers that are to be ignored.
All inputs are finite; a program needn't handle non-finite values.
Results may differ from a plain program's by a relative error of at most 0.0041.
Values may be sent and summed in bfloat16 or wider, within the bound.
No kernel may reach another device: no remote copies, remote signals or barrier semaphores. Data moves between devices by JAX's collectives and lax.ppermute only.
A program may use at most 64 MiB of HBM per device.

v0:
```python
import jax
import jax.numpy as jnp
from jax import lax
from jax.sharding import PartitionSpec as P

TILE = 256
DESC = 128
VECS = 32


tile_batch = 8


def block_side(feat_rows, scale_rows, vec_rows):
    span = feat_rows.shape[0] // TILE
    feat_wide = feat_rows.astype(jnp.float32)
    norm_rows = jnp.sum(feat_wide * feat_wide, axis=1).reshape(span, TILE)
    return (
        feat_rows.reshape(span, TILE, DESC),
        norm_rows,
        scale_rows.astype(jnp.float32).reshape(span, TILE),
        vec_rows.reshape(VECS, span, TILE),
    )


def tile_products(tile_pairs, start_slot, stop_slot, row_side, col_side, partial_sums):
    row_feat, row_norm, row_scale, row_vec = row_side
    col_feat, col_norm, col_scale, col_vec = col_side
    row_span = row_feat.shape[0]
    col_span = col_feat.shape[0]
    capacity = tile_pairs.shape[1]

    def group_step(group_index, carry):
        forward_sum, mirror_sum = carry
        slot_ids = start_slot + group_index * tile_batch + jnp.arange(tile_batch, dtype=jnp.int32)
        live_slot = slot_ids < stop_slot
        picked = jnp.clip(slot_ids, 0, capacity - 1)
        block_rows = tile_pairs[0][picked]
        block_cols = tile_pairs[1][picked]
        local_rows = block_rows % row_span
        local_cols = block_cols // row_span
        inner_dot = jnp.einsum(
            "gpd,gqd->gpq",
            row_feat[local_rows],
            col_feat[local_cols],
            preferred_element_type=jnp.float32,
        )
        exponent = (
            2.0 * inner_dot - row_norm[local_rows][:, :, None] - col_norm[local_cols][:, None, :]
        ) / DESC
        tile_block = (
            row_scale[local_rows][:, :, None]
            * col_scale[local_cols][:, None, :]
            * jnp.exp(exponent)
        ).astype(jnp.bfloat16)
        forward_part = jnp.einsum(
            "gpq,kgq->gkp", tile_block, col_vec[:, local_cols], preferred_element_type=jnp.float32
        )
        mirror_part = jnp.einsum(
            "gpq,kgp->gkq", tile_block, row_vec[:, local_rows], preferred_element_type=jnp.float32
        )
        row_hit = (
            (local_rows[:, None] == jnp.arange(row_span, dtype=jnp.int32)[None, :])
            & live_slot[:, None]
        ).astype(jnp.float32)
        mirror_live = live_slot & (block_rows != block_cols)
        col_hit = (
            (local_cols[:, None] == jnp.arange(col_span, dtype=jnp.int32)[None, :])
            & mirror_live[:, None]
        ).astype(jnp.float32)
        forward_sum = forward_sum + jnp.einsum(
            "ga,gkp->kap", row_hit, forward_part, precision=lax.Precision.HIGHEST
        )
        mirror_sum = mirror_sum + jnp.einsum(
            "gb,gkq->kbq", col_hit, mirror_part, precision=lax.Precision.HIGHEST
        )
        return (forward_sum, mirror_sum)

    groups = jnp.maximum(stop_slot - start_slot + tile_batch - 1, 0) // tile_batch
    return lax.fori_loop(0, groups, group_step, partial_sums)


def body(features, scales, vectors, pattern, counts):
    narrow = vectors.astype(jnp.bfloat16)
    row_feat, row_scale, row_vec = (
        lax.all_gather(features, "col", axis=0, tiled=True),
        lax.all_gather(scales, "col", axis=0, tiled=True),
        lax.all_gather(narrow, "col", axis=1, tiled=True),
    )
    col_feat, col_scale, col_vec = (
        lax.all_gather(features, "row", axis=0, tiled=True),
        lax.all_gather(scales, "row", axis=0, tiled=True),
        lax.all_gather(narrow, "row", axis=1, tiled=True),
    )
    row_side = block_side(row_feat, row_scale, row_vec)
    col_side = block_side(col_feat, col_scale, col_vec)
    row_span = row_side[0].shape[0]
    col_span = col_side[0].shape[0]
    tile_pairs = pattern[0, 0]
    tile_count = counts[0, 0]
    forward_zero = jnp.zeros((VECS, row_span, TILE), jnp.float32)
    mirror_zero = jnp.zeros((VECS, col_span, TILE), jnp.float32)
    forward_sum, mirror_sum = tile_products(
        tile_pairs, 0, tile_count, row_side, col_side, (forward_zero, mirror_zero)
    )
    forward = lax.psum_scatter(
        forward_sum.reshape(VECS, row_span * TILE), "col", scatter_dimension=1, tiled=True
    )
    mirrored = lax.psum_scatter(
        mirror_sum.reshape(VECS, col_span * TILE), "row", scatter_dimension=1, tiled=True
    )
    return forward + mirrored


def solution(mesh):
    placed = (
        P(("row", "col"), None),
        P(("row", "col")),
        P(None, ("row", "col")),
        P("row", "col", None, None),
        P("row", "col"),
    )
    return jax.shard_map(
        body, mesh=mesh, in_specs=placed, out_specs=P(None, ("row", "col")), check_vma=False
    )
```

profile of v0, /device:TPU:6, one launch (start us, length us, event | category | flops | bytes accessed | tf_op | source)
XLA Modules:
  0.0 607.1 jit_solution(15629664079876163862)
XLA Ops:
  9.5 41.4 %all_gather.23 = bf16[32,8192]{1,0:T(8,128)(2,1)S(1)} all-gather(bf16[32,256]{1,0:T(8,128)(2,1)S(1)} %convert_element_type.19), channel_id=1, replica_groups=mesh['row'=16,'col'=32] {'col'}, dimensions={1}, use_global_device_ids=true | all-gather | bytes 540672 | tf_op jit(solution)/shard_map/all_gather | solution.py:88
  51.7 35.8 %all_gather.18 = bf16[32,4096]{1,0:T(8,128)(2,1)S(1)} all-gather(bf16[32,256]{1,0:T(8,128)(2,1)S(1)} %convert_element_type.19), channel_id=1, replica_groups=mesh['row'=16,'col'=32] {'row'}, dimensions={1}, use_global_device_ids=true | all-gather | bytes 278528 | tf_op jit(solution)/shard_map/all_gather | solution.py:93
  87.6 44.5 %all-gather = bf16[32,1,256]{2,1,0:T(2,128)(2,1)S(1)} all-gather(bf16[1,1,256]{2,1,0:T(2,128)(2,1)S(1)} %reshape.279), channel_id=1, replica_groups=mesh['row'=16,'col'=32] {'col'}, dimensions={0}, use_global_device_ids=true | all-gather | bytes 16896 | tf_op jit(solution)/shard_map/all_gather | solution.py:87
  132.0 29.6 %all-gather.1 = bf16[16,1,256]{2,1,0:T(2,128)(2,1)S(1)} all-gather(bf16[1,1,256]{2,1,0:T(2,128)(2,1)S(1)} %reshape.279), channel_id=1, replica_groups=mesh['row'=16,'col'=32] {'row'}, dimensions={0}, use_global_device_ids=true | all-gather | bytes 8704 | tf_op jit(solution)/shard_map/all_gather | solution.py:92
  161.7 1.8 multiply_reduce_fusion.1
  163.6 2.7 multiply_reduce_fusion
  166.5 262.7 %while.14 = (s32[]{:T(128)}, f32[32,32,256]{2,1,0:T(8,128)S(1)}, f32[32,16,256]{2,1,0:T(8,128)S(1)}, s32[]{:T(128)}, s32[2,128]{1,0:T(2,128)}, /*index=5*/bf16[3...) while((s32[]{:T(128)}, f32[32,32,256]{2,1,0:T(8,128)S(1)}, ...), condition=%wide.region_3.4_spmd, body=%wide.region_2.3_spmd.sunk | while | flops 243142944 | bytes 11385997 | solution.py:80
  168.0 2.2 gather_fusion.1
  170.9 2.6 gather_fusion.3
  175.8 2.0 multiply_convert_fusion.2
  180.4 1.6 gather_fusion.9
  184.4 2.2 gather_fusion.1
  187.4 2.6 gather_fusion.3
  192.2 2.0 multiply_convert_fusion.2
  196.8 1.6 gather_fusion.9
  200.8 2.2 gather_fusion.1
  203.8 2.6 gather_fusion.3
  208.7 2.0 multiply_convert_fusion.2
  213.2 1.6 gather_fusion.9
  217.3 2.2 gather_fusion.1
  220.2 2.6 gather_fusion.3
  225.1 2.0 multiply_convert_fusion.2
  229.7 1.6 gather_fusion.9
  233.7 2.2 gather_fusion.1
  236.6 2.6 gather_fusion.3
  241.5 2.0 multiply_convert_fusion.2
  250.1 2.2 gather_fusion.1
  253.0 2.6 gather_fusion.3
  257.9 2.0 multiply_convert_fusion.2
  262.5 1.6 gather_fusion.9
  266.5 2.2 gather_fusion.1
  269.4 2.6 gather_fusion.3
  274.3 2.0 multiply_convert_fusion.2
  278.9 1.6 gather_fusion.9
  282.9 2.2 gather_fusion.1
  285.9 2.6 gather_fusion.3
  290.8 2.0 multiply_convert_fusion.2
  299.4 2.2 gather_fusion.1
  302.3 2.6 gather_fusion.3
  307.2 2.0 multiply_convert_fusion.2
  311.8 1.6 gather_fusion.9
  315.8 2.2 gather_fusion.1
  318.7 2.6 gather_fusion.3
  323.6 2.0 multiply_convert_fusion.2
  332.2 2.2 gather_fusion.1
  335.1 2.6 gather_fusion.3
  340.0 2.0 multiply_convert_fusion.2
  348.6 2.2 gather_fusion.1
  351.6 2.6 gather_fusion.3
  356.4 2.0 multiply_convert_fusion.2
  365.1 2.2 gather_fusion.1
  368.0 2.6 gather_fusion.3
  372.9 2.0 multiply_convert_fusion.2
  381.5 2.2 gather_fusion.1
  384.4 2.6 gather_fusion.3
  389.3 2.0 multiply_convert_fusion.2
  397.9 2.2 gather_fusion.1
  400.8 2.6 gather_fusion.3
  405.7 2.0 multiply_convert_fusion.2
  414.3 2.2 gather_fusion.1
  417.2 2.6 gather_fusion.3
  422.1 2.0 multiply_convert_fusion.2
  432.1 70.4 %reduce-scatter.5.cloned.1.call-done = f32[32,256]{1,0:T(8,128)} async-done(((f32[32,4096]{1,0:T(8,128)}), f32[32,256]{1,0:T(8,128)}) %reduce-scatter.5.cloned.1.call-update) | async-done | bytes 32784 | tf_op jit(solution)/shard_map/reduce_scatter | solution.py:109
  502.4 96.8 %reduce-scatter.3.cloned.1.call-done = f32[32,256]{1,0:T(8,128)} async-done(((f32[32,8192]{1,0:T(8,128)}), f32[32,256]{1,0:T(8,128)}) %reduce-scatter.3.cloned.1.call-update) | async-done | bytes 32784 | tf_op jit(solution)/shard_map/reduce_scatter | solution.py:106
  (370 shorter events, 146.7 us)
Async XLA Ops:
  6.5 81.0 %copy-start = (bf16[256]{0:T(256)(128)(2,1)S(1)}, bf16[256]{0:T(256)(128)(2,1)}, u32[]{:S(2)}) copy-start(bf16[256]{0:T(256)(128)(2,1)} %param.8) | copy-start | bytes 1540
  6.5 155.2 %all-gather.7.cloned.1.call-start = ((), (), s32[]{:S(2)}) async-start(), calls=%async_computation.3 | async-start | bytes 1114112 | tf_op jit(solution)/shard_map/all_gather | solution.py:91
  7.3 156.3 %all-gather.5.cloned.1.call-start = ((), (), s32[]{:S(2)}) async-start(), calls=%async_computation.2 | async-start | bytes 2162688 | tf_op jit(solution)/shard_map/all_gather | solution.py:86
  8.0 494.4 %reduce-scatter.5.cloned.1.call-start = ((), (), s32[]{:S(2)}) async-start(), calls=%async_computation.5 | async-start | bytes 557056 | tf_op jit(solution)/shard_map/reduce_scatter | solution.py:109
  430.4 168.8 %reduce-scatter.3.cloned.1.call-start = ((), (), s32[]{:S(2)}) async-start(), calls=%async_computation.4 | async-start | bytes 1081344 | tf_op jit(solution)/shard_map/reduce_scatter | solution.py:106
Sparse Core Ops, SparseCore 0:
  9.4 77.1 all-gather.6
  89.8 55.4 all-gather.4
  430.5 71.8 reduce-scatter.4
  507.3 91.8 reduce-scatter.2
where the time goes:
time: 611 us; the launch traced here: 607 us
  local copies, waits for them, and re-layouts  185 us (30%)
  waiting for transfers between devices  169 us (28%)
  blocking collectives  151 us (25%)
  matrix products  67.6 us (11%)
  other arithmetic  18.7 us (3%)
  between operations  13.9 us (2%)
    reduce_scatter x1, waiting for transfers between devices, body(): lax.psum_scatter(forward_sum.reshape(VECS, row_span * TILE), 'col', scatt...  96.8 us
    reduce_scatter x1, waiting for transfers between devices, body(): lax.psum_scatter(mirror_sum.reshape(VECS, col_span * TILE), 'row', scatte...  70.4 us
    all_gather x1, blocking collectives, body(): lax.all_gather(scales, 'col', axis=0, tiled=True)  44.5 us
    gather x16, local copies, waits for them, and re-layouts, group_step(): col_feat[local_cols]  42 us
    all_gather x1, blocking collectives, body(): lax.all_gather(narrow, 'col', axis=1, tiled=True)  41.4 us
    gather x16, local copies, waits for them, and re-layouts, group_step(): row_feat[local_rows]  35.8 us
    all_gather x1, blocking collectives, body(): lax.all_gather(narrow, 'row', axis=1, tiled=True)  35.8 us
    dot_general x16, matrix products, group_step(): jnp.einsum('gpd,gqd->gpq', row_feat[local_rows], col_feat[local_cols], pr...  32.4 us
  transfers between devices with their start and end apart: 4, of which 2 were waited for; matrix products, arithmetic and copies ran while one was open for 1% of the time, Pallas kernels for 0%

commit v1 on v0

v1 whole, which is shorter than its diff:
```python
import math

import jax
import jax.numpy as jnp
from jax import lax
from jax.experimental import pallas as pl
from jax.experimental.pallas import tpu as pltpu
from jax.sharding import PartitionSpec as P

TILE = 256
DESC = 128
VECS = 32
AUG = 16
DEPTH = DESC + AUG
PACK = DEPTH + VECS
UNROLL = 4

COL_SIZES = (4, 4, 2)
ROW_SIZES = (2, 8)
ROW_PARTS = 8
COL_PARTS = 1

POWER = math.log2(math.e) * 2.0 / DESC


def pack_kernel(feat_ref, scale_ref, vec_ref, row_ref, col_ref):
    turned = feat_ref[...].astype(jnp.float32).T
    norm = jnp.sum(turned * turned, axis=0, keepdims=True)
    offset = (DESC // 2) * jnp.log(scale_ref[...].astype(jnp.float32)) - 0.5 * norm
    high = offset.astype(jnp.bfloat16).astype(jnp.float32)
    rest = offset - high
    middle = rest.astype(jnp.bfloat16).astype(jnp.float32)
    low = (rest - middle).astype(jnp.bfloat16).astype(jnp.float32)
    place = lax.broadcasted_iota(jnp.int32, (AUG, TILE), 0)

    def offset_rows(first_own, first_one):
        own = place - first_own
        rows = jnp.where(own == 0, high, jnp.where(own == 1, middle, jnp.where(own == 2, low, 0.0)))
        one = place - first_one
        return jnp.where((one >= 0) & (one < 3), 1.0, rows).astype(jnp.bfloat16)

    descriptors = turned.astype(jnp.bfloat16)
    narrow = vec_ref[...].astype(jnp.bfloat16)
    for ref, rows in ((row_ref, offset_rows(0, 3)), (col_ref, offset_rows(3, 0))):
        ref[0:DESC, :] = descriptors
        ref[DESC:DEPTH, :] = rows
        ref[DEPTH:PACK, :] = narrow


def pack_blocks(features, scales, vectors):
    shape = jax.ShapeDtypeStruct((PACK, TILE), jnp.bfloat16)
    return pl.pallas_call(pack_kernel, out_shape=(shape, shape), name="pack_blocks")(
        features, scales.reshape(1, TILE), vectors
    )


def tiles_kernel(slots_ref, count_ref, *refs):
    rows_from, cols_from = refs[:ROW_PARTS], refs[ROW_PARTS : ROW_PARTS + COL_PARTS]
    forward_ref, mirror_ref = refs[ROW_PARTS + COL_PARTS : ROW_PARTS + COL_PARTS + 2]
    rows_ref, cols_ref, turned_ref, fsum_ref, msum_ref, row_sems, col_sems = refs[ROW_PARTS + COL_PARTS + 2 :]
    row_span = rows_ref.shape[0]
    col_span = cols_ref.shape[0]

    def copies(sources, target, sems):
        size = target.shape[0] // len(sources)
        return [
            pltpu.make_async_copy(source, target.at[pl.ds(at * size, size)], sems.at[at])
            for at, source in enumerate(sources)
        ]

    row_copies = copies(rows_from, rows_ref, row_sems)
    col_copies = copies(cols_from, cols_ref, col_sems)
    for copy in row_copies + col_copies:
        copy.start()

    fsum_ref[...] = jnp.zeros_like(fsum_ref)
    msum_ref[...] = jnp.zeros_like(msum_ref)

    part = row_span // ROW_PARTS
    for at, copy in enumerate(row_copies):
        copy.wait()

        @pl.loop(at * part, (at + 1) * part)
        def _(block):
            turned_ref[block] = rows_ref[block, 0:DEPTH, :].T

    for copy in col_copies:
        copy.wait()

    def tile(slot):
        row_at = slots_ref[0, slot]
        col_at = slots_ref[1, slot]
        score = jnp.dot(turned_ref[row_at], cols_ref[col_at, 0:DEPTH, :], preferred_element_type=jnp.float32)
        block = jnp.exp2(score * POWER).astype(jnp.bfloat16)
        forward = lax.dot_general(
            cols_ref[col_at, DEPTH:PACK, :], block, (((1,), (1,)), ((), ())), preferred_element_type=jnp.float32
        )
        mirror = jnp.dot(rows_ref[row_at, DEPTH:PACK, :], block, preferred_element_type=jnp.float32)
        return slots_ref[2, slot], slots_ref[3, slot], forward, mirror

    @pl.loop(0, lax.div(count_ref[0, 0] + (UNROLL - 1), UNROLL))
    def _(group):
        done = [tile(group * UNROLL + step) for step in range(UNROLL)]
        for forward_at, mirror_at, forward, mirror in done:
            fsum_ref[forward_at] += forward
            msum_ref[mirror_at] += mirror

    forward_ref[...] = fsum_ref[0:row_span].astype(jnp.bfloat16)
    mirror_ref[...] = msum_ref[0:col_span].astype(jnp.bfloat16)


def tile_products(slots, tile_count, row_parts, col_parts):
    row_span = sum(part.shape[0] for part in row_parts)
    col_span = sum(part.shape[0] for part in col_parts)
    smem = pl.BlockSpec(memory_space=pltpu.SMEM)
    vmem = pl.BlockSpec(memory_space=pltpu.VMEM)
    anywhere = pl.BlockSpec(memory_space=pl.ANY)
    return pl.pallas_call(
        tiles_kernel,
        out_shape=(
            jax.ShapeDtypeStruct((row_span, VECS, TILE), jnp.bfloat16),
            jax.ShapeDtypeStruct((col_span, VECS, TILE), jnp.bfloat16),
        ),
        in_specs=[smem, smem] + [anywhere] * (ROW_PARTS + COL_PARTS),
        out_specs=(vmem, vmem),
        scratch_shapes=[
            pltpu.VMEM((row_span, PACK, TILE), jnp.bfloat16),
            pltpu.VMEM((col_span, PACK, TILE), jnp.bfloat16),
            pltpu.VMEM((row_span, TILE, DEPTH), jnp.bfloat16),
            pltpu.VMEM((row_span + 1, VECS, TILE), jnp.float32),
            pltpu.VMEM((col_span + 1, VECS, TILE), jnp.float32),
            pltpu.SemaphoreType.DMA((ROW_PARTS,)),
            pltpu.SemaphoreType.DMA((COL_PARTS,)),
        ],
        compiler_params=pltpu.CompilerParams(vmem_limit_bytes=48 * 1024 * 1024),
        name="tile_products",
    )(slots, tile_count, *row_parts, *col_parts)


def shifted(value, axis, sizes, part, distance):
    pairs = []
    for source in range(math.prod(sizes)):
        place = list(split_index(source, sizes))
        place[part] = (place[part] + distance) % sizes[part]
        target = 0
        for at, size in zip(place, sizes):
            target = target * size + at
        pairs.append((source, target))
    return lax.ppermute(value, axis, pairs)


def split_index(index, sizes):
    place = []
    for size in reversed(sizes):
        place.append(index & (size - 1))
        index = index >> (size.bit_length() - 1)
    return tuple(reversed(place))


def gather_rows(own):
    along_y = jnp.stack([own] + [shifted(own, "col", COL_SIZES, 0, step) for step in range(1, 4)])
    parts = [along_y] + [shifted(along_y, "col", COL_SIZES, 1, step) for step in range(1, 4)]
    return parts + [shifted(part, "col", COL_SIZES, 2, 1) for part in parts]


def gather_cols(own):
    span = math.prod(ROW_SIZES)
    return [lax.all_to_all(jnp.broadcast_to(own, (span,) + own.shape), "row", 0, 0, tiled=True)]


def slot_places(tile_pairs, tile_count):
    row_span = math.prod(COL_SIZES)
    col_span = math.prod(ROW_SIZES)
    i, j = tile_pairs[0], tile_pairs[1]
    local_row, local_col = lax.rem(i, row_span), lax.div(j, row_span)

    here = split_index(lax.axis_index("col"), COL_SIZES)
    there = split_index(local_row, COL_SIZES)
    y_hi, x, core = [(mine - other) & (size - 1) for mine, other, size in zip(here, there, COL_SIZES)]
    live = jnp.arange(tile_pairs.shape[1], dtype=jnp.int32) < tile_count
    return jnp.stack(
        [
            (core * 4 + x) * 4 + y_hi,
            local_col,
            jnp.where(live, local_row, row_span),
            jnp.where(live & (i != j), local_col, col_span),
        ]
    )


def body(features, scales, vectors, pattern, counts):
    row_own, col_own = pack_blocks(features, scales, vectors)
    row_parts = gather_rows(row_own)
    col_parts = gather_cols(col_own)
    slots = slot_places(pattern[0, 0], counts[0, 0])
    forward, mirror = tile_products(slots, counts, row_parts, col_parts)
    forward = lax.all_to_all(forward, "col", 0, 0, tiled=True)
    mirror = lax.all_to_all(mirror, "row", 0, 0, tiled=True)
    return jnp.sum(forward.astype(jnp.float32), axis=0) + jnp.sum(mirror.astype(jnp.float32), axis=0)


def solution(mesh):
    placed = (
        P(("row", "col"), None),
        P(("row", "col")),
        P(None, ("row", "col")),
        P("row", "col", None, None),
        P("row", "col"),
    )
    return jax.shard_map(
        body, mesh=mesh, in_specs=placed, out_specs=P(None, ("row", "col")), check_vma=False
    )
```

time: 611 us -> 153 us (0.25)
  the two profiles are of different devices: /device:TPU:6 before, /device:TPU:1 now
where the time goes in v1:
time: 153 us; the launch traced here: 152 us
  starting transfers between devices  61.2 us (40%)
  Pallas kernels  38.9 us (25%)
  waiting for transfers between devices  34 us (22%)
  blocking collectives  12.7 us (8%)
  local copies, waits for them, and re-layouts  3.33 us (2%)
    ppermute x10, starting transfers between devices, shifted(): return lax.ppermute(value, axis, pairs)  40.9 us
    pallas_call x1, Pallas kernels, tile_products(): pl.pallas_call(tiles_kernel, out_shape=(jax.ShapeDtypeStruct((row_span, V...  37.3 us
    all_to_all x1, waiting for transfers between devices, body(): forward = lax.all_to_all(forward, 'col', 0, 0, tiled=True)  17.9 us
    ppermute x10, waiting for transfers between devices, shifted(): return lax.ppermute(value, axis, pairs)  16.1 us
    all_to_all x1, blocking collectives, body(): mirror = lax.all_to_all(mirror, 'row', 0, 0, tiled=True)  12.7 us
    all_to_all x1, starting transfers between devices, gather_cols(): lax.all_to_all(jnp.broadcast_to(own, (span,) + own.shape), 'row', 0, 0, t...  12.1 us
    all_to_all x1, starting transfers between devices, body(): forward = lax.all_to_all(forward, 'col', 0, 0, tiled=True)  8.21 us
  transfers between devices with their start and end apart: 12, of which 4 were waited for; matrix products, arithmetic and copies ran while one was open for 0% of the time, Pallas kernels for 0%

profile of v1, /device:TPU:1, one launch (start us, length us, event | category | flops | bytes accessed | tf_op | source)
XLA Modules:
  0.0 151.9 jit_solution(802190936554729644)
XLA Ops:
  0.0 1.2 reshape.179.scale_ref
  1.2 1.7 %pack_blocks.1 = (bf16[176,256]{1,0:T(8,128)(2,1)}, bf16[176,256]{1,0:T(8,128)(2,1)}) custom-call(bf16[256,128]{1,0:T(8,128)(2,1)} %feat_ref.1, bf16[1,256]{1,0:T(2,128)(2,1)} %reshape.179.scale_ref, f32[32,256]{1,0:T(8,128)} %vec_ref.1), custom_call_target="tpu_custom_call" | custom-call | tf_op jit(solution)/shard_map/pack_blocks/pallas_call | solution.py:52
  2.9 2.1 %broadcast_in_dim.9 = bf16[16,176,256]{2,1,0:T(8,128)(2,1)} broadcast(bf16[176,256]{1,0:T(8,128)(2,1)} %get-tuple-element.10), dimensions={1,2} | broadcast | bytes 1531904 | tf_op jit(solution)/shard_map/broadcast_in_dim | solution.py:168
  5.0 0.0 copy-start
  5.0 0.0 copy-start.1
  5.0 12.1 %all-to-all-start = ((bf16[16,176,256]{2,1,0:T(8,128)(2,1)}), bf16[16,176,256]{2,1,0:T(8,128)(2,1)S(1)}, u32[]{:S(2)}, u32[]{:S(2)}) async-start(bf16[16,176,256]{2,1,0:T(8,128)(2,1)} %broadcast_in_dim.9), calls=%async_computation | async-start | bytes 2883584 | tf_op jit(solution)/shard_map/all_to_all | solution.py:168
  17.1 0.0 copy-done
  17.1 5.0 %collective-permute-start.2 = (bf16[176,256]{1,0:T(8,128)(2,1)S(1)}, bf16[176,256]{1,0:T(8,128)(2,1)S(1)}, u32[]{:S(2)}, u32[]{:S(2)}) collective-permute-start(bf16[176,256]{1,0:T(8,128)(2,1)S(1)} %copy-done), channel_id=1, source_target_pairs={{0,24},{1,25},{2,26},{3,27},{4,28},{5,29},{6,30},{7,31},{8,0},{9,1... | collective-permute-start | bytes 270344 | tf_op jit(solution)/shard_map/ppermute | solution.py:149
  22.1 4.4 %collective-permute-start.1 = (bf16[176,256]{1,0:T(8,128)(2,1)S(1)}, bf16[176,256]{1,0:T(8,128)(2,1)S(1)}, u32[]{:S(2)}, u32[]{:S(2)}) collective-permute-start(bf16[176,256]{1,0:T(8,128)(2,1)S(1)} %copy-done), channel_id=1, source_target_pairs={{0,16},{1,17},{2,18},{3,19},{4,20},{5,21},{6,22},{7,23},{8,24},{9,... | collective-permute-start | bytes 270344 | tf_op jit(solution)/shard_map/ppermute | solution.py:149
  26.5 3.3 %collective-permute-start = (bf16[176,256]{1,0:T(8,128)(2,1)S(1)}, bf16[176,256]{1,0:T(8,128)(2,1)S(1)}, u32[]{:S(2)}, u32[]{:S(2)}) collective-permute-start(bf16[176,256]{1,0:T(8,128)(2,1)S(1)} %copy-done), channel_id=1, source_target_pairs={{0,8},{1,9},{2,10},{3,11},{4,12},{5,13},{6,14},{7,15},{8,16},{9,17... | collective-permute-start | bytes 270344 | tf_op jit(solution)/shard_map/ppermute | solution.py:149
  29.9 0.0 collective-permute-done.2
  29.9 15.2 %collective-permute-done.1 = bf16[176,256]{1,0:T(8,128)(2,1)S(1)} collective-permute-done((bf16[176,256]{1,0:T(8,128)(2,1)S(1)}, bf16[176,256]{1,0:T(8,128)(2,1)S(1)}, u32[]{:S(2)}, u32[]{:S(2)}) %collective-permute-start.1) | collective-permute-done | bytes 90144 | tf_op jit(solution)/shard_map/ppermute | solution.py:149
  45.1 0.2 collective-permute-done
  45.4 4.4 %collective-permute-start.5 = (bf16[4,176,256]{2,1,0:T(8,128)(2,1)S(1)}, bf16[4,176,256]{2,1,0:T(8,128)(2,1)S(1)}, u32[]{:S(2)}, u32[]{:S(2)}) collective-permute-start(bf16[4,176,256]{2,1,0:T(8,128)(2,1)S(1)} %pad_maximum_fusion.refs_0_), channel_id=1, source_target_pairs={{0,6},{1,7},{2,0},{3,1},{4,2},{5,3},{6,4},{7,5},{8,14},{9,15},{10,... | collective-permute-start | bytes 1081352 | tf_op jit(solution)/shard_map/ppermute | solution.py:149
  49.8 2.4 %collective-permute-start.4 = (bf16[4,176,256]{2,1,0:T(8,128)(2,1)S(1)}, bf16[4,176,256]{2,1,0:T(8,128)(2,1)S(1)}, u32[]{:S(2)}, u32[]{:S(2)}) collective-permute-start(bf16[4,176,256]{2,1,0:T(8,128)(2,1)S(1)} %pad_maximum_fusion.refs_0_), channel_id=1, source_target_pairs={{0,4},{1,5},{2,6},{3,7},{4,0},{5,1},{6,2},{7,3},{8,12},{9,13},{10,... | collective-permute-start | bytes 1081352 | tf_op jit(solution)/shard_map/ppermute | solution.py:149
  52.2 2.5 %collective-permute-start.3 = (bf16[4,176,256]{2,1,0:T(8,128)(2,1)S(1)}, bf16[4,176,256]{2,1,0:T(8,128)(2,1)S(1)}, u32[]{:S(2)}, u32[]{:S(2)}) collective-permute-start(bf16[4,176,256]{2,1,0:T(8,128)(2,1)S(1)} %pad_maximum_fusion.refs_0_), channel_id=1, source_target_pairs={{0,2},{1,3},{2,4},{3,5},{4,6},{5,7},{6,0},{7,1},{8,10},{9,11},{10,... | collective-permute-start | bytes 1081352 | tf_op jit(solution)/shard_map/ppermute | solution.py:149
  54.7 6.2 %collective-permute-start.6 = (bf16[4,176,256]{2,1,0:T(8,128)(2,1)S(1)}, bf16[4,176,256]{2,1,0:T(8,128)(2,1)S(1)}, u32[]{:S(2)}, u32[]{:S(2)}) collective-permute-start(bf16[4,176,256]{2,1,0:T(8,128)(2,1)S(1)} %pad_maximum_fusion.refs_0_), channel_id=1, source_target_pairs={{0,1},{1,0},{2,3},{3,2},{4,5},{5,4},{6,7},{7,6},{8,9},{9,8},{10,11... | collective-permute-start | bytes 1081352 | tf_op jit(solution)/shard_map/ppermute | solution.py:149
  60.9 0.0 collective-permute-done.5.refs_3_
  60.9 7.1 %collective-permute-start.9 = (bf16[4,176,256]{2,1,0:T(8,128)(2,1)S(1)}, bf16[4,176,256]{2,1,0:T(8,128)(2,1)}, u32[]{:S(2)}, u32[]{:S(2)}) collective-permute-start(bf16[4,176,256]{2,1,0:T(8,128)(2,1)S(1)} %collective-permute-done.5.refs_3_), channel_id=1, source_target_pairs={{0,1},{1,0},{2,3},{3,2},{4,5},{5,4},{6,7},{7,6},{8,9},{9,8},{10,11... | collective-permute-start | bytes 1081352 | tf_op jit(solution)/shard_map/ppermute | solution.py:149
  68.0 0.0 collective-permute-done.4.refs_2_
  68.0 1.9 %collective-permute-start.8 = (bf16[4,176,256]{2,1,0:T(8,128)(2,1)S(1)}, bf16[4,176,256]{2,1,0:T(8,128)(2,1)}, u32[]{:S(2)}, u32[]{:S(2)}) collective-permute-start(bf16[4,176,256]{2,1,0:T(8,128)(2,1)S(1)} %collective-permute-done.4.refs_2_), channel_id=1, source_target_pairs={{0,1},{1,0},{2,3},{3,2},{4,5},{5,4},{6,7},{7,6},{8,9},{9,8},{10,11... | collective-permute-start | bytes 1081352 | tf_op jit(solution)/shard_map/ppermute | solution.py:149
  70.0 0.0 collective-permute-done.3.refs_1_
  70.0 3.6 %collective-permute-start.7 = (bf16[4,176,256]{2,1,0:T(8,128)(2,1)S(1)}, bf16[4,176,256]{2,1,0:T(8,128)(2,1)}, u32[]{:S(2)}, u32[]{:S(2)}) collective-permute-start(bf16[4,176,256]{2,1,0:T(8,128)(2,1)S(1)} %collective-permute-done.3.refs_1_), channel_id=1, source_target_pairs={{0,1},{1,0},{2,3},{3,2},{4,5},{5,4},{6,7},{7,6},{8,9},{9,8},{10,11... | collective-permute-start | bytes 1081352 | tf_op jit(solution)/shard_map/ppermute | solution.py:149
  74.3 0.0 copy-done.1
  74.3 0.0 collective-permute-done.6.refs_4_
  74.3 0.0 collective-permute-done.9.refs_7_
  74.3 0.0 collective-permute-done.8.refs_6_
  74.3 0.7 collective-permute-done.7.refs_5_
  75.0 0.0 all-to-all-done.refs_8_
  75.0 37.3 %tile_products.1 = (bf16[32,32,256]{2,1,0:T(8,128)(2,1)}, bf16[16,32,256]{2,1,0:T(8,128)(2,1)S(1)}) custom-call(s32[4,128]{1,0:T(4,128)S(1)} %pad_add_fusion.slots_ref, s32[1,1]{1,0:T(1,128)} %copy.6.count_ref, bf16[4,176,256]{2,1,0:T(8,128)(2,1)S(1)} %pad_maximum_fusion.refs_0_, bf16[4,176,256]{2,1,0:T(8,128)(2,1)S(1)} %collective-permute-done.3.refs_1_, ...), custom_call_target="tpu_custom_call" | custom-call | tf_op jit(solution)/shard_map/tile_products/pallas_call | solution.py:118
  112.3 12.7 %all_to_all.15 = bf16[16,32,256]{2,1,0:T(8,128)(2,1)S(1)} all-to-all(bf16[16,32,256]{2,1,0:T(8,128)(2,1)S(1)} %get-tuple-element.12), channel_id=1, replica_groups=mesh['row'=16,'col'=32] {'row'}, dimensions={0} | all-to-all | bytes 524288 | tf_op jit(solution)/shard_map/all_to_all | solution.py:198
  125.0 8.2 %all-to-all-start.1 = ((bf16[32,32,256]{2,1,0:T(8,128)(2,1)}), bf16[32,32,256]{2,1,0:T(8,128)(2,1)S(1)}, u32[]{:S(2)}, u32[]{:S(2)}) async-start(bf16[32,32,256]{2,1,0:T(8,128)(2,1)} %get-tuple-element.11), calls=%async_computation.1 | async-start | bytes 1048576 | tf_op jit(solution)/shard_map/all_to_all | solution.py:197
  133.3 17.9 %all-to-all-done.1 = bf16[32,32,256]{2,1,0:T(8,128)(2,1)S(1)} async-done(((bf16[32,32,256]{2,1,0:T(8,128)(2,1)}), bf16[32,32,256]{2,1,0:T(8,128)(2,1)S(1)}, u32[]{:S(2)}, u32[]{:S(2)}) %all-to-all-start.1) | async-done | bytes 524320 | tf_op jit(solution)/shard_map/all_to_all | solution.py:197
  151.2 0.1 convert_reduce_fusion
  151.3 0.6 add.25
  (4 shorter events, 0.1 us)
Async XLA Ops:
  5.0 12.1 %copy-start = (bf16[176,256]{1,0:T(8,128)(2,1)S(1)}, bf16[176,256]{1,0:T(8,128)(2,1)}, u32[]{:S(2)}) copy-start(bf16[176,256]{1,0:T(8,128)(2,1)} %get-tuple-element.9) | copy-start | bytes 270340
  5.0 69.3 %copy-start.1 = (s32[1,1,2,128]{3,2,1,0:T(2,128)S(1)}, s32[1,1,2,128]{3,2,1,0:T(2,128)}, u32[]{:S(2)}) copy-start(s32[1,1,2,128]{3,2,1,0:T(2,128)} %param.8) | copy-start | bytes 3076
  5.0 70.0 %all-to-all-start = ((bf16[16,176,256]{2,1,0:T(8,128)(2,1)}), bf16[16,176,256]{2,1,0:T(8,128)(2,1)S(1)}, u32[]{:S(2)}, u32[]{:S(2)}) async-start(bf16[16,176,256]{2,1,0:T(8,128)(2,1)} %broadcast_in_dim.9), calls=%async_computation | async-start | bytes 2883584 | tf_op jit(solution)/shard_map/all_to_all | solution.py:168
  17.1 12.8 %collective-permute-start.2 = (bf16[176,256]{1,0:T(8,128)(2,1)S(1)}, bf16[176,256]{1,0:T(8,128)(2,1)S(1)}, u32[]{:S(2)}, u32[]{:S(2)}) collective-permute-start(bf16[176,256]{1,0:T(8,128)(2,1)S(1)} %copy-done), channel_id=1, source_target_pairs={{0,24},{1,25},{2,26},{3,27},{4,28},{5,29},{6,30},{7,31},{8,0},{9,1... | collective-permute-start | bytes 270344 | tf_op jit(solution)/shard_map/ppermute | solution.py:149
  22.1 23.0 %collective-permute-start.1 = (bf16[176,256]{1,0:T(8,128)(2,1)S(1)}, bf16[176,256]{1,0:T(8,128)(2,1)S(1)}, u32[]{:S(2)}, u32[]{:S(2)}) collective-permute-start(bf16[176,256]{1,0:T(8,128)(2,1)S(1)} %copy-done), channel_id=1, source_target_pairs={{0,16},{1,17},{2,18},{3,19},{4,20},{5,21},{6,22},{7,23},{8,24},{9,... | collective-permute-start | bytes 270344 | tf_op jit(solution)/shard_map/ppermute | solution.py:149
  26.5 18.8 %collective-permute-start = (bf16[176,256]{1,0:T(8,128)(2,1)S(1)}, bf16[176,256]{1,0:T(8,128)(2,1)S(1)}, u32[]{:S(2)}, u32[]{:S(2)}) collective-permute-start(bf16[176,256]{1,0:T(8,128)(2,1)S(1)} %copy-done), channel_id=1, source_target_pairs={{0,8},{1,9},{2,10},{3,11},{4,12},{5,13},{6,14},{7,15},{8,16},{9,17... | collective-permute-start | bytes 270344 | tf_op jit(solution)/shard_map/ppermute | solution.py:149
  45.4 15.6 %collective-permute-start.5 = (bf16[4,176,256]{2,1,0:T(8,128)(2,1)S(1)}, bf16[4,176,256]{2,1,0:T(8,128)(2,1)S(1)}, u32[]{:S(2)}, u32[]{:S(2)}) collective-permute-start(bf16[4,176,256]{2,1,0:T(8,128)(2,1)S(1)} %pad_maximum_fusion.refs_0_), channel_id=1, source_target_pairs={{0,6},{1,7},{2,0},{3,1},{4,2},{5,3},{6,4},{7,5},{8,14},{9,15},{10,... | collective-permute-start | bytes 1081352 | tf_op jit(solution)/shard_map/ppermute | solution.py:149
  49.8 18.3 %collective-permute-start.4 = (bf16[4,176,256]{2,1,0:T(8,128)(2,1)S(1)}, bf16[4,176,256]{2,1,0:T(8,128)(2,1)S(1)}, u32[]{:S(2)}, u32[]{:S(2)}) collective-permute-start(bf16[4,176,256]{2,1,0:T(8,128)(2,1)S(1)} %pad_maximum_fusion.refs_0_), channel_id=1, source_target_pairs={{0,4},{1,5},{2,6},{3,7},{4,0},{5,1},{6,2},{7,3},{8,12},{9,13},{10,... | collective-permute-start | bytes 1081352 | tf_op jit(solution)/shard_map/ppermute | solution.py:149
  52.2 17.8 %collective-permute-start.3 = (bf16[4,176,256]{2,1,0:T(8,128)(2,1)S(1)}, bf16[4,176,256]{2,1,0:T(8,128)(2,1)S(1)}, u32[]{:S(2)}, u32[]{:S(2)}) collective-permute-start(bf16[4,176,256]{2,1,0:T(8,128)(2,1)S(1)} %pad_maximum_fusion.refs_0_), channel_id=1, source_target_pairs={{0,2},{1,3},{2,4},{3,5},{4,6},{5,7},{6,0},{7,1},{8,10},{9,11},{10,... | collective-permute-start | bytes 1081352 | tf_op jit(solution)/shard_map/ppermute | solution.py:149
  54.7 19.6 %collective-permute-start.6 = (bf16[4,176,256]{2,1,0:T(8,128)(2,1)S(1)}, bf16[4,176,256]{2,1,0:T(8,128)(2,1)S(1)}, u32[]{:S(2)}, u32[]{:S(2)}) collective-permute-start(bf16[4,176,256]{2,1,0:T(8,128)(2,1)S(1)} %pad_maximum_fusion.refs_0_), channel_id=1, source_target_pairs={{0,1},{1,0},{2,3},{3,2},{4,5},{5,4},{6,7},{7,6},{8,9},{9,8},{10,11... | collective-permute-start | bytes 1081352 | tf_op jit(solution)/shard_map/ppermute | solution.py:149
  60.9 13.4 %collective-permute-start.9 = (bf16[4,176,256]{2,1,0:T(8,128)(2,1)S(1)}, bf16[4,176,256]{2,1,0:T(8,128)(2,1)}, u32[]{:S(2)}, u32[]{:S(2)}) collective-permute-start(bf16[4,176,256]{2,1,0:T(8,128)(2,1)S(1)} %collective-permute-done.5.refs_3_), channel_id=1, source_target_pairs={{0,1},{1,0},{2,3},{3,2},{4,5},{5,4},{6,7},{7,6},{8,9},{9,8},{10,11... | collective-permute-start | bytes 1081352 | tf_op jit(solution)/shard_map/ppermute | solution.py:149
  68.0 6.3 %collective-permute-start.8 = (bf16[4,176,256]{2,1,0:T(8,128)(2,1)S(1)}, bf16[4,176,256]{2,1,0:T(8,128)(2,1)}, u32[]{:S(2)}, u32[]{:S(2)}) collective-permute-start(bf16[4,176,256]{2,1,0:T(8,128)(2,1)S(1)} %collective-permute-done.4.refs_2_), channel_id=1, source_target_pairs={{0,1},{1,0},{2,3},{3,2},{4,5},{5,4},{6,7},{7,6},{8,9},{9,8},{10,11... | collective-permute-start | bytes 1081352 | tf_op jit(solution)/shard_map/ppermute | solution.py:149
  70.0 5.1 %collective-permute-start.7 = (bf16[4,176,256]{2,1,0:T(8,128)(2,1)S(1)}, bf16[4,176,256]{2,1,0:T(8,128)(2,1)}, u32[]{:S(2)}, u32[]{:S(2)}) collective-permute-start(bf16[4,176,256]{2,1,0:T(8,128)(2,1)S(1)} %collective-permute-done.3.refs_1_), channel_id=1, source_target_pairs={{0,1},{1,0},{2,3},{3,2},{4,5},{5,4},{6,7},{7,6},{8,9},{9,8},{10,11... | collective-permute-start | bytes 1081352 | tf_op jit(solution)/shard_map/ppermute | solution.py:149
  125.0 26.2 %all-to-all-start.1 = ((bf16[32,32,256]{2,1,0:T(8,128)(2,1)}), bf16[32,32,256]{2,1,0:T(8,128)(2,1)S(1)}, u32[]{:S(2)}, u32[]{:S(2)}) async-start(bf16[32,32,256]{2,1,0:T(8,128)(2,1)} %get-tuple-element.11), calls=%async_computation.1 | async-start | bytes 1048576 | tf_op jit(solution)/shard_map/all_to_all | solution.py:197

commit v2 on v1

--- a/solution.py
+++ b/solution.py
@@ -13,7 +13,8 @@
 AUG = 16
 DEPTH = DESC + AUG
 PACK = DEPTH + VECS
-UNROLL = 4
+FULL = 256
+UNROLL = 8
 
 COL_SIZES = (4, 4, 2)
 ROW_SIZES = (2, 8)
@@ -56,15 +57,17 @@
 
 def tiles_kernel(slots_ref, count_ref, *refs):
     rows_from, cols_from = refs[:ROW_PARTS], refs[ROW_PARTS : ROW_PARTS + COL_PARTS]
-    forward_ref, mirror_ref = refs[ROW_PARTS + COL_PARTS : ROW_PARTS + COL_PARTS + 2]
-    rows_ref, cols_ref, turned_ref, fsum_ref, msum_ref, row_sems, col_sems = refs[ROW_PARTS + COL_PARTS + 2 :]
+    forward_ref, other_ref, mirror_ref = refs[ROW_PARTS + COL_PARTS : ROW_PARTS + COL_PARTS + 3]
+    rows_ref, cols_ref, turned_ref, fsum_ref, msum_ref, row_sems, col_sems = refs[ROW_PARTS + COL_PARTS + 3 :]
     row_span = rows_ref.shape[0]
     col_span = cols_ref.shape[0]
+
+    cols_ref[:, PACK:FULL, :] = jnp.zeros((col_span, FULL - PACK, TILE), jnp.bfloat16)
 
     def copies(sources, target, sems):
         size = target.shape[0] // len(sources)
         return [
-            pltpu.make_async_copy(source, target.at[pl.ds(at * size, size)], sems.at[at])
+            pltpu.make_async_copy(source, target.at[pl.ds(at * size, size), pl.ds(0, PACK)], sems.at[at])
             for at, source in enumerate(sources)
         ]
 
@@ -82,7 +85,10 @@
 
         @pl.loop(at * part, (at + 1) * part)
         def _(block):
-            turned_ref[block] = rows_ref[block, 0:DEPTH, :].T
+            turned_ref[block, :, 0:DESC] = rows_ref[block, 0:DESC, :].T
+            offsets = rows_ref[block, DESC:DEPTH, :]
+            padded = jnp.concatenate([offsets, jnp.zeros((FULL - DEPTH, TILE), jnp.bfloat16)], axis=0)
+            turned_ref[block, :, DESC:FULL] = padded.T
 
     for copy in col_copies:
         copy.wait()
@@ -90,7 +96,7 @@
     def tile(slot):
         row_at = slots_ref[0, slot]
         col_at = slots_ref[1, slot]
-        score = jnp.dot(turned_ref[row_at], cols_ref[col_at, 0:DEPTH, :], preferred_element_type=jnp.float32)
+        score = jnp.dot(turned_ref[row_at], cols_ref[col_at], preferred_element_type=jnp.float32)
         block = jnp.exp2(score * POWER).astype(jnp.bfloat16)
         forward = lax.dot_general(
             cols_ref[col_at, DEPTH:PACK, :], block, (((1,), (1,)), ((), ())), preferred_element_type=jnp.float32
@@ -105,7 +111,9 @@
             fsum_ref[forward_at] += forward
             msum_ref[mirror_at] += mirror
 
-    forward_ref[...] = fsum_ref[0:row_span].astype(jnp.bfloat16)
+    half = row_span // 2
+    forward_ref[...] = fsum_ref[0:half]
+    other_ref[...] = fsum_ref[half:row_span].astype(jnp.bfloat16)
     mirror_ref[...] = msum_ref[0:col_span].astype(jnp.bfloat16)
 
 
@@ -118,15 +126,16 @@
     return pl.pallas_call(
         tiles_kernel,
         out_shape=(
-            jax.ShapeDtypeStruct((row_span, VECS, TILE), jnp.bfloat16),
+            jax.ShapeDtypeStruct((row_span // 2, VECS, TILE), jnp.float32),
+            jax.ShapeDtypeStruct((row_span // 2, VECS, TILE), jnp.bfloat16),
             jax.ShapeDtypeStruct((col_span, VECS, TILE), jnp.bfloat16),
         ),
         in_specs=[smem, smem] + [anywhere] * (ROW_PARTS + COL_PARTS),
-        out_specs=(vmem, vmem),
+        out_specs=(vmem, vmem, vmem),
         scratch_shapes=[
             pltpu.VMEM((row_span, PACK, TILE), jnp.bfloat16),
-            pltpu.VMEM((col_span, PACK, TILE), jnp.bfloat16),
-            pltpu.VMEM((row_span, TILE, DEPTH), jnp.bfloat16),
+            pltpu.VMEM((col_span, FULL, TILE), jnp.bfloat16),
+            pltpu.VMEM((row_span, TILE, FULL), jnp.bfloat16),
             pltpu.VMEM((row_span + 1, VECS, TILE), jnp.float32),
             pltpu.VMEM((col_span + 1, VECS, TILE), jnp.float32),
             pltpu.SemaphoreType.DMA((ROW_PARTS,)),
@@ -163,9 +172,20 @@
     return parts + [shifted(part, "col", COL_SIZES, 2, 1) for part in parts]
 
 
-def gather_cols(own):
-    span = math.prod(ROW_SIZES)
-    return [lax.all_to_all(jnp.broadcast_to(own, (span,) + own.shape), "row", 0, 0, tiled=True)]
+def grouped_all_to_all(value, axis, sizes, part_of):
+    groups = {}
+    for index in range(math.prod(sizes)):
+        groups.setdefault(part_of(split_index(index, sizes)), []).append(index)
+    return lax.all_to_all(value, axis, 0, 0, axis_index_groups=list(groups.values()), tiled=True)
+
+
+def gather_pair(own):
+    pair = jnp.stack([own, shifted(own, "row", ROW_SIZES, 0, 1)])
+    return jnp.broadcast_to(pair[None], (ROW_SIZES[1],) + pair.shape).reshape((-1,) + own.shape)
+
+
+def gather_cols(pairs):
+    return [grouped_all_to_all(pairs, "row", ROW_SIZES, lambda place: place[0])]
 
 
 def slot_places(tile_pairs, tile_count):
@@ -174,15 +194,15 @@
     i, j = tile_pairs[0], tile_pairs[1]
     local_row, local_col = lax.rem(i, row_span), lax.div(j, row_span)
 
-    here = split_index(lax.axis_index("col"), COL_SIZES)
-    there = split_index(local_row, COL_SIZES)
-    y_hi, x, core = [(mine - other) & (size - 1) for mine, other, size in zip(here, there, COL_SIZES)]
+    row_here, row_there = split_index(lax.axis_index("row"), ROW_SIZES), split_index(local_col, ROW_SIZES)
+    col_here, col_there = split_index(lax.axis_index("col"), COL_SIZES), split_index(local_row, COL_SIZES)
+    y_hi, x, core = [(mine - other) & (size - 1) for mine, other, size in zip(col_here, col_there, COL_SIZES)]
     live = jnp.arange(tile_pairs.shape[1], dtype=jnp.int32) < tile_count
     return jnp.stack(
         [
             (core * 4 + x) * 4 + y_hi,
-            local_col,
-            jnp.where(live, local_row, row_span),
+            row_there[1] * 2 + (row_there[0] ^ row_here[0]),
+            jnp.where(live, core * (row_span // 2) + (local_row >> 1), row_span),
             jnp.where(live & (i != j), local_col, col_span),
         ]
     )
@@ -190,12 +210,15 @@
 
 def body(features, scales, vectors, pattern, counts):
     row_own, col_own = pack_blocks(features, scales, vectors)
+    pairs, row_own = lax.optimization_barrier((gather_pair(col_own), row_own))
+    col_parts = gather_cols(pairs)
     row_parts = gather_rows(row_own)
-    col_parts = gather_cols(col_own)
     slots = slot_places(pattern[0, 0], counts[0, 0])
-    forward, mirror = tile_products(slots, counts, row_parts, col_parts)
-    forward = lax.all_to_all(forward, "col", 0, 0, tiled=True)
+    forward, for_other_core, mirror = tile_products(slots, counts, row_parts, col_parts)
+    for_other_core = shifted(for_other_core, "col", COL_SIZES, 2, 1)
     mirror = lax.all_to_all(mirror, "row", 0, 0, tiled=True)
+    forward = (forward + for_other_core.astype(jnp.float32)).astype(jnp.bfloat16)
+    forward = grouped_all_to_all(forward, "col", COL_SIZES, lambda place: place[2])
     return jnp.sum(forward.astype(jnp.float32), axis=0) + jnp.sum(mirror.astype(jnp.float32), axis=0)
 
 

time: 153 us -> 146 us (0.954)
  the two profiles are of different devices: /device:TPU:1 before, /device:TPU:6 now
where the time goes in v2:
time: 146 us; the launch traced here: 144 us
  starting transfers between devices  64.8 us (44%)
  Pallas kernels  38.8 us (27%)
  waiting for transfers between devices  32 us (22%)
  local copies, waits for them, and re-layouts  4.86 us (3%)
  other arithmetic  2.47 us (2%)
    ppermute x12, starting transfers between devices, shifted(): return lax.ppermute(value, axis, pairs)  37.8 us
    pallas_call x1, Pallas kernels, tile_products(): pl.pallas_call(tiles_kernel, out_shape=(jax.ShapeDtypeStruct((row_span //...  37.1 us
    all_to_all x2, starting transfers between devices, grouped_all_to_all(): lax.all_to_all(value, axis, 0, 0, axis_index_groups=list(groups.values())...  23.5 us
    ppermute x12, waiting for transfers between devices, shifted(): return lax.ppermute(value, axis, pairs)  13.7 us
    all_to_all x2, waiting for transfers between devices, grouped_all_to_all(): lax.all_to_all(value, axis, 0, 0, axis_index_groups=list(groups.values())...  9.2 us
    all_to_all x1, waiting for transfers between devices, body(): mirror = lax.all_to_all(mirror, 'row', 0, 0, tiled=True)  9.15 us
    all_to_all x1, starting transfers between devices, body(): mirror = lax.all_to_all(mirror, 'row', 0, 0, tiled=True)  3.54 us
  transfers between devices with their start and end apart: 15, of which 7 were waited for; matrix products, arithmetic and copies ran while one was open for 1% of the time, Pallas kernels for 0%

profile of v2, /device:TPU:6, one launch (start us, length us, event | category | flops | bytes accessed | tf_op | source)
XLA Modules:
  0.0 143.8 jit_solution(8979630193127861948)
XLA Ops:
  0.0 1.2 reshape.207.scale_ref
  1.2 1.7 %pack_blocks.1 = (bf16[176,256]{1,0:T(8,128)(2,1)}, bf16[176,256]{1,0:T(8,128)(2,1)}) custom-call(bf16[256,128]{1,0:T(8,128)(2,1)} %feat_ref.1, bf16[1,256]{1,0:T(2,128)(2,1)} %reshape.207.scale_ref, f32[32,256]{1,0:T(8,128)} %vec_ref.1), custom_call_target="tpu_custom_call" | custom-call | tf_op jit(solution)/shard_map/pack_blocks/pallas_call | solution.py:53
  2.9 3.5 %collective-permute-start = (bf16[176,256]{1,0:T(8,128)(2,1)}, bf16[176,256]{1,0:T(8,128)(2,1)S(1)}, u32[]{:S(2)}, u32[]{:S(2)}) collective-permute-start(bf16[176,256]{1,0:T(8,128)(2,1)} %get-tuple-element.12), channel_id=1, source_target_pairs={{0,256},{32,288},{64,320},{96,352},{128,384},{160,416},{192,448},{... | collective-permute-start | bytes 270344 | tf_op jit(solution)/shard_map/ppermute | solution.py:158
  6.4 3.1 %collective-permute-done = bf16[176,256]{1,0:T(8,128)(2,1)S(1)} collective-permute-done((bf16[176,256]{1,0:T(8,128)(2,1)}, bf16[176,256]{1,0:T(8,128)(2,1)S(1)}, u32[]{:S(2)}, u32[]{:S(2)}) %collective-permute-start) | collective-permute-done | bytes 90144 | tf_op jit(solution)/shard_map/ppermute | solution.py:158
  9.5 0.9 pad_maximum_fusion.1
  10.4 1.2 broadcast_in_dim.4
  11.6 0.0 copy-start.3
  11.6 0.0 copy-start.4
  11.6 10.4 %all-to-all-start = ((bf16[16,176,256]{2,1,0:T(8,128)(2,1)}), bf16[16,176,256]{2,1,0:T(8,128)(2,1)S(1)}, u32[]{:S(2)}, u32[]{:S(2)}) async-start(bf16[16,176,256]{2,1,0:T(8,128)(2,1)} %bitcast.5), calls=%async_computation | async-start | bytes 2883584 | tf_op jit(solution)/shard_map/all_to_all | solution.py:179
  22.1 0.0 copy-done.3
  22.1 6.2 %collective-permute-start.3 = (bf16[176,256]{1,0:T(8,128)(2,1)S(1)}, bf16[176,256]{1,0:T(8,128)(2,1)S(1)}, u32[]{:S(2)}, u32[]{:S(2)}) collective-permute-start(bf16[176,256]{1,0:T(8,128)(2,1)S(1)} %copy-done.3), channel_id=1, source_target_pairs={{0,24},{1,25},{2,26},{3,27},{4,28},{5,29},{6,30},{7,31},{8,0},{9,1... | collective-permute-start | bytes 270344 | tf_op jit(solution)/shard_map/ppermute | solution.py:158
  28.3 3.8 %collective-permute-start.2 = (bf16[176,256]{1,0:T(8,128)(2,1)S(1)}, bf16[176,256]{1,0:T(8,128)(2,1)S(1)}, u32[]{:S(2)}, u32[]{:S(2)}) collective-permute-start(bf16[176,256]{1,0:T(8,128)(2,1)S(1)} %copy-done.3), channel_id=1, source_target_pairs={{0,16},{1,17},{2,18},{3,19},{4,20},{5,21},{6,22},{7,23},{8,24},{9,... | collective-permute-start | bytes 270344 | tf_op jit(solution)/shard_map/ppermute | solution.py:158
  32.1 4.5 %collective-permute-start.1 = (bf16[176,256]{1,0:T(8,128)(2,1)S(1)}, bf16[176,256]{1,0:T(8,128)(2,1)S(1)}, u32[]{:S(2)}, u32[]{:S(2)}) collective-permute-start(bf16[176,256]{1,0:T(8,128)(2,1)S(1)} %copy-done.3), channel_id=1, source_target_pairs={{0,8},{1,9},{2,10},{3,11},{4,12},{5,13},{6,14},{7,15},{8,16},{9,17... | collective-permute-start | bytes 270344 | tf_op jit(solution)/shard_map/ppermute | solution.py:158
  36.6 0.0 collective-permute-done.3
  36.6 2.8 %collective-permute-done.2 = bf16[176,256]{1,0:T(8,128)(2,1)S(1)} collective-permute-done((bf16[176,256]{1,0:T(8,128)(2,1)S(1)}, bf16[176,256]{1,0:T(8,128)(2,1)S(1)}, u32[]{:S(2)}, u32[]{:S(2)}) %collective-permute-start.2) | collective-permute-done | bytes 90144 | tf_op jit(solution)/shard_map/ppermute | solution.py:158
  39.4 1.2 collective-permute-done.1
  40.7 2.7 %collective-permute-start.6 = (bf16[4,176,256]{2,1,0:T(8,128)(2,1)S(1)}, bf16[4,176,256]{2,1,0:T(8,128)(2,1)S(1)}, u32[]{:S(2)}, u32[]{:S(2)}) collective-permute-start(bf16[4,176,256]{2,1,0:T(8,128)(2,1)S(1)} %pad_maximum_fusion.refs_0_), channel_id=1, source_target_pairs={{0,6},{1,7},{2,0},{3,1},{4,2},{5,3},{6,4},{7,5},{8,14},{9,15},{10,... | collective-permute-start | bytes 1081352 | tf_op jit(solution)/shard_map/ppermute | solution.py:158
  43.4 3.0 %collective-permute-start.5 = (bf16[4,176,256]{2,1,0:T(8,128)(2,1)S(1)}, bf16[4,176,256]{2,1,0:T(8,128)(2,1)S(1)}, u32[]{:S(2)}, u32[]{:S(2)}) collective-permute-start(bf16[4,176,256]{2,1,0:T(8,128)(2,1)S(1)} %pad_maximum_fusion.refs_0_), channel_id=1, source_target_pairs={{0,4},{1,5},{2,6},{3,7},{4,0},{5,1},{6,2},{7,3},{8,12},{9,13},{10,... | collective-permute-start | bytes 1081352 | tf_op jit(solution)/shard_map/ppermute | solution.py:158
  46.5 4.0 %collective-permute-start.4 = (bf16[4,176,256]{2,1,0:T(8,128)(2,1)S(1)}, bf16[4,176,256]{2,1,0:T(8,128)(2,1)S(1)}, u32[]{:S(2)}, u32[]{:S(2)}) collective-permute-start(bf16[4,176,256]{2,1,0:T(8,128)(2,1)S(1)} %pad_maximum_fusion.refs_0_), channel_id=1, source_target_pairs={{0,2},{1,3},{2,4},{3,5},{4,6},{5,7},{6,0},{7,1},{8,10},{9,11},{10,... | collective-permute-start | bytes 1081352 | tf_op jit(solution)/shard_map/ppermute | solution.py:158
  50.5 1.9 %collective-permute-start.7 = (bf16[4,176,256]{2,1,0:T(8,128)(2,1)S(1)}, bf16[4,176,256]{2,1,0:T(8,128)(2,1)S(1)}, u32[]{:S(2)}, u32[]{:S(2)}) collective-permute-start(bf16[4,176,256]{2,1,0:T(8,128)(2,1)S(1)} %pad_maximum_fusion.refs_0_), channel_id=1, source_target_pairs={{0,1},{1,0},{2,3},{3,2},{4,5},{5,4},{6,7},{7,6},{8,9},{9,8},{10,11... | collective-permute-start | bytes 1081352 | tf_op jit(solution)/shard_map/ppermute | solution.py:158
  52.4 6.2 %collective-permute-done.6.refs_3_ = bf16[4,176,256]{2,1,0:T(8,128)(2,1)S(1)} collective-permute-done((bf16[4,176,256]{2,1,0:T(8,128)(2,1)S(1)}, bf16[4,176,256]{2,1,0:T(8,128)(2,1)S(1)}, u32[]{:S(2)}, u32[]{:S(2)}) %collective-permute-start.6) | collective-permute-done | bytes 360480 | tf_op jit(solution)/shard_map/ppermute | solution.py:158
  58.6 1.9 %collective-permute-start.10 = (bf16[4,176,256]{2,1,0:T(8,128)(2,1)S(1)}, bf16[4,176,256]{2,1,0:T(8,128)(2,1)}, u32[]{:S(2)}, u32[]{:S(2)}) collective-permute-start(bf16[4,176,256]{2,1,0:T(8,128)(2,1)S(1)} %collective-permute-done.6.refs_3_), channel_id=1, source_target_pairs={{0,1},{1,0},{2,3},{3,2},{4,5},{5,4},{6,7},{7,6},{8,9},{9,8},{10,11... | collective-permute-start | bytes 1081352 | tf_op jit(solution)/shard_map/ppermute | solution.py:158
  60.5 0.0 collective-permute-done.5.refs_2_
  60.5 2.4 %collective-permute-start.9 = (bf16[4,176,256]{2,1,0:T(8,128)(2,1)S(1)}, bf16[4,176,256]{2,1,0:T(8,128)(2,1)}, u32[]{:S(2)}, u32[]{:S(2)}) collective-permute-start(bf16[4,176,256]{2,1,0:T(8,128)(2,1)S(1)} %collective-permute-done.5.refs_2_), channel_id=1, source_target_pairs={{0,1},{1,0},{2,3},{3,2},{4,5},{5,4},{6,7},{7,6},{8,9},{9,8},{10,11... | collective-permute-start | bytes 1081352 | tf_op jit(solution)/shard_map/ppermute | solution.py:158
  62.9 0.0 collective-permute-done.4.refs_1_
  63.0 1.9 %collective-permute-start.8 = (bf16[4,176,256]{2,1,0:T(8,128)(2,1)S(1)}, bf16[4,176,256]{2,1,0:T(8,128)(2,1)}, u32[]{:S(2)}, u32[]{:S(2)}) collective-permute-start(bf16[4,176,256]{2,1,0:T(8,128)(2,1)S(1)} %collective-permute-done.4.refs_1_), channel_id=1, source_target_pairs={{0,1},{1,0},{2,3},{3,2},{4,5},{5,4},{6,7},{7,6},{8,9},{9,8},{10,11... | collective-permute-start | bytes 1081352 | tf_op jit(solution)/shard_map/ppermute | solution.py:158
  65.5 0.0 copy-done.4
  65.6 0.0 collective-permute-done.7.refs_4_
  65.6 0.0 copy-start
  65.6 0.7 copy-done
  66.4 0.0 collective-permute-done.10.refs_7_
  66.4 0.0 collective-permute-done.9.refs_6_
  66.4 0.3 collective-permute-done.8.refs_5_
  66.7 0.0 all-to-all-done.refs_8_
  66.7 0.0 copy-start.1
  66.7 1.0 copy-done.1
  67.6 37.1 %tile_products.1 = (f32[16,32,256]{2,1,0:T(8,128)S(1)}, bf16[16,32,256]{2,1,0:T(8,128)(2,1)}, bf16[16,32,256]{2,1,0:T(8,128)(2,1)S(1)}) custom-call(s32[4,128]{1,0:T(4,128)S(1)} %pad_add_fusion.slots_ref, s32[1,1]{1,0:T(1,128)} %copy.6.count_ref, bf16[4,176,256]{2,1,0:T(8,128)(2,1)S(1)} %pad_maximum_fusion.refs_0_, ...), custom_call_target="tpu_custom_call" | custom-call | tf_op jit(solution)/shard_map/tile_products/pallas_call | solution.py:126
  104.8 0.0 copy-start.2
  104.8 0.7 copy-done.2
  105.5 1.9 %collective-permute-start.11 = (bf16[16,32,256]{2,1,0:T(8,128)(2,1)}, bf16[16,32,256]{2,1,0:T(8,128)(2,1)S(1)}, u32[]{:S(2)}, u32[]{:S(2)}) collective-permute-start(bf16[16,32,256]{2,1,0:T(8,128)(2,1)} %get-tuple-element.17), channel_id=1, source_target_pairs={{0,1},{1,0},{2,3},{3,2},{4,5},{5,4},{6,7},{7,6},{8,9},{9,8},{10,11... | collective-permute-start | bytes 786440 | tf_op jit(solution)/shard_map/ppermute | solution.py:158
  107.4 3.5 %all-to-all-start.2 = ((bf16[16,32,256]{2,1,0:T(8,128)(2,1)}), bf16[16,32,256]{2,1,0:T(8,128)(2,1)S(1)}, u32[]{:S(2)}, u32[]{:S(2)}) async-start(bf16[16,32,256]{2,1,0:T(8,128)(2,1)} %copy-done.2), calls=%async_computation.2 | async-start | bytes 524288 | tf_op jit(solution)/shard_map/all_to_all | solution.py:219
  110.9 0.0 collective-permute-done.11
  110.9 0.8 add_convert_fusion
  111.7 9.1 %all-to-all-done.2 = bf16[16,32,256]{2,1,0:T(8,128)(2,1)S(1)} async-done(((bf16[16,32,256]{2,1,0:T(8,128)(2,1)}), bf16[16,32,256]{2,1,0:T(8,128)(2,1)S(1)}, u32[]{:S(2)}, u32[]{:S(2)}) %all-to-all-start.2) | async-done | bytes 262176 | tf_op jit(solution)/shard_map/all_to_all | solution.py:219
  120.9 13.0 %all-to-all-start.1 = ((bf16[16,32,256]{2,1,0:T(8,128)(2,1)}), bf16[16,32,256]{2,1,0:T(8,128)(2,1)S(1)}, u32[]{:S(2)}, u32[]{:S(2)}) async-start(bf16[16,32,256]{2,1,0:T(8,128)(2,1)} %add_convert_fusion), calls=%async_computation.1 | async-start | bytes 524288 | tf_op jit(solution)/shard_map/all_to_all | solution.py:179
  133.9 9.2 %all-to-all-done.1 = bf16[16,32,256]{2,1,0:T(8,128)(2,1)S(1)} async-done(((bf16[16,32,256]{2,1,0:T(8,128)(2,1)}), bf16[16,32,256]{2,1,0:T(8,128)(2,1)S(1)}, u32[]{:S(2)}, u32[]{:S(2)}) %all-to-all-start.1) | async-done | bytes 262176 | tf_op jit(solution)/shard_map/all_to_all | solution.py:179
  143.2 0.6 add.51
  (5 shorter events, 0.2 us)
Async XLA Ops:
  2.9 6.6 %collective-permute-start = (bf16[176,256]{1,0:T(8,128)(2,1)}, bf16[176,256]{1,0:T(8,128)(2,1)S(1)}, u32[]{:S(2)}, u32[]{:S(2)}) collective-permute-start(bf16[176,256]{1,0:T(8,128)(2,1)} %get-tuple-element.12), channel_id=1, source_target_pairs={{0,256},{32,288},{64,320},{96,352},{128,384},{160,416},{192,448},{... | collective-permute-start | bytes 270344 | tf_op jit(solution)/shard_map/ppermute | solution.py:158
  11.6 10.5 %copy-start.3 = (bf16[176,256]{1,0:T(8,128)(2,1)S(1)}, bf16[176,256]{1,0:T(8,128)(2,1)}, u32[]{:S(2)}) copy-start(bf16[176,256]{1,0:T(8,128)(2,1)} %get-tuple-element.14) | copy-start | bytes 270340
  11.6 53.9 %copy-start.4 = (s32[1,1,2,128]{3,2,1,0:T(2,128)S(1)}, s32[1,1,2,128]{3,2,1,0:T(2,128)}, u32[]{:S(2)}) copy-start(s32[1,1,2,128]{3,2,1,0:T(2,128)} %param.8) | copy-start | bytes 3076
  11.6 55.0 %all-to-all-start = ((bf16[16,176,256]{2,1,0:T(8,128)(2,1)}), bf16[16,176,256]{2,1,0:T(8,128)(2,1)S(1)}, u32[]{:S(2)}, u32[]{:S(2)}) async-start(bf16[16,176,256]{2,1,0:T(8,128)(2,1)} %bitcast.5), calls=%async_computation | async-start | bytes 2883584 | tf_op jit(solution)/shard_map/all_to_all | solution.py:179
  22.1 14.5 %collective-permute-start.3 = (bf16[176,256]{1,0:T(8,128)(2,1)S(1)}, bf16[176,256]{1,0:T(8,128)(2,1)S(1)}, u32[]{:S(2)}, u32[]{:S(2)}) collective-permute-start(bf16[176,256]{1,0:T(8,128)(2,1)S(1)} %copy-done.3), channel_id=1, source_target_pairs={{0,24},{1,25},{2,26},{3,27},{4,28},{5,29},{6,30},{7,31},{8,0},{9,1... | collective-permute-start | bytes 270344 | tf_op jit(solution)/shard_map/ppermute | solution.py:158
  28.3 11.1 %collective-permute-start.2 = (bf16[176,256]{1,0:T(8,128)(2,1)S(1)}, bf16[176,256]{1,0:T(8,128)(2,1)S(1)}, u32[]{:S(2)}, u32[]{:S(2)}) collective-permute-start(bf16[176,256]{1,0:T(8,128)(2,1)S(1)} %copy-done.3), channel_id=1, source_target_pairs={{0,16},{1,17},{2,18},{3,19},{4,20},{5,21},{6,22},{7,23},{8,24},{9,... | collective-permute-start | bytes 270344 | tf_op jit(solution)/shard_map/ppermute | solution.py:158
  32.1 8.6 %collective-permute-start.1 = (bf16[176,256]{1,0:T(8,128)(2,1)S(1)}, bf16[176,256]{1,0:T(8,128)(2,1)S(1)}, u32[]{:S(2)}, u32[]{:S(2)}) collective-permute-start(bf16[176,256]{1,0:T(8,128)(2,1)S(1)} %copy-done.3), channel_id=1, source_target_pairs={{0,8},{1,9},{2,10},{3,11},{4,12},{5,13},{6,14},{7,15},{8,16},{9,17... | collective-permute-start | bytes 270344 | tf_op jit(solution)/shard_map/ppermute | solution.py:158
  40.7 17.9 %collective-permute-start.6 = (bf16[4,176,256]{2,1,0:T(8,128)(2,1)S(1)}, bf16[4,176,256]{2,1,0:T(8,128)(2,1)S(1)}, u32[]{:S(2)}, u32[]{:S(2)}) collective-permute-start(bf16[4,176,256]{2,1,0:T(8,128)(2,1)S(1)} %pad_maximum_fusion.refs_0_), channel_id=1, source_target_pairs={{0,6},{1,7},{2,0},{3,1},{4,2},{5,3},{6,4},{7,5},{8,14},{9,15},{10,... | collective-permute-start | bytes 1081352 | tf_op jit(solution)/shard_map/ppermute | solution.py:158
  43.4 17.1 %collective-permute-start.5 = (bf16[4,176,256]{2,1,0:T(8,128)(2,1)S(1)}, bf16[4,176,256]{2,1,0:T(8,128)(2,1)S(1)}, u32[]{:S(2)}, u32[]{:S(2)}) collective-permute-start(bf16[4,176,256]{2,1,0:T(8,128)(2,1)S(1)} %pad_maximum_fusion.refs_0_), channel_id=1, source_target_pairs={{0,4},{1,5},{2,6},{3,7},{4,0},{5,1},{6,2},{7,3},{8,12},{9,13},{10,... | collective-permute-start | bytes 1081352 | tf_op jit(solution)/shard_map/ppermute | solution.py:158
  46.5 16.5 %collective-permute-start.4 = (bf16[4,176,256]{2,1,0:T(8,128)(2,1)S(1)}, bf16[4,176,256]{2,1,0:T(8,128)(2,1)S(1)}, u32[]{:S(2)}, u32[]{:S(2)}) collective-permute-start(bf16[4,176,256]{2,1,0:T(8,128)(2,1)S(1)} %pad_maximum_fusion.refs_0_), channel_id=1, source_target_pairs={{0,2},{1,3},{2,4},{3,5},{4,6},{5,7},{6,0},{7,1},{8,10},{9,11},{10,... | collective-permute-start | bytes 1081352 | tf_op jit(solution)/shard_map/ppermute | solution.py:158
  50.5 15.1 %collective-permute-start.7 = (bf16[4,176,256]{2,1,0:T(8,128)(2,1)S(1)}, bf16[4,176,256]{2,1,0:T(8,128)(2,1)S(1)}, u32[]{:S(2)}, u32[]{:S(2)}) collective-permute-start(bf16[4,176,256]{2,1,0:T(8,128)(2,1)S(1)} %pad_maximum_fusion.refs_0_), channel_id=1, source_target_pairs={{0,1},{1,0},{2,3},{3,2},{4,5},{5,4},{6,7},{7,6},{8,9},{9,8},{10,11... | collective-permute-start | bytes 1081352 | tf_op jit(solution)/shard_map/ppermute | solution.py:158
  58.6 7.8 %collective-permute-start.10 = (bf16[4,176,256]{2,1,0:T(8,128)(2,1)S(1)}, bf16[4,176,256]{2,1,0:T(8,128)(2,1)}, u32[]{:S(2)}, u32[]{:S(2)}) collective-permute-start(bf16[4,176,256]{2,1,0:T(8,128)(2,1)S(1)} %collective-permute-done.6.refs_3_), channel_id=1, source_target_pairs={{0,1},{1,0},{2,3},{3,2},{4,5},{5,4},{6,7},{7,6},{8,9},{9,8},{10,11... | collective-permute-start | bytes 1081352 | tf_op jit(solution)/shard_map/ppermute | solution.py:158
  60.5 5.8 %collective-permute-start.9 = (bf16[4,176,256]{2,1,0:T(8,128)(2,1)S(1)}, bf16[4,176,256]{2,1,0:T(8,128)(2,1)}, u32[]{:S(2)}, u32[]{:S(2)}) collective-permute-start(bf16[4,176,256]{2,1,0:T(8,128)(2,1)S(1)} %collective-permute-done.5.refs_2_), channel_id=1, source_target_pairs={{0,1},{1,0},{2,3},{3,2},{4,5},{5,4},{6,7},{7,6},{8,9},{9,8},{10,11... | collective-permute-start | bytes 1081352 | tf_op jit(solution)/shard_map/ppermute | solution.py:158
  63.0 3.7 %collective-permute-start.8 = (bf16[4,176,256]{2,1,0:T(8,128)(2,1)S(1)}, bf16[4,176,256]{2,1,0:T(8,128)(2,1)}, u32[]{:S(2)}, u32[]{:S(2)}) collective-permute-start(bf16[4,176,256]{2,1,0:T(8,128)(2,1)S(1)} %collective-permute-done.4.refs_1_), channel_id=1, source_target_pairs={{0,1},{1,0},{2,3},{3,2},{4,5},{5,4},{6,7},{7,6},{8,9},{9,8},{10,11... | collective-permute-start | bytes 1081352 | tf_op jit(solution)/shard_map/ppermute | solution.py:158
  65.6 0.8 copy-start
  66.7 1.0 copy-start.1
  104.8 0.7 copy-start.2
  105.5 5.5 %collective-permute-start.11 = (bf16[16,32,256]{2,1,0:T(8,128)(2,1)}, bf16[16,32,256]{2,1,0:T(8,128)(2,1)S(1)}, u32[]{:S(2)}, u32[]{:S(2)}) collective-permute-start(bf16[16,32,256]{2,1,0:T(8,128)(2,1)} %get-tuple-element.17), channel_id=1, source_target_pairs={{0,1},{1,0},{2,3},{3,2},{4,5},{5,4},{6,7},{7,6},{8,9},{9,8},{10,11... | collective-permute-start | bytes 786440 | tf_op jit(solution)/shard_map/ppermute | solution.py:158
  107.4 13.5 %all-to-all-start.2 = ((bf16[16,32,256]{2,1,0:T(8,128)(2,1)}), bf16[16,32,256]{2,1,0:T(8,128)(2,1)S(1)}, u32[]{:S(2)}, u32[]{:S(2)}) async-start(bf16[16,32,256]{2,1,0:T(8,128)(2,1)} %copy-done.2), calls=%async_computation.2 | async-start | bytes 524288 | tf_op jit(solution)/shard_map/all_to_all | solution.py:219
  120.9 22.3 %all-to-all-start.1 = ((bf16[16,32,256]{2,1,0:T(8,128)(2,1)}), bf16[16,32,256]{2,1,0:T(8,128)(2,1)S(1)}, u32[]{:S(2)}, u32[]{:S(2)}) async-start(bf16[16,32,256]{2,1,0:T(8,128)(2,1)} %add_convert_fusion), calls=%async_computation.1 | async-start | bytes 524288 | tf_op jit(solution)/shard_map/all_to_all | solution.py:179

commit v3 on v2

--- a/solution.py
+++ b/solution.py
@@ -14,12 +14,13 @@
 DEPTH = DESC + AUG
 PACK = DEPTH + VECS
 FULL = 256
+LANES = 128
 UNROLL = 8
 
 COL_SIZES = (4, 4, 2)
 ROW_SIZES = (2, 8)
 ROW_PARTS = 8
-COL_PARTS = 1
+COL_PARTS = 2
 
 POWER = math.log2(math.e) * 2.0 / DESC
 
@@ -42,23 +43,30 @@
 
     descriptors = turned.astype(jnp.bfloat16)
     narrow = vec_ref[...].astype(jnp.bfloat16)
-    for ref, rows in ((row_ref, offset_rows(0, 3)), (col_ref, offset_rows(3, 0))):
-        ref[0:DESC, :] = descriptors
-        ref[DESC:DEPTH, :] = rows
-        ref[DEPTH:PACK, :] = narrow
+    row_offsets, col_offsets = offset_rows(0, 3), offset_rows(3, 0)
+    row_ref[0:DESC, :] = descriptors
+    row_ref[DESC:DEPTH, :] = row_offsets
+    row_ref[DEPTH:PACK, :] = narrow
+    for copy in range(col_ref.shape[0]):
+        col_ref[copy, 0:DESC, :] = descriptors
+        col_ref[copy, DESC:DEPTH, :] = col_offsets
+        col_ref[copy, DEPTH:PACK, :] = narrow
 
 
 def pack_blocks(features, scales, vectors):
-    shape = jax.ShapeDtypeStruct((PACK, TILE), jnp.bfloat16)
-    return pl.pallas_call(pack_kernel, out_shape=(shape, shape), name="pack_blocks")(
+    shapes = (
+        jax.ShapeDtypeStruct((PACK, TILE), jnp.bfloat16),
+        jax.ShapeDtypeStruct((ROW_SIZES[1], PACK, TILE), jnp.bfloat16),
+    )
+    return pl.pallas_call(pack_kernel, out_shape=shapes, name="pack_blocks")(
         features, scales.reshape(1, TILE), vectors
     )
 
 
 def tiles_kernel(slots_ref, count_ref, *refs):
     rows_from, cols_from = refs[:ROW_PARTS], refs[ROW_PARTS : ROW_PARTS + COL_PARTS]
-    forward_ref, other_ref, mirror_ref = refs[ROW_PARTS + COL_PARTS : ROW_PARTS + COL_PARTS + 3]
-    rows_ref, cols_ref, turned_ref, fsum_ref, msum_ref, row_sems, col_sems = refs[ROW_PARTS + COL_PARTS + 3 :]
+    forward_ref, forward_other_ref, mirror_ref, mirror_other_ref = refs[ROW_PARTS + COL_PARTS :][:4]
+    rows_ref, cols_ref, turned_ref, vecs_ref, fsum_ref, msum_ref, row_sems, col_sems = refs[ROW_PARTS + COL_PARTS + 4 :]
     row_span = rows_ref.shape[0]
     col_span = cols_ref.shape[0]
 
@@ -93,14 +101,17 @@
     for copy in col_copies:
         copy.wait()
 
+    @pl.loop(0, col_span)
+    def _(block):
+        narrow = cols_ref[block, DEPTH:PACK, :]
+        vecs_ref[block] = jnp.concatenate([narrow, jnp.zeros((LANES - VECS, TILE), jnp.bfloat16)], axis=0).T
+
     def tile(slot):
         row_at = slots_ref[0, slot]
         col_at = slots_ref[1, slot]
         score = jnp.dot(turned_ref[row_at], cols_ref[col_at], preferred_element_type=jnp.float32)
         block = jnp.exp2(score * POWER).astype(jnp.bfloat16)
-        forward = lax.dot_general(
-            cols_ref[col_at, DEPTH:PACK, :], block, (((1,), (1,)), ((), ())), preferred_element_type=jnp.float32
-        )
+        forward = jnp.dot(block, vecs_ref[col_at], preferred_element_type=jnp.float32)
         mirror = jnp.dot(rows_ref[row_at, DEPTH:PACK, :], block, preferred_element_type=jnp.float32)
         return slots_ref[2, slot], slots_ref[3, slot], forward, mirror
 
@@ -112,9 +123,14 @@
             msum_ref[mirror_at] += mirror
 
     half = row_span // 2
-    forward_ref[...] = fsum_ref[0:half]
-    other_ref[...] = fsum_ref[half:row_span].astype(jnp.bfloat16)
-    mirror_ref[...] = msum_ref[0:col_span].astype(jnp.bfloat16)
+
+    @pl.loop(0, half)
+    def _(block):
+        forward_ref[block] = fsum_ref[block].T[0:VECS]
+        forward_other_ref[block] = fsum_ref[half + block].T[0:VECS].astype(jnp.bfloat16)
+
+    mirror_ref[...] = msum_ref[0 : col_span // 2]
+    mirror_other_ref[...] = msum_ref[col_span // 2 : col_span].astype(jnp.bfloat16)
 
 
 def tile_products(slots, tile_count, row_parts, col_parts):
@@ -128,15 +144,17 @@
         out_shape=(
             jax.ShapeDtypeStruct((row_span // 2, VECS, TILE), jnp.float32),
             jax.ShapeDtypeStruct((row_span // 2, VECS, TILE), jnp.bfloat16),
-            jax.ShapeDtypeStruct((col_span, VECS, TILE), jnp.bfloat16),
+            jax.ShapeDtypeStruct((col_span // 2, VECS, TILE), jnp.float32),
+            jax.ShapeDtypeStruct((col_span // 2, VECS, TILE), jnp.bfloat16),
         ),
         in_specs=[smem, smem] + [anywhere] * (ROW_PARTS + COL_PARTS),
-        out_specs=(vmem, vmem, vmem),
+        out_specs=(vmem, vmem, vmem, vmem),
         scratch_shapes=[
             pltpu.VMEM((row_span, PACK, TILE), jnp.bfloat16),
             pltpu.VMEM((col_span, FULL, TILE), jnp.bfloat16),
             pltpu.VMEM((row_span, TILE, FULL), jnp.bfloat16),
-            pltpu.VMEM((row_span + 1, VECS, TILE), jnp.float32),
+            pltpu.VMEM((col_span, TILE, LANES), jnp.bfloat16),
+            pltpu.VMEM((row_span + 1, TILE, LANES), jnp.float32),
             pltpu.VMEM((col_span + 1, VECS, TILE), jnp.float32),
             pltpu.SemaphoreType.DMA((ROW_PARTS,)),
             pltpu.SemaphoreType.DMA((COL_PARTS,)),
@@ -146,16 +164,24 @@
     )(slots, tile_count, *row_parts, *col_parts)
 
 
-def shifted(value, axis, sizes, part, distance):
+def moved(value, axis, sizes, part, place_to):
     pairs = []
     for source in range(math.prod(sizes)):
         place = list(split_index(source, sizes))
-        place[part] = (place[part] + distance) % sizes[part]
+        place[part] = place_to(place[part])
         target = 0
         for at, size in zip(place, sizes):
             target = target * size + at
         pairs.append((source, target))
     return lax.ppermute(value, axis, pairs)
+
+
+def shifted(value, axis, sizes, part, distance):
+    return moved(value, axis, sizes, part, lambda place: (place + distance) % sizes[part])
+
+
+def swapped(value, axis, sizes, part, bit):
+    return moved(value, axis, sizes, part, lambda place: place ^ bit)
 
 
 def split_index(index, sizes):
@@ -179,13 +205,20 @@
     return lax.all_to_all(value, axis, 0, 0, axis_index_groups=list(groups.values()), tiled=True)
 
 
-def gather_pair(own):
-    pair = jnp.stack([own, shifted(own, "row", ROW_SIZES, 0, 1)])
-    return jnp.broadcast_to(pair[None], (ROW_SIZES[1],) + pair.shape).reshape((-1,) + own.shape)
-
-
-def gather_cols(pairs):
-    return [grouped_all_to_all(pairs, "row", ROW_SIZES, lambda place: place[0])]
+def gather_cols(copies):
+    along_z = grouped_all_to_all(copies, "row", ROW_SIZES, lambda place: place[0])
+    return [along_z, swapped(along_z, "row", ROW_SIZES, 0, 1)]
+
+
+def add_mirrors(mirror, for_neighbour, after):
+    mirror = mirror + swapped(for_neighbour, "row", ROW_SIZES, 0, 1).astype(jnp.float32)
+    bit = ROW_SIZES[1] // 2
+    while bit:
+        sent = mirror[bit:].astype(jnp.bfloat16) if bit > 2 else mirror[bit:]
+        sent, _ = lax.optimization_barrier((sent, after))
+        mirror = mirror[:bit] + swapped(sent, "row", ROW_SIZES, 1, bit).astype(jnp.float32)
+        bit //= 2
+    return mirror[0]
 
 
 def slot_places(tile_pairs, tile_count):
@@ -201,25 +234,24 @@
     return jnp.stack(
         [
             (core * 4 + x) * 4 + y_hi,
-            row_there[1] * 2 + (row_there[0] ^ row_here[0]),
+            (row_there[0] ^ row_here[0]) * (col_span // 2) + row_there[1],
             jnp.where(live, core * (row_span // 2) + (local_row >> 1), row_span),
-            jnp.where(live & (i != j), local_col, col_span),
+            jnp.where(live & (i != j), local_col ^ lax.axis_index("row"), col_span),
         ]
     )
 
 
 def body(features, scales, vectors, pattern, counts):
-    row_own, col_own = pack_blocks(features, scales, vectors)
-    pairs, row_own = lax.optimization_barrier((gather_pair(col_own), row_own))
-    col_parts = gather_cols(pairs)
+    row_own, col_copies = pack_blocks(features, scales, vectors)
+    col_parts = gather_cols(col_copies)
     row_parts = gather_rows(row_own)
     slots = slot_places(pattern[0, 0], counts[0, 0])
-    forward, for_other_core, mirror = tile_products(slots, counts, row_parts, col_parts)
-    for_other_core = shifted(for_other_core, "col", COL_SIZES, 2, 1)
-    mirror = lax.all_to_all(mirror, "row", 0, 0, tiled=True)
+    forward, for_other_core, mirror, for_neighbour = tile_products(slots, counts, row_parts, col_parts)
+    for_other_core = swapped(for_other_core, "col", COL_SIZES, 2, 1)
     forward = (forward + for_other_core.astype(jnp.float32)).astype(jnp.bfloat16)
+    mirror = add_mirrors(mirror, for_neighbour, forward)
     forward = grouped_all_to_all(forward, "col", COL_SIZES, lambda place: place[2])
-    return jnp.sum(forward.astype(jnp.float32), axis=0) + jnp.sum(mirror.astype(jnp.float32), axis=0)
+    return jnp.sum(forward.astype(jnp.float32), axis=0) + mirror
 
 
 def solution(mesh):

time: 146 us -> 127 us (0.87); the launches traced: 144 us -> 127 us
  waiting for transfers between devices: 32 us -> 23.2 us
  Pallas kernels: 38.8 us -> 35.1 us
  local copies, waits for them, and re-layouts: 4.86 us -> 1.92 us
    ppermute x12 -> x16, waiting for transfers between devices: 13.7 us -> 23 us  [moved(): return lax.ppermute(value, axis, pairs)]
    all_to_all x1 -> x0, waiting for transfers between devices: 9.15 us -> none  [body(): mirror = lax.all_to_all(mirror, 'row', 0, 0, tiled=True)]
    all_to_all x2, waiting for transfers between devices: 9.2 us -> 0.25 us  [grouped_all_to_all(): lax.all_to_all(value, axis, 0, 0, axis_index_groups=list(groups.values())...]
    ppermute x12 -> x16, starting transfers between devices: 37.8 us -> 46.6 us  [moved(): return lax.ppermute(value, axis, pairs)]
    all_to_all x2, starting transfers between devices: 23.5 us -> 17.2 us  [grouped_all_to_all(): lax.all_to_all(value, axis, 0, 0, axis_index_groups=list(groups.values())...]
    pallas_call x1, Pallas kernels: 37.1 us -> 33.2 us  [tile_products(): pl.pallas_call(tiles_kernel, out_shape=(jax.ShapeDtypeStruct((row_span //...]
    all_to_all x1 -> x0, starting transfers between devices: 3.54 us -> none  [body(): mirror = lax.all_to_all(mirror, 'row', 0, 0, tiled=True)]
    unnamed x10 -> x4, local copies, waits for them, and re-layouts: 2.43 us -> 0.68 us
  transfers between devices with their start and end apart: 15 -> 18, of which waited for: 7 -> 9; matrix products, arithmetic and copies ran while one was open for 1% -> 0% of each run, Pallas kernels for 0% -> 0%
where the time goes in v3:
time: 127 us
  starting transfers between devices  63.9 us (50%)
  Pallas kernels  35.1 us (28%)
  waiting for transfers between devices  23.2 us (18%)
  local copies, waits for them, and re-layouts  1.92 us (2%)
  other arithmetic  1.56 us (1%)
    ppermute x16, starting transfers between devices, moved(): return lax.ppermute(value, axis, pairs)  46.6 us
    pallas_call x1, Pallas kernels, tile_products(): pl.pallas_call(tiles_kernel, out_shape=(jax.ShapeDtypeStruct((row_span //...  33.2 us
    ppermute x16, waiting for transfers between devices, moved(): return lax.ppermute(value, axis, pairs)  23 us
    all_to_all x2, starting transfers between devices, grouped_all_to_all(): lax.all_to_all(value, axis, 0, 0, axis_index_groups=list(groups.values())...  17.2 us
  transfers between devices with their start and end apart: 18, of which 9 were waited for; matrix products, arithmetic and copies ran while one was open for 0% of the time, Pallas kernels for 0%

profile of v3, /device:TPU:6, one launch (start us, length us, event | category | flops | bytes accessed | tf_op | source)
XLA Modules:
  0.0 126.6 jit_solution(5495755352080037362)
XLA Ops:
  0.0 1.2 reshape.206.scale_ref
  1.2 1.9 %pack_blocks.1 = (bf16[176,256]{1,0:T(8,128)(2,1)}, bf16[8,176,256]{2,1,0:T(8,128)(2,1)}) custom-call(bf16[256,128]{1,0:T(8,128)(2,1)} %feat_ref.1, bf16[1,256]{1,0:T(2,128)(2,1)} %reshape.206.scale_ref, f32[32,256]{1,0:T(8,128)} %vec_ref.1), custom_call_target="tpu_custom_call" | custom-call | tf_op jit(solution)/shard_map/pack_blocks/pallas_call | solution.py:61
  3.1 0.0 copy-start
  3.1 10.4 %all-to-all-start = ((bf16[8,176,256]{2,1,0:T(8,128)(2,1)}), bf16[8,176,256]{2,1,0:T(8,128)(2,1)S(1)}, u32[]{:S(2)}, u32[]{:S(2)}) async-start(bf16[8,176,256]{2,1,0:T(8,128)(2,1)} %get-tuple-element.15), calls=%async_computation | async-start | bytes 1441792 | tf_op jit(solution)/shard_map/all_to_all | solution.py:205
  13.6 0.0 copy-done
  13.6 6.2 %collective-permute-start.2 = (bf16[176,256]{1,0:T(8,128)(2,1)S(1)}, bf16[176,256]{1,0:T(8,128)(2,1)S(1)}, u32[]{:S(2)}, u32[]{:S(2)}) collective-permute-start(bf16[176,256]{1,0:T(8,128)(2,1)S(1)} %copy-done), channel_id=1, source_target_pairs={{0,24},{1,25},{2,26},{3,27},{4,28},{5,29},{6,30},{7,31},{8,0},{9,1... | collective-permute-start | bytes 270344 | tf_op jit(solution)/shard_map/ppermute | solution.py:176
  19.7 3.8 %collective-permute-start.1 = (bf16[176,256]{1,0:T(8,128)(2,1)S(1)}, bf16[176,256]{1,0:T(8,128)(2,1)S(1)}, u32[]{:S(2)}, u32[]{:S(2)}) collective-permute-start(bf16[176,256]{1,0:T(8,128)(2,1)S(1)} %copy-done), channel_id=1, source_target_pairs={{0,16},{1,17},{2,18},{3,19},{4,20},{5,21},{6,22},{7,23},{8,24},{9,... | collective-permute-start | bytes 270344 | tf_op jit(solution)/shard_map/ppermute | solution.py:176
  23.6 4.5 %collective-permute-start = (bf16[176,256]{1,0:T(8,128)(2,1)S(1)}, bf16[176,256]{1,0:T(8,128)(2,1)S(1)}, u32[]{:S(2)}, u32[]{:S(2)}) collective-permute-start(bf16[176,256]{1,0:T(8,128)(2,1)S(1)} %copy-done), channel_id=1, source_target_pairs={{0,8},{1,9},{2,10},{3,11},{4,12},{5,13},{6,14},{7,15},{8,16},{9,17... | collective-permute-start | bytes 270344 | tf_op jit(solution)/shard_map/ppermute | solution.py:176
  28.1 0.0 collective-permute-done.2
  28.1 4.6 %collective-permute-done.1 = bf16[176,256]{1,0:T(8,128)(2,1)S(1)} collective-permute-done((bf16[176,256]{1,0:T(8,128)(2,1)S(1)}, bf16[176,256]{1,0:T(8,128)(2,1)S(1)}, u32[]{:S(2)}, u32[]{:S(2)}) %collective-permute-start.1) | collective-permute-done | bytes 90144 | tf_op jit(solution)/shard_map/ppermute | solution.py:176
  32.7 0.0 collective-permute-done
  32.8 2.7 %collective-permute-start.5 = (bf16[4,176,256]{2,1,0:T(8,128)(2,1)S(1)}, bf16[4,176,256]{2,1,0:T(8,128)(2,1)S(1)}, u32[]{:S(2)}, u32[]{:S(2)}) collective-permute-start(bf16[4,176,256]{2,1,0:T(8,128)(2,1)S(1)} %pad_maximum_fusion.refs_0_), channel_id=1, source_target_pairs={{0,6},{1,7},{2,0},{3,1},{4,2},{5,3},{6,4},{7,5},{8,14},{9,15},{10,... | collective-permute-start | bytes 1081352 | tf_op jit(solution)/shard_map/ppermute | solution.py:176
  35.5 3.0 %collective-permute-start.4 = (bf16[4,176,256]{2,1,0:T(8,128)(2,1)S(1)}, bf16[4,176,256]{2,1,0:T(8,128)(2,1)S(1)}, u32[]{:S(2)}, u32[]{:S(2)}) collective-permute-start(bf16[4,176,256]{2,1,0:T(8,128)(2,1)S(1)} %pad_maximum_fusion.refs_0_), channel_id=1, source_target_pairs={{0,4},{1,5},{2,6},{3,7},{4,0},{5,1},{6,2},{7,3},{8,12},{9,13},{10,... | collective-permute-start | bytes 1081352 | tf_op jit(solution)/shard_map/ppermute | solution.py:176
  38.5 4.0 %collective-permute-start.3 = (bf16[4,176,256]{2,1,0:T(8,128)(2,1)S(1)}, bf16[4,176,256]{2,1,0:T(8,128)(2,1)S(1)}, u32[]{:S(2)}, u32[]{:S(2)}) collective-permute-start(bf16[4,176,256]{2,1,0:T(8,128)(2,1)S(1)} %pad_maximum_fusion.refs_0_), channel_id=1, source_target_pairs={{0,2},{1,3},{2,4},{3,5},{4,6},{5,7},{6,0},{7,1},{8,10},{9,11},{10,... | collective-permute-start | bytes 1081352 | tf_op jit(solution)/shard_map/ppermute | solution.py:176
  42.5 0.0 all-to-all-done.refs_8_
  42.5 4.7 %collective-permute-start.10 = (bf16[8,176,256]{2,1,0:T(8,128)(2,1)S(1)}, bf16[8,176,256]{2,1,0:T(8,128)(2,1)S(1)}, u32[]{:S(2)}, u32[]{:S(2)}) collective-permute-start(bf16[8,176,256]{2,1,0:T(8,128)(2,1)S(1)} %all-to-all-done.refs_8_), channel_id=1, source_target_pairs={{0,256},{32,288},{64,320},{96,352},{128,384},{160,416},{192,448},{... | collective-permute-start | bytes 2162696 | tf_op jit(solution)/shard_map/ppermute | solution.py:176
  47.2 1.9 %collective-permute-start.6 = (bf16[4,176,256]{2,1,0:T(8,128)(2,1)S(1)}, bf16[4,176,256]{2,1,0:T(8,128)(2,1)S(1)}, u32[]{:S(2)}, u32[]{:S(2)}) collective-permute-start(bf16[4,176,256]{2,1,0:T(8,128)(2,1)S(1)} %pad_maximum_fusion.refs_0_), channel_id=1, source_target_pairs={{0,1},{1,0},{2,3},{3,2},{4,5},{5,4},{6,7},{7,6},{8,9},{9,8},{10,11... | collective-permute-start | bytes 1081352 | tf_op jit(solution)/shard_map/ppermute | solution.py:176
  49.1 2.5 %collective-permute-done.5.refs_3_ = bf16[4,176,256]{2,1,0:T(8,128)(2,1)S(1)} collective-permute-done((bf16[4,176,256]{2,1,0:T(8,128)(2,1)S(1)}, bf16[4,176,256]{2,1,0:T(8,128)(2,1)S(1)}, u32[]{:S(2)}, u32[]{:S(2)}) %collective-permute-start.5) | collective-permute-done | bytes 360480 | tf_op jit(solution)/shard_map/ppermute | solution.py:176
  51.7 1.9 %collective-permute-start.9 = (bf16[4,176,256]{2,1,0:T(8,128)(2,1)S(1)}, bf16[4,176,256]{2,1,0:T(8,128)(2,1)}, u32[]{:S(2)}, u32[]{:S(2)}) collective-permute-start(bf16[4,176,256]{2,1,0:T(8,128)(2,1)S(1)} %collective-permute-done.5.refs_3_), channel_id=1, source_target_pairs={{0,1},{1,0},{2,3},{3,2},{4,5},{5,4},{6,7},{7,6},{8,9},{9,8},{10,11... | collective-permute-start | bytes 1081352 | tf_op jit(solution)/shard_map/ppermute | solution.py:176
  53.6 0.0 collective-permute-done.4.refs_2_
  53.6 2.4 %collective-permute-start.8 = (bf16[4,176,256]{2,1,0:T(8,128)(2,1)S(1)}, bf16[4,176,256]{2,1,0:T(8,128)(2,1)}, u32[]{:S(2)}, u32[]{:S(2)}) collective-permute-start(bf16[4,176,256]{2,1,0:T(8,128)(2,1)S(1)} %collective-permute-done.4.refs_2_), channel_id=1, source_target_pairs={{0,1},{1,0},{2,3},{3,2},{4,5},{5,4},{6,7},{7,6},{8,9},{9,8},{10,11... | collective-permute-start | bytes 1081352 | tf_op jit(solution)/shard_map/ppermute | solution.py:176
  56.0 0.0 collective-permute-done.3.refs_1_
  56.0 1.9 %collective-permute-start.7 = (bf16[4,176,256]{2,1,0:T(8,128)(2,1)S(1)}, bf16[4,176,256]{2,1,0:T(8,128)(2,1)}, u32[]{:S(2)}, u32[]{:S(2)}) collective-permute-start(bf16[4,176,256]{2,1,0:T(8,128)(2,1)S(1)} %collective-permute-done.3.refs_1_), channel_id=1, source_target_pairs={{0,1},{1,0},{2,3},{3,2},{4,5},{5,4},{6,7},{7,6},{8,9},{9,8},{10,11... | collective-permute-start | bytes 1081352 | tf_op jit(solution)/shard_map/ppermute | solution.py:176
  58.6 0.0 copy-start.1
  58.6 0.7 copy-done.1
  59.3 0.0 collective-permute-done.6.refs_4_
  59.3 0.0 collective-permute-done.9.refs_7_
  59.3 0.0 collective-permute-done.8.refs_6_
  59.4 0.4 collective-permute-done.7.refs_5_
  59.7 2.3 %collective-permute-done.10.refs_9_ = bf16[8,176,256]{2,1,0:T(8,128)(2,1)S(1)} collective-permute-done((bf16[8,176,256]{2,1,0:T(8,128)(2,1)S(1)}, bf16[8,176,256]{2,1,0:T(8,128)(2,1)S(1)}, u32[]{:S(2)}, u32[]{:S(2)}) %collective-permute-start.10) | collective-permute-done | bytes 720928 | tf_op jit(solution)/shard_map/ppermute | solution.py:176
  62.1 33.2 %tile_products.1 = (f32[16,32,256]{2,1,0:T(8,128)S(1)}, bf16[16,32,256]{2,1,0:T(8,128)(2,1)S(1)}, f32[8,32,256]{2,1,0:T(8,128)S(1)}, bf16[8,32,256]{2,1,0:T(8,128)(2,1)S(1)}) custom-call(s32[4,128]{1,0:T(4,128)S(1)} %pad_add_fusion.slots_ref, s32[1,1]{1,0:T(1,128)} %copy.6.count_ref, bf16[4,176,256]{2,1,0:T(8,128)(2,1)S(1)} %pad_maximum_fusion.refs_0_, ...), custom_call_target="tpu_custom_call" | custom-call | tf_op jit(solution)/shard_map/tile_products/pallas_call | solution.py:142
  95.3 1.9 %collective-permute-start.12 = (bf16[8,32,256]{2,1,0:T(8,128)(2,1)S(1)}, bf16[8,32,256]{2,1,0:T(8,128)(2,1)S(1)}, u32[]{:S(2)}, u32[]{:S(2)}) collective-permute-start(bf16[8,32,256]{2,1,0:T(8,128)(2,1)S(1)} %get-tuple-element.19), channel_id=1, source_target_pairs={{0,256},{32,288},{64,320},{96,352},{128,384},{160,416},{192,448},{... | collective-permute-start | bytes 393224 | tf_op jit(solution)/shard_map/ppermute | solution.py:176
  97.2 1.9 %collective-permute-start.11 = (bf16[16,32,256]{2,1,0:T(8,128)(2,1)S(1)}, bf16[16,32,256]{2,1,0:T(8,128)(2,1)S(1)}, u32[]{:S(2)}, u32[]{:S(2)}) collective-permute-start(bf16[16,32,256]{2,1,0:T(8,128)(2,1)S(1)} %get-tuple-element.17), channel_id=1, source_target_pairs={{0,1},{1,0},{2,3},{3,2},{4,5},{5,4},{6,7},{7,6},{8,9},{9,8},{10,11... | collective-permute-start | bytes 786440 | tf_op jit(solution)/shard_map/ppermute | solution.py:176
  99.1 3.0 %collective-permute-done.12 = bf16[8,32,256]{2,1,0:T(8,128)(2,1)S(1)} collective-permute-done((bf16[8,32,256]{2,1,0:T(8,128)(2,1)S(1)}, bf16[8,32,256]{2,1,0:T(8,128)(2,1)S(1)}, u32[]{:S(2)}, u32[]{:S(2)}) %collective-permute-start.12) | collective-permute-done | bytes 131104 | tf_op jit(solution)/shard_map/ppermute | solution.py:176
  102.2 0.0 collective-permute-done.11
  102.2 0.8 add_convert_fusion
  103.0 1.9 %collective-permute-start.13 = (bf16[4,32,256]{2,1,0:T(8,128)(2,1)S(1)}, bf16[4,32,256]{2,1,0:T(8,128)(2,1)S(1)}, u32[]{:S(2)}, u32[]{:S(2)}) collective-permute-start(bf16[4,32,256]{2,1,0:T(8,128)(2,1)S(1)} %slice.61), channel_id=1, source_target_pairs={{0,128},{32,160},{64,192},{96,224},{128,0},{160,32},{192,64},{224,... | collective-permute-start | bytes 196616 | tf_op jit(solution)/shard_map/ppermute | solution.py:176
  104.9 6.8 %all-to-all-start.1 = ((bf16[16,32,256]{2,1,0:T(8,128)(2,1)}), bf16[16,32,256]{2,1,0:T(8,128)(2,1)S(1)}, u32[]{:S(2)}, u32[]{:S(2)}) async-start(bf16[16,32,256]{2,1,0:T(8,128)(2,1)} %add_convert_fusion), calls=%async_computation.1 | async-start | bytes 524288 | tf_op jit(solution)/shard_map/all_to_all | solution.py:205
  111.7 1.4 %collective-permute-done.13 = bf16[4,32,256]{2,1,0:T(8,128)(2,1)S(1)} collective-permute-done((bf16[4,32,256]{2,1,0:T(8,128)(2,1)S(1)}, bf16[4,32,256]{2,1,0:T(8,128)(2,1)S(1)}, u32[]{:S(2)}, u32[]{:S(2)}) %collective-permute-start.13) | collective-permute-done | bytes 65568 | tf_op jit(solution)/shard_map/ppermute | solution.py:176
  113.1 1.9 %collective-permute-start.14 = (f32[2,32,256]{2,1,0:T(8,128)S(1)}, f32[2,32,256]{2,1,0:T(8,128)S(1)}, u32[]{:S(2)}, u32[]{:S(2)}) collective-permute-start(f32[2,32,256]{2,1,0:T(8,128)S(1)} %slice.38), channel_id=1, source_target_pairs={{0,64},{32,96},{64,0},{96,32},{128,192},{160,224},{192,128},{224,1... | collective-permute-start | bytes 196616 | tf_op jit(solution)/shard_map/ppermute | solution.py:176
  115.0 5.1 %collective-permute-done.14 = f32[2,32,256]{2,1,0:T(8,128)S(1)} collective-permute-done((f32[2,32,256]{2,1,0:T(8,128)S(1)}, f32[2,32,256]{2,1,0:T(8,128)S(1)}, u32[]{:S(2)}, u32[]{:S(2)}) %collective-permute-start.14) | collective-permute-done | bytes 65568 | tf_op jit(solution)/shard_map/ppermute | solution.py:176
  120.1 1.9 %collective-permute-start.15 = (f32[1,32,256]{2,1,0:T(8,128)S(1)}, f32[1,32,256]{2,1,0:T(8,128)S(1)}, u32[]{:S(2)}, u32[]{:S(2)}) collective-permute-start(f32[1,32,256]{2,1,0:T(8,128)S(1)} %slice.40), channel_id=1, source_target_pairs={{0,32},{32,0},{64,96},{96,64},{128,160},{160,128},{192,224},{224,1... | collective-permute-start | bytes 98312 | tf_op jit(solution)/shard_map/ppermute | solution.py:176
  122.1 0.2 all-to-all-done.1
  122.4 3.6 %collective-permute-done.15 = f32[1,32,256]{2,1,0:T(8,128)S(1)} collective-permute-done((f32[1,32,256]{2,1,0:T(8,128)S(1)}, f32[1,32,256]{2,1,0:T(8,128)S(1)}, u32[]{:S(2)}, u32[]{:S(2)}) %collective-permute-start.15) | collective-permute-done | bytes 32800 | tf_op jit(solution)/shard_map/ppermute | solution.py:176
  126.0 0.6 fusion.1
  (10 shorter events, 0.2 us)
Async XLA Ops:
  3.1 10.5 %copy-start = (bf16[176,256]{1,0:T(8,128)(2,1)S(1)}, bf16[176,256]{1,0:T(8,128)(2,1)}, u32[]{:S(2)}) copy-start(bf16[176,256]{1,0:T(8,128)(2,1)} %get-tuple-element.14) | copy-start | bytes 270340
  3.1 39.4 %all-to-all-start = ((bf16[8,176,256]{2,1,0:T(8,128)(2,1)}), bf16[8,176,256]{2,1,0:T(8,128)(2,1)S(1)}, u32[]{:S(2)}, u32[]{:S(2)}) async-start(bf16[8,176,256]{2,1,0:T(8,128)(2,1)} %get-tuple-element.15), calls=%async_computation | async-start | bytes 1441792 | tf_op jit(solution)/shard_map/all_to_all | solution.py:205
  13.6 14.5 %collective-permute-start.2 = (bf16[176,256]{1,0:T(8,128)(2,1)S(1)}, bf16[176,256]{1,0:T(8,128)(2,1)S(1)}, u32[]{:S(2)}, u32[]{:S(2)}) collective-permute-start(bf16[176,256]{1,0:T(8,128)(2,1)S(1)} %copy-done), channel_id=1, source_target_pairs={{0,24},{1,25},{2,26},{3,27},{4,28},{5,29},{6,30},{7,31},{8,0},{9,1... | collective-permute-start | bytes 270344 | tf_op jit(solution)/shard_map/ppermute | solution.py:176
  19.7 12.9 %collective-permute-start.1 = (bf16[176,256]{1,0:T(8,128)(2,1)S(1)}, bf16[176,256]{1,0:T(8,128)(2,1)S(1)}, u32[]{:S(2)}, u32[]{:S(2)}) collective-permute-start(bf16[176,256]{1,0:T(8,128)(2,1)S(1)} %copy-done), channel_id=1, source_target_pairs={{0,16},{1,17},{2,18},{3,19},{4,20},{5,21},{6,22},{7,23},{8,24},{9,... | collective-permute-start | bytes 270344 | tf_op jit(solution)/shard_map/ppermute | solution.py:176
  23.6 9.1 %collective-permute-start = (bf16[176,256]{1,0:T(8,128)(2,1)S(1)}, bf16[176,256]{1,0:T(8,128)(2,1)S(1)}, u32[]{:S(2)}, u32[]{:S(2)}) collective-permute-start(bf16[176,256]{1,0:T(8,128)(2,1)S(1)} %copy-done), channel_id=1, source_target_pairs={{0,8},{1,9},{2,10},{3,11},{4,12},{5,13},{6,14},{7,15},{8,16},{9,17... | collective-permute-start | bytes 270344 | tf_op jit(solution)/shard_map/ppermute | solution.py:176
  32.8 18.9 %collective-permute-start.5 = (bf16[4,176,256]{2,1,0:T(8,128)(2,1)S(1)}, bf16[4,176,256]{2,1,0:T(8,128)(2,1)S(1)}, u32[]{:S(2)}, u32[]{:S(2)}) collective-permute-start(bf16[4,176,256]{2,1,0:T(8,128)(2,1)S(1)} %pad_maximum_fusion.refs_0_), channel_id=1, source_target_pairs={{0,6},{1,7},{2,0},{3,1},{4,2},{5,3},{6,4},{7,5},{8,14},{9,15},{10,... | collective-permute-start | bytes 1081352 | tf_op jit(solution)/shard_map/ppermute | solution.py:176
  35.5 18.1 %collective-permute-start.4 = (bf16[4,176,256]{2,1,0:T(8,128)(2,1)S(1)}, bf16[4,176,256]{2,1,0:T(8,128)(2,1)S(1)}, u32[]{:S(2)}, u32[]{:S(2)}) collective-permute-start(bf16[4,176,256]{2,1,0:T(8,128)(2,1)S(1)} %pad_maximum_fusion.refs_0_), channel_id=1, source_target_pairs={{0,4},{1,5},{2,6},{3,7},{4,0},{5,1},{6,2},{7,3},{8,12},{9,13},{10,... | collective-permute-start | bytes 1081352 | tf_op jit(solution)/shard_map/ppermute | solution.py:176
  38.5 17.5 %collective-permute-start.3 = (bf16[4,176,256]{2,1,0:T(8,128)(2,1)S(1)}, bf16[4,176,256]{2,1,0:T(8,128)(2,1)S(1)}, u32[]{:S(2)}, u32[]{:S(2)}) collective-permute-start(bf16[4,176,256]{2,1,0:T(8,128)(2,1)S(1)} %pad_maximum_fusion.refs_0_), channel_id=1, source_target_pairs={{0,2},{1,3},{2,4},{3,5},{4,6},{5,7},{6,0},{7,1},{8,10},{9,11},{10,... | collective-permute-start | bytes 1081352 | tf_op jit(solution)/shard_map/ppermute | solution.py:176
  42.5 19.5 %collective-permute-start.10 = (bf16[8,176,256]{2,1,0:T(8,128)(2,1)S(1)}, bf16[8,176,256]{2,1,0:T(8,128)(2,1)S(1)}, u32[]{:S(2)}, u32[]{:S(2)}) collective-permute-start(bf16[8,176,256]{2,1,0:T(8,128)(2,1)S(1)} %all-to-all-done.refs_8_), channel_id=1, source_target_pairs={{0,256},{32,288},{64,320},{96,352},{128,384},{160,416},{192,448},{... | collective-permute-start | bytes 2162696 | tf_op jit(solution)/shard_map/ppermute | solution.py:176
  47.2 12.1 %collective-permute-start.6 = (bf16[4,176,256]{2,1,0:T(8,128)(2,1)S(1)}, bf16[4,176,256]{2,1,0:T(8,128)(2,1)S(1)}, u32[]{:S(2)}, u32[]{:S(2)}) collective-permute-start(bf16[4,176,256]{2,1,0:T(8,128)(2,1)S(1)} %pad_maximum_fusion.refs_0_), channel_id=1, source_target_pairs={{0,1},{1,0},{2,3},{3,2},{4,5},{5,4},{6,7},{7,6},{8,9},{9,8},{10,11... | collective-permute-start | bytes 1081352 | tf_op jit(solution)/shard_map/ppermute | solution.py:176
  51.7 7.7 %collective-permute-start.9 = (bf16[4,176,256]{2,1,0:T(8,128)(2,1)S(1)}, bf16[4,176,256]{2,1,0:T(8,128)(2,1)}, u32[]{:S(2)}, u32[]{:S(2)}) collective-permute-start(bf16[4,176,256]{2,1,0:T(8,128)(2,1)S(1)} %collective-permute-done.5.refs_3_), channel_id=1, source_target_pairs={{0,1},{1,0},{2,3},{3,2},{4,5},{5,4},{6,7},{7,6},{8,9},{9,8},{10,11... | collective-permute-start | bytes 1081352 | tf_op jit(solution)/shard_map/ppermute | solution.py:176
  53.6 5.8 %collective-permute-start.8 = (bf16[4,176,256]{2,1,0:T(8,128)(2,1)S(1)}, bf16[4,176,256]{2,1,0:T(8,128)(2,1)}, u32[]{:S(2)}, u32[]{:S(2)}) collective-permute-start(bf16[4,176,256]{2,1,0:T(8,128)(2,1)S(1)} %collective-permute-done.4.refs_2_), channel_id=1, source_target_pairs={{0,1},{1,0},{2,3},{3,2},{4,5},{5,4},{6,7},{7,6},{8,9},{9,8},{10,11... | collective-permute-start | bytes 1081352 | tf_op jit(solution)/shard_map/ppermute | solution.py:176
  56.0 3.7 %collective-permute-start.7 = (bf16[4,176,256]{2,1,0:T(8,128)(2,1)S(1)}, bf16[4,176,256]{2,1,0:T(8,128)(2,1)}, u32[]{:S(2)}, u32[]{:S(2)}) collective-permute-start(bf16[4,176,256]{2,1,0:T(8,128)(2,1)S(1)} %collective-permute-done.3.refs_1_), channel_id=1, source_target_pairs={{0,1},{1,0},{2,3},{3,2},{4,5},{5,4},{6,7},{7,6},{8,9},{9,8},{10,11... | collective-permute-start | bytes 1081352 | tf_op jit(solution)/shard_map/ppermute | solution.py:176
  58.6 0.7 copy-start.1
  95.3 6.9 %collective-permute-start.12 = (bf16[8,32,256]{2,1,0:T(8,128)(2,1)S(1)}, bf16[8,32,256]{2,1,0:T(8,128)(2,1)S(1)}, u32[]{:S(2)}, u32[]{:S(2)}) collective-permute-start(bf16[8,32,256]{2,1,0:T(8,128)(2,1)S(1)} %get-tuple-element.19), channel_id=1, source_target_pairs={{0,256},{32,288},{64,320},{96,352},{128,384},{160,416},{192,448},{... | collective-permute-start | bytes 393224 | tf_op jit(solution)/shard_map/ppermute | solution.py:176
  97.2 5.0 %collective-permute-start.11 = (bf16[16,32,256]{2,1,0:T(8,128)(2,1)S(1)}, bf16[16,32,256]{2,1,0:T(8,128)(2,1)S(1)}, u32[]{:S(2)}, u32[]{:S(2)}) collective-permute-start(bf16[16,32,256]{2,1,0:T(8,128)(2,1)S(1)} %get-tuple-element.17), channel_id=1, source_target_pairs={{0,1},{1,0},{2,3},{3,2},{4,5},{5,4},{6,7},{7,6},{8,9},{9,8},{10,11... | collective-permute-start | bytes 786440 | tf_op jit(solution)/shard_map/ppermute | solution.py:176
  103.0 10.1 %collective-permute-start.13 = (bf16[4,32,256]{2,1,0:T(8,128)(2,1)S(1)}, bf16[4,32,256]{2,1,0:T(8,128)(2,1)S(1)}, u32[]{:S(2)}, u32[]{:S(2)}) collective-permute-start(bf16[4,32,256]{2,1,0:T(8,128)(2,1)S(1)} %slice.61), channel_id=1, source_target_pairs={{0,128},{32,160},{64,192},{96,224},{128,0},{160,32},{192,64},{224,... | collective-permute-start | bytes 196616 | tf_op jit(solution)/shard_map/ppermute | solution.py:176
  104.9 17.4 %all-to-all-start.1 = ((bf16[16,32,256]{2,1,0:T(8,128)(2,1)}), bf16[16,32,256]{2,1,0:T(8,128)(2,1)S(1)}, u32[]{:S(2)}, u32[]{:S(2)}) async-start(bf16[16,32,256]{2,1,0:T(8,128)(2,1)} %add_convert_fusion), calls=%async_computation.1 | async-start | bytes 524288 | tf_op jit(solution)/shard_map/all_to_all | solution.py:205
  113.1 7.1 %collective-permute-start.14 = (f32[2,32,256]{2,1,0:T(8,128)S(1)}, f32[2,32,256]{2,1,0:T(8,128)S(1)}, u32[]{:S(2)}, u32[]{:S(2)}) collective-permute-start(f32[2,32,256]{2,1,0:T(8,128)S(1)} %slice.38), channel_id=1, source_target_pairs={{0,64},{32,96},{64,0},{96,32},{128,192},{160,224},{192,128},{224,1... | collective-permute-start | bytes 196616 | tf_op jit(solution)/shard_map/ppermute | solution.py:176
  120.1 5.8 %collective-permute-start.15 = (f32[1,32,256]{2,1,0:T(8,128)S(1)}, f32[1,32,256]{2,1,0:T(8,128)S(1)}, u32[]{:S(2)}, u32[]{:S(2)}) collective-permute-start(f32[1,32,256]{2,1,0:T(8,128)S(1)} %slice.40), channel_id=1, source_target_pairs={{0,32},{32,0},{64,96},{96,64},{128,160},{160,128},{192,224},{224,1... | collective-permute-start | bytes 98312 | tf_op jit(solution)/shard_map/ppermute | solution.py:176

commit v4 on v3

--- a/solution.py
+++ b/solution.py
@@ -15,6 +15,8 @@
 PACK = DEPTH + VECS
 FULL = 256
 LANES = 128
+AUG_GROUP = LANES // AUG
+VEC_GROUP = LANES // VECS
 UNROLL = 8
 
 COL_SIZES = (4, 4, 2)
@@ -28,7 +30,7 @@
 def pack_kernel(feat_ref, scale_ref, vec_ref, row_ref, col_ref):
     turned = feat_ref[...].astype(jnp.float32).T
     norm = jnp.sum(turned * turned, axis=0, keepdims=True)
-    offset = (DESC // 2) * jnp.log(scale_ref[...].astype(jnp.float32)) - 0.5 * norm
+    offset = (DESC // 2) * jnp.log(scale_ref[...].astype(jnp.float32).reshape(1, TILE)) - 0.5 * norm
     high = offset.astype(jnp.bfloat16).astype(jnp.float32)
     rest = offset - high
     middle = rest.astype(jnp.bfloat16).astype(jnp.float32)
@@ -44,7 +46,8 @@
     descriptors = turned.astype(jnp.bfloat16)
     narrow = vec_ref[...].astype(jnp.bfloat16)
     row_offsets, col_offsets = offset_rows(0, 3), offset_rows(3, 0)
-    row_ref[0:DESC, :] = descriptors
+    row_ref[0:DESC, 0:DESC] = feat_ref[0:DESC, :]
+    row_ref[0:DESC, DESC:TILE] = feat_ref[DESC:TILE, :]
     row_ref[DESC:DEPTH, :] = row_offsets
     row_ref[DEPTH:PACK, :] = narrow
     for copy in range(col_ref.shape[0]):
@@ -59,57 +62,72 @@
         jax.ShapeDtypeStruct((ROW_SIZES[1], PACK, TILE), jnp.bfloat16),
     )
     return pl.pallas_call(pack_kernel, out_shape=shapes, name="pack_blocks")(
-        features, scales.reshape(1, TILE), vectors
+        features, scales, vectors
     )
 
 
 def tiles_kernel(slots_ref, count_ref, *refs):
     rows_from, cols_from = refs[:ROW_PARTS], refs[ROW_PARTS : ROW_PARTS + COL_PARTS]
     forward_ref, forward_other_ref, mirror_ref, mirror_other_ref = refs[ROW_PARTS + COL_PARTS :][:4]
-    rows_ref, cols_ref, turned_ref, vecs_ref, fsum_ref, msum_ref, row_sems, col_sems = refs[ROW_PARTS + COL_PARTS + 4 :]
+    rows_ref, cols_ref, cvecs_ref, left_ref, vecs_ref, fsum_ref, msum_ref, row_sems, col_sems, vec_sems = refs[ROW_PARTS + COL_PARTS + 4 :]
     row_span = rows_ref.shape[0]
     col_span = cols_ref.shape[0]
 
-    cols_ref[:, PACK:FULL, :] = jnp.zeros((col_span, FULL - PACK, TILE), jnp.bfloat16)
-
-    def copies(sources, target, sems):
+    def copies(sources, target, sems, first, last):
         size = target.shape[0] // len(sources)
         return [
-            pltpu.make_async_copy(source, target.at[pl.ds(at * size, size), pl.ds(0, PACK)], sems.at[at])
+            pltpu.make_async_copy(
+                source.at[:, pl.ds(first, last - first)], target.at[pl.ds(at * size, size), pl.ds(0, last - first)], sems.at[at]
+            )
             for at, source in enumerate(sources)
         ]
 
-    row_copies = copies(rows_from, rows_ref, row_sems)
-    col_copies = copies(cols_from, cols_ref, col_sems)
-    for copy in row_copies + col_copies:
+    row_copies = copies(rows_from, rows_ref, row_sems, 0, PACK)
+    col_copies = copies(cols_from, cols_ref, col_sems, 0, DEPTH)
+    vec_copies = copies(cols_from, cvecs_ref, vec_sems, DEPTH, PACK)
+    for copy in row_copies + col_copies + vec_copies:
         copy.start()
 
     fsum_ref[...] = jnp.zeros_like(fsum_ref)
     msum_ref[...] = jnp.zeros_like(msum_ref)
-
-    part = row_span // ROW_PARTS
-    for at, copy in enumerate(row_copies):
+    lane = lax.broadcasted_iota(jnp.int32, (TILE, LANES), 1)
+
+    def lanes_of(group, width):
+        return jnp.where(lax.div(lane, width) == group, 1.0, 0.0).astype(jnp.bfloat16)
+
+    for copy in row_copies:
         copy.wait()
 
-        @pl.loop(at * part, (at + 1) * part)
-        def _(block):
-            turned_ref[block, :, 0:DESC] = rows_ref[block, 0:DESC, :].T
-            offsets = rows_ref[block, DESC:DEPTH, :]
-            padded = jnp.concatenate([offsets, jnp.zeros((FULL - DEPTH, TILE), jnp.bfloat16)], axis=0)
-            turned_ref[block, :, DESC:FULL] = padded.T
-
-    for copy in col_copies:
+    @pl.loop(0, row_span)
+    def _(block):
+        left_ref[block, 0:DESC, 0:DESC] = rows_ref[block, 0:DESC, 0:DESC]
+        left_ref[block, DESC:TILE, 0:DESC] = rows_ref[block, 0:DESC, DESC:TILE]
+
+    @pl.loop(0, row_span // AUG_GROUP)
+    def _(group):
+        offsets = rows_ref[pl.ds(group * AUG_GROUP, AUG_GROUP), DESC:DEPTH, :].reshape(LANES, TILE).T
+        for at in range(AUG_GROUP):
+            left_ref[group * AUG_GROUP + at, :, DESC:FULL] = offsets * lanes_of(at, AUG)
+
+    for copy in col_copies + vec_copies:
         copy.wait()
 
     @pl.loop(0, col_span)
     def _(block):
-        narrow = cols_ref[block, DEPTH:PACK, :]
-        vecs_ref[block] = jnp.concatenate([narrow, jnp.zeros((LANES - VECS, TILE), jnp.bfloat16)], axis=0).T
+        offsets = cols_ref[block, DESC:DEPTH, :]
+        for at in range(1, AUG_GROUP):
+            cols_ref[block, DESC + at * AUG : DESC + (at + 1) * AUG, :] = offsets
+
+    @pl.loop(0, col_span // VEC_GROUP)
+    def _(group):
+        narrow = cvecs_ref[pl.ds(group * VEC_GROUP, VEC_GROUP)].reshape(LANES, TILE).T
+        for at in range(VEC_GROUP):
+            vecs_ref[group * VEC_GROUP + at] = narrow * lanes_of(at, VECS)
 
     def tile(slot):
         row_at = slots_ref[0, slot]
         col_at = slots_ref[1, slot]
-        score = jnp.dot(turned_ref[row_at], cols_ref[col_at], preferred_element_type=jnp.float32)
+        score = jnp.dot(left_ref[row_at], cols_ref[col_at], preferred_element_type=jnp.float32)
         block = jnp.exp2(score * POWER).astype(jnp.bfloat16)
         forward = jnp.dot(block, vecs_ref[col_at], preferred_element_type=jnp.float32)
         mirror = jnp.dot(rows_ref[row_at, DEPTH:PACK, :], block, preferred_element_type=jnp.float32)
@@ -124,10 +142,14 @@
 
     half = row_span // 2
 
+    def total(block):
+        turned = fsum_ref[block].T
+        return sum(turned[at * VECS : (at + 1) * VECS] for at in range(VEC_GROUP))
+
     @pl.loop(0, half)
     def _(block):
-        forward_ref[block] = fsum_ref[block].T[0:VECS]
-        forward_other_ref[block] = fsum_ref[half + block].T[0:VECS].astype(jnp.bfloat16)
+        forward_ref[block] = total(block)
+        forward_other_ref[block] = total(half + block).astype(jnp.bfloat16)
 
     mirror_ref[...] = msum_ref[0 : col_span // 2]
     mirror_other_ref[...] = msum_ref[col_span // 2 : col_span].astype(jnp.bfloat16)
@@ -152,11 +174,13 @@
         scratch_shapes=[
             pltpu.VMEM((row_span, PACK, TILE), jnp.bfloat16),
             pltpu.VMEM((col_span, FULL, TILE), jnp.bfloat16),
+            pltpu.VMEM((col_span, VECS, TILE), jnp.bfloat16),
             pltpu.VMEM((row_span, TILE, FULL), jnp.bfloat16),
             pltpu.VMEM((col_span, TILE, LANES), jnp.bfloat16),
             pltpu.VMEM((row_span + 1, TILE, LANES), jnp.float32),
             pltpu.VMEM((col_span + 1, VECS, TILE), jnp.float32),
             pltpu.SemaphoreType.DMA((ROW_PARTS,)),
+            pltpu.SemaphoreType.DMA((COL_PARTS,)),
             pltpu.SemaphoreType.DMA((COL_PARTS,)),
         ],
         compiler_params=pltpu.CompilerParams(vmem_limit_bytes=48 * 1024 * 1024),
@@ -211,7 +235,8 @@
 
 
 def add_mirrors(mirror, for_neighbour, after):
-    mirror = mirror + swapped(for_neighbour, "row", ROW_SIZES, 0, 1).astype(jnp.float32)
+    received, _ = lax.optimization_barrier((swapped(for_neighbour, "row", ROW_SIZES, 0, 1), after))
+    mirror = mirror + received.astype(jnp.float32)
     bit = ROW_SIZES[1] // 2
     while bit:
         sent = mirror[bit:].astype(jnp.bfloat16) if bit > 2 else mirror[bit:]

time: 127 us -> 128 us (level)
  the two profiles are of different devices: /device:TPU:6 before, /device:TPU:2 now
where the time goes in v4:
time: 128 us; the launch traced here: 127 us
  starting transfers between devices  65 us (51%)
  Pallas kernels  33.7 us (26%)
  waiting for transfers between devices  25.4 us (20%)
  other arithmetic  1.56 us (1%)
    ppermute x16, starting transfers between devices, moved(): return lax.ppermute(value, axis, pairs)  47.9 us
    pallas_call x1, Pallas kernels, tile_products(): pl.pallas_call(tiles_kernel, out_shape=(jax.ShapeDtypeStruct((row_span //...  31.9 us
    ppermute x16, waiting for transfers between devices, moved(): return lax.ppermute(value, axis, pairs)  25.4 us
    all_to_all x2, starting transfers between devices, grouped_all_to_all(): lax.all_to_all(value, axis, 0, 0, axis_index_groups=list(groups.values())...  17.1 us
  transfers between devices with their start and end apart: 18, of which 6 were waited for; matrix products, arithmetic and copies ran while one was open for 1% of the time, Pallas kernels for 0%

profile of v4, /device:TPU:2, one launch (start us, length us, event | category | flops | bytes accessed | tf_op | source)
XLA Modules:
  0.0 127.3 jit_solution(10235414673218328947)
XLA Ops:
  0.0 1.9 %pack_blocks.1 = (bf16[176,256]{1,0:T(8,128)(2,1)}, bf16[8,176,256]{2,1,0:T(8,128)(2,1)}) custom-call(bf16[256,128]{1,0:T(8,128)(2,1)} %feat_ref.1, bf16[256]{0:T(256)(128)(2,1)} %scale_ref.1, f32[32,256]{1,0:T(8,128)} %vec_ref.1), custom_call_target="tpu_custom_call" | custom-call | tf_op jit(solution)/shard_map/pack_blocks/pallas_call | solution.py:64
  1.9 0.0 copy-start
  1.9 10.4 %all-to-all-start = ((bf16[8,176,256]{2,1,0:T(8,128)(2,1)}), bf16[8,176,256]{2,1,0:T(8,128)(2,1)S(1)}, u32[]{:S(2)}, u32[]{:S(2)}) async-start(bf16[8,176,256]{2,1,0:T(8,128)(2,1)} %get-tuple-element.16), calls=%async_computation | async-start | bytes 1441792 | tf_op jit(solution)/shard_map/all_to_all | solution.py:229
  12.3 0.0 copy-done
  12.3 6.2 %collective-permute-start.2 = (bf16[176,256]{1,0:T(8,128)(2,1)S(1)}, bf16[176,256]{1,0:T(8,128)(2,1)S(1)}, u32[]{:S(2)}, u32[]{:S(2)}) collective-permute-start(bf16[176,256]{1,0:T(8,128)(2,1)S(1)} %copy-done), channel_id=1, source_target_pairs={{0,24},{1,25},{2,26},{3,27},{4,28},{5,29},{6,30},{7,31},{8,0},{9,1... | collective-permute-start | bytes 270344 | tf_op jit(solution)/shard_map/ppermute | solution.py:200
  18.5 3.8 %collective-permute-start.1 = (bf16[176,256]{1,0:T(8,128)(2,1)S(1)}, bf16[176,256]{1,0:T(8,128)(2,1)S(1)}, u32[]{:S(2)}, u32[]{:S(2)}) collective-permute-start(bf16[176,256]{1,0:T(8,128)(2,1)S(1)} %copy-done), channel_id=1, source_target_pairs={{0,16},{1,17},{2,18},{3,19},{4,20},{5,21},{6,22},{7,23},{8,24},{9,... | collective-permute-start | bytes 270344 | tf_op jit(solution)/shard_map/ppermute | solution.py:200
  22.3 4.5 %collective-permute-start = (bf16[176,256]{1,0:T(8,128)(2,1)S(1)}, bf16[176,256]{1,0:T(8,128)(2,1)S(1)}, u32[]{:S(2)}, u32[]{:S(2)}) collective-permute-start(bf16[176,256]{1,0:T(8,128)(2,1)S(1)} %copy-done), channel_id=1, source_target_pairs={{0,8},{1,9},{2,10},{3,11},{4,12},{5,13},{6,14},{7,15},{8,16},{9,17... | collective-permute-start | bytes 270344 | tf_op jit(solution)/shard_map/ppermute | solution.py:200
  26.8 0.0 collective-permute-done.2
  26.8 4.6 %collective-permute-done.1 = bf16[176,256]{1,0:T(8,128)(2,1)S(1)} collective-permute-done((bf16[176,256]{1,0:T(8,128)(2,1)S(1)}, bf16[176,256]{1,0:T(8,128)(2,1)S(1)}, u32[]{:S(2)}, u32[]{:S(2)}) %collective-permute-start.1) | collective-permute-done | bytes 90144 | tf_op jit(solution)/shard_map/ppermute | solution.py:200
  31.5 0.0 collective-permute-done
  31.5 2.4 %collective-permute-start.5 = (bf16[4,176,256]{2,1,0:T(8,128)(2,1)S(1)}, bf16[4,176,256]{2,1,0:T(8,128)(2,1)S(1)}, u32[]{:S(2)}, u32[]{:S(2)}) collective-permute-start(bf16[4,176,256]{2,1,0:T(8,128)(2,1)S(1)} %pad_maximum_fusion.refs_0_), channel_id=1, source_target_pairs={{0,6},{1,7},{2,0},{3,1},{4,2},{5,3},{6,4},{7,5},{8,14},{9,15},{10,... | collective-permute-start | bytes 1081352 | tf_op jit(solution)/shard_map/ppermute | solution.py:200
  34.0 4.3 %collective-permute-start.4 = (bf16[4,176,256]{2,1,0:T(8,128)(2,1)S(1)}, bf16[4,176,256]{2,1,0:T(8,128)(2,1)S(1)}, u32[]{:S(2)}, u32[]{:S(2)}) collective-permute-start(bf16[4,176,256]{2,1,0:T(8,128)(2,1)S(1)} %pad_maximum_fusion.refs_0_), channel_id=1, source_target_pairs={{0,4},{1,5},{2,6},{3,7},{4,0},{5,1},{6,2},{7,3},{8,12},{9,13},{10,... | collective-permute-start | bytes 1081352 | tf_op jit(solution)/shard_map/ppermute | solution.py:200
  38.3 3.7 %collective-permute-start.3 = (bf16[4,176,256]{2,1,0:T(8,128)(2,1)S(1)}, bf16[4,176,256]{2,1,0:T(8,128)(2,1)S(1)}, u32[]{:S(2)}, u32[]{:S(2)}) collective-permute-start(bf16[4,176,256]{2,1,0:T(8,128)(2,1)S(1)} %pad_maximum_fusion.refs_0_), channel_id=1, source_target_pairs={{0,2},{1,3},{2,4},{3,5},{4,6},{5,7},{6,0},{7,1},{8,10},{9,11},{10,... | collective-permute-start | bytes 1081352 | tf_op jit(solution)/shard_map/ppermute | solution.py:200
  42.0 0.0 all-to-all-done.refs_8_
  42.0 4.7 %collective-permute-start.10 = (bf16[8,176,256]{2,1,0:T(8,128)(2,1)S(1)}, bf16[8,176,256]{2,1,0:T(8,128)(2,1)S(1)}, u32[]{:S(2)}, u32[]{:S(2)}) collective-permute-start(bf16[8,176,256]{2,1,0:T(8,128)(2,1)S(1)} %all-to-all-done.refs_8_), channel_id=1, source_target_pairs={{0,256},{32,288},{64,320},{96,352},{128,384},{160,416},{192,448},{... | collective-permute-start | bytes 2162696 | tf_op jit(solution)/shard_map/ppermute | solution.py:200
  46.7 1.9 %collective-permute-start.6 = (bf16[4,176,256]{2,1,0:T(8,128)(2,1)S(1)}, bf16[4,176,256]{2,1,0:T(8,128)(2,1)S(1)}, u32[]{:S(2)}, u32[]{:S(2)}) collective-permute-start(bf16[4,176,256]{2,1,0:T(8,128)(2,1)S(1)} %pad_maximum_fusion.refs_0_), channel_id=1, source_target_pairs={{0,1},{1,0},{2,3},{3,2},{4,5},{5,4},{6,7},{7,6},{8,9},{9,8},{10,11... | collective-permute-start | bytes 1081352 | tf_op jit(solution)/shard_map/ppermute | solution.py:200
  48.6 0.0 collective-permute-done.5.refs_3_
  48.6 2.4 %collective-permute-start.9 = (bf16[4,176,256]{2,1,0:T(8,128)(2,1)S(1)}, bf16[4,176,256]{2,1,0:T(8,128)(2,1)}, u32[]{:S(2)}, u32[]{:S(2)}) collective-permute-start(bf16[4,176,256]{2,1,0:T(8,128)(2,1)S(1)} %collective-permute-done.5.refs_3_), channel_id=1, source_target_pairs={{0,1},{1,0},{2,3},{3,2},{4,5},{5,4},{6,7},{7,6},{8,9},{9,8},{10,11... | collective-permute-start | bytes 1081352 | tf_op jit(solution)/shard_map/ppermute | solution.py:200
  51.1 0.0 collective-permute-done.4.refs_2_
  51.1 1.9 %collective-permute-start.8 = (bf16[4,176,256]{2,1,0:T(8,128)(2,1)S(1)}, bf16[4,176,256]{2,1,0:T(8,128)(2,1)}, u32[]{:S(2)}, u32[]{:S(2)}) collective-permute-start(bf16[4,176,256]{2,1,0:T(8,128)(2,1)S(1)} %collective-permute-done.4.refs_2_), channel_id=1, source_target_pairs={{0,1},{1,0},{2,3},{3,2},{4,5},{5,4},{6,7},{7,6},{8,9},{9,8},{10,11... | collective-permute-start | bytes 1081352 | tf_op jit(solution)/shard_map/ppermute | solution.py:200
  53.0 0.0 collective-permute-done.3.refs_1_
  53.0 2.4 %collective-permute-start.7 = (bf16[4,176,256]{2,1,0:T(8,128)(2,1)S(1)}, bf16[4,176,256]{2,1,0:T(8,128)(2,1)}, u32[]{:S(2)}, u32[]{:S(2)}) collective-permute-start(bf16[4,176,256]{2,1,0:T(8,128)(2,1)S(1)} %collective-permute-done.3.refs_1_), channel_id=1, source_target_pairs={{0,1},{1,0},{2,3},{3,2},{4,5},{5,4},{6,7},{7,6},{8,9},{9,8},{10,11... | collective-permute-start | bytes 1081352 | tf_op jit(solution)/shard_map/ppermute | solution.py:200
  56.1 0.0 copy-start.1
  56.1 0.7 copy-done.1
  56.8 0.0 collective-permute-done.6.refs_4_
  56.8 0.0 collective-permute-done.9.refs_7_
  56.8 0.0 collective-permute-done.8.refs_6_
  56.8 0.0 collective-permute-done.7.refs_5_
  56.8 4.7 %collective-permute-done.10.refs_9_ = bf16[8,176,256]{2,1,0:T(8,128)(2,1)S(1)} collective-permute-done((bf16[8,176,256]{2,1,0:T(8,128)(2,1)S(1)}, bf16[8,176,256]{2,1,0:T(8,128)(2,1)S(1)}, u32[]{:S(2)}, u32[]{:S(2)}) %collective-permute-start.10) | collective-permute-done | bytes 720928 | tf_op jit(solution)/shard_map/ppermute | solution.py:200
  61.5 31.9 %tile_products.1 = (f32[16,32,256]{2,1,0:T(8,128)S(1)}, bf16[16,32,256]{2,1,0:T(8,128)(2,1)S(1)}, f32[8,32,256]{2,1,0:T(8,128)S(1)}, bf16[8,32,256]{2,1,0:T(8,128)(2,1)S(1)}) custom-call(s32[4,128]{1,0:T(4,128)S(1)} %pad_add_fusion.slots_ref, s32[1,1]{1,0:T(1,128)} %copy.6.count_ref, bf16[4,176,256]{2,1,0:T(8,128)(2,1)S(1)} %pad_maximum_fusion.refs_0_, ...), custom_call_target="tpu_custom_call" | custom-call | tf_op jit(solution)/shard_map/tile_products/pallas_call | solution.py:164
  93.4 1.9 %collective-permute-start.11 = (bf16[16,32,256]{2,1,0:T(8,128)(2,1)S(1)}, bf16[16,32,256]{2,1,0:T(8,128)(2,1)S(1)}, u32[]{:S(2)}, u32[]{:S(2)}) collective-permute-start(bf16[16,32,256]{2,1,0:T(8,128)(2,1)S(1)} %get-tuple-element.18), channel_id=1, source_target_pairs={{0,1},{1,0},{2,3},{3,2},{4,5},{5,4},{6,7},{7,6},{8,9},{9,8},{10,11... | collective-permute-start | bytes 786440 | tf_op jit(solution)/shard_map/ppermute | solution.py:200
  95.3 1.9 %collective-permute-start.12 = (bf16[8,32,256]{2,1,0:T(8,128)(2,1)S(1)}, bf16[8,32,256]{2,1,0:T(8,128)(2,1)S(1)}, u32[]{:S(2)}, u32[]{:S(2)}) collective-permute-start(bf16[8,32,256]{2,1,0:T(8,128)(2,1)S(1)} %get-tuple-element.20), channel_id=1, source_target_pairs={{0,256},{32,288},{64,320},{96,352},{128,384},{160,416},{192,448},{... | collective-permute-start | bytes 393224 | tf_op jit(solution)/shard_map/ppermute | solution.py:200
  97.3 0.0 collective-permute-done.11
  97.3 0.8 add_convert_fusion
  98.1 5.1 %collective-permute-done.12 = bf16[8,32,256]{2,1,0:T(8,128)(2,1)S(1)} collective-permute-done((bf16[8,32,256]{2,1,0:T(8,128)(2,1)S(1)}, bf16[8,32,256]{2,1,0:T(8,128)(2,1)S(1)}, u32[]{:S(2)}, u32[]{:S(2)}) %collective-permute-start.12) | collective-permute-done | bytes 131104 | tf_op jit(solution)/shard_map/ppermute | solution.py:200
  103.2 1.9 %collective-permute-start.13 = (bf16[4,32,256]{2,1,0:T(8,128)(2,1)S(1)}, bf16[4,32,256]{2,1,0:T(8,128)(2,1)S(1)}, u32[]{:S(2)}, u32[]{:S(2)}) collective-permute-start(bf16[4,32,256]{2,1,0:T(8,128)(2,1)S(1)} %slice.61), channel_id=1, source_target_pairs={{0,128},{32,160},{64,192},{96,224},{128,0},{160,32},{192,64},{224,... | collective-permute-start | bytes 196616 | tf_op jit(solution)/shard_map/ppermute | solution.py:200
  105.1 6.7 %all-to-all-start.1 = ((bf16[16,32,256]{2,1,0:T(8,128)(2,1)}), bf16[16,32,256]{2,1,0:T(8,128)(2,1)S(1)}, u32[]{:S(2)}, u32[]{:S(2)}) async-start(bf16[16,32,256]{2,1,0:T(8,128)(2,1)} %add_convert_fusion), calls=%async_computation.1 | async-start | bytes 524288 | tf_op jit(solution)/shard_map/all_to_all | solution.py:229
  111.8 1.5 %collective-permute-done.13 = bf16[4,32,256]{2,1,0:T(8,128)(2,1)S(1)} collective-permute-done((bf16[4,32,256]{2,1,0:T(8,128)(2,1)S(1)}, bf16[4,32,256]{2,1,0:T(8,128)(2,1)S(1)}, u32[]{:S(2)}, u32[]{:S(2)}) %collective-permute-start.13) | collective-permute-done | bytes 65568 | tf_op jit(solution)/shard_map/ppermute | solution.py:200
  113.3 1.9 %collective-permute-start.14 = (f32[2,32,256]{2,1,0:T(8,128)S(1)}, f32[2,32,256]{2,1,0:T(8,128)S(1)}, u32[]{:S(2)}, u32[]{:S(2)}) collective-permute-start(f32[2,32,256]{2,1,0:T(8,128)S(1)} %slice.38), channel_id=1, source_target_pairs={{0,64},{32,96},{64,0},{96,32},{128,192},{160,224},{192,128},{224,1... | collective-permute-start | bytes 196616 | tf_op jit(solution)/shard_map/ppermute | solution.py:200
  115.2 5.7 %collective-permute-done.14 = f32[2,32,256]{2,1,0:T(8,128)S(1)} collective-permute-done((f32[2,32,256]{2,1,0:T(8,128)S(1)}, f32[2,32,256]{2,1,0:T(8,128)S(1)}, u32[]{:S(2)}, u32[]{:S(2)}) %collective-permute-start.14) | collective-permute-done | bytes 65568 | tf_op jit(solution)/shard_map/ppermute | solution.py:200
  120.9 1.9 %collective-permute-start.15 = (f32[1,32,256]{2,1,0:T(8,128)S(1)}, f32[1,32,256]{2,1,0:T(8,128)S(1)}, u32[]{:S(2)}, u32[]{:S(2)}) collective-permute-start(f32[1,32,256]{2,1,0:T(8,128)S(1)} %slice.40), channel_id=1, source_target_pairs={{0,32},{32,0},{64,96},{96,64},{128,160},{160,128},{192,224},{224,1... | collective-permute-start | bytes 98312 | tf_op jit(solution)/shard_map/ppermute | solution.py:200
  122.8 0.0 all-to-all-done.1
  122.9 3.8 %collective-permute-done.15 = f32[1,32,256]{2,1,0:T(8,128)S(1)} collective-permute-done((f32[1,32,256]{2,1,0:T(8,128)S(1)}, f32[1,32,256]{2,1,0:T(8,128)S(1)}, u32[]{:S(2)}, u32[]{:S(2)}) %collective-permute-start.15) | collective-permute-done | bytes 32800 | tf_op jit(solution)/shard_map/ppermute | solution.py:200
  126.7 0.6 fusion.1
  (10 shorter events, 0.2 us)
Async XLA Ops:
  1.9 10.5 %copy-start = (bf16[176,256]{1,0:T(8,128)(2,1)S(1)}, bf16[176,256]{1,0:T(8,128)(2,1)}, u32[]{:S(2)}) copy-start(bf16[176,256]{1,0:T(8,128)(2,1)} %get-tuple-element.15) | copy-start | bytes 270340
  1.9 40.1 %all-to-all-start = ((bf16[8,176,256]{2,1,0:T(8,128)(2,1)}), bf16[8,176,256]{2,1,0:T(8,128)(2,1)S(1)}, u32[]{:S(2)}, u32[]{:S(2)}) async-start(bf16[8,176,256]{2,1,0:T(8,128)(2,1)} %get-tuple-element.16), calls=%async_computation | async-start | bytes 1441792 | tf_op jit(solution)/shard_map/all_to_all | solution.py:229
  12.3 14.5 %collective-permute-start.2 = (bf16[176,256]{1,0:T(8,128)(2,1)S(1)}, bf16[176,256]{1,0:T(8,128)(2,1)S(1)}, u32[]{:S(2)}, u32[]{:S(2)}) collective-permute-start(bf16[176,256]{1,0:T(8,128)(2,1)S(1)} %copy-done), channel_id=1, source_target_pairs={{0,24},{1,25},{2,26},{3,27},{4,28},{5,29},{6,30},{7,31},{8,0},{9,1... | collective-permute-start | bytes 270344 | tf_op jit(solution)/shard_map/ppermute | solution.py:200
  18.5 12.9 %collective-permute-start.1 = (bf16[176,256]{1,0:T(8,128)(2,1)S(1)}, bf16[176,256]{1,0:T(8,128)(2,1)S(1)}, u32[]{:S(2)}, u32[]{:S(2)}) collective-permute-start(bf16[176,256]{1,0:T(8,128)(2,1)S(1)} %copy-done), channel_id=1, source_target_pairs={{0,16},{1,17},{2,18},{3,19},{4,20},{5,21},{6,22},{7,23},{8,24},{9,... | collective-permute-start | bytes 270344 | tf_op jit(solution)/shard_map/ppermute | solution.py:200
  22.3 9.1 %collective-permute-start = (bf16[176,256]{1,0:T(8,128)(2,1)S(1)}, bf16[176,256]{1,0:T(8,128)(2,1)S(1)}, u32[]{:S(2)}, u32[]{:S(2)}) collective-permute-start(bf16[176,256]{1,0:T(8,128)(2,1)S(1)} %copy-done), channel_id=1, source_target_pairs={{0,8},{1,9},{2,10},{3,11},{4,12},{5,13},{6,14},{7,15},{8,16},{9,17... | collective-permute-start | bytes 270344 | tf_op jit(solution)/shard_map/ppermute | solution.py:200
  31.5 17.1 %collective-permute-start.5 = (bf16[4,176,256]{2,1,0:T(8,128)(2,1)S(1)}, bf16[4,176,256]{2,1,0:T(8,128)(2,1)S(1)}, u32[]{:S(2)}, u32[]{:S(2)}) collective-permute-start(bf16[4,176,256]{2,1,0:T(8,128)(2,1)S(1)} %pad_maximum_fusion.refs_0_), channel_id=1, source_target_pairs={{0,6},{1,7},{2,0},{3,1},{4,2},{5,3},{6,4},{7,5},{8,14},{9,15},{10,... | collective-permute-start | bytes 1081352 | tf_op jit(solution)/shard_map/ppermute | solution.py:200
  34.0 17.1 %collective-permute-start.4 = (bf16[4,176,256]{2,1,0:T(8,128)(2,1)S(1)}, bf16[4,176,256]{2,1,0:T(8,128)(2,1)S(1)}, u32[]{:S(2)}, u32[]{:S(2)}) collective-permute-start(bf16[4,176,256]{2,1,0:T(8,128)(2,1)S(1)} %pad_maximum_fusion.refs_0_), channel_id=1, source_target_pairs={{0,4},{1,5},{2,6},{3,7},{4,0},{5,1},{6,2},{7,3},{8,12},{9,13},{10,... | collective-permute-start | bytes 1081352 | tf_op jit(solution)/shard_map/ppermute | solution.py:200
  38.3 14.7 %collective-permute-start.3 = (bf16[4,176,256]{2,1,0:T(8,128)(2,1)S(1)}, bf16[4,176,256]{2,1,0:T(8,128)(2,1)S(1)}, u32[]{:S(2)}, u32[]{:S(2)}) collective-permute-start(bf16[4,176,256]{2,1,0:T(8,128)(2,1)S(1)} %pad_maximum_fusion.refs_0_), channel_id=1, source_target_pairs={{0,2},{1,3},{2,4},{3,5},{4,6},{5,7},{6,0},{7,1},{8,10},{9,11},{10,... | collective-permute-start | bytes 1081352 | tf_op jit(solution)/shard_map/ppermute | solution.py:200
  42.0 19.5 %collective-permute-start.10 = (bf16[8,176,256]{2,1,0:T(8,128)(2,1)S(1)}, bf16[8,176,256]{2,1,0:T(8,128)(2,1)S(1)}, u32[]{:S(2)}, u32[]{:S(2)}) collective-permute-start(bf16[8,176,256]{2,1,0:T(8,128)(2,1)S(1)} %all-to-all-done.refs_8_), channel_id=1, source_target_pairs={{0,256},{32,288},{64,320},{96,352},{128,384},{160,416},{192,448},{... | collective-permute-start | bytes 2162696 | tf_op jit(solution)/shard_map/ppermute | solution.py:200
  46.7 10.1 %collective-permute-start.6 = (bf16[4,176,256]{2,1,0:T(8,128)(2,1)S(1)}, bf16[4,176,256]{2,1,0:T(8,128)(2,1)S(1)}, u32[]{:S(2)}, u32[]{:S(2)}) collective-permute-start(bf16[4,176,256]{2,1,0:T(8,128)(2,1)S(1)} %pad_maximum_fusion.refs_0_), channel_id=1, source_target_pairs={{0,1},{1,0},{2,3},{3,2},{4,5},{5,4},{6,7},{7,6},{8,9},{9,8},{10,11... | collective-permute-start | bytes 1081352 | tf_op jit(solution)/shard_map/ppermute | solution.py:200
  48.6 8.2 %collective-permute-start.9 = (bf16[4,176,256]{2,1,0:T(8,128)(2,1)S(1)}, bf16[4,176,256]{2,1,0:T(8,128)(2,1)}, u32[]{:S(2)}, u32[]{:S(2)}) collective-permute-start(bf16[4,176,256]{2,1,0:T(8,128)(2,1)S(1)} %collective-permute-done.5.refs_3_), channel_id=1, source_target_pairs={{0,1},{1,0},{2,3},{3,2},{4,5},{5,4},{6,7},{7,6},{8,9},{9,8},{10,11... | collective-permute-start | bytes 1081352 | tf_op jit(solution)/shard_map/ppermute | solution.py:200
  51.1 5.8 %collective-permute-start.8 = (bf16[4,176,256]{2,1,0:T(8,128)(2,1)S(1)}, bf16[4,176,256]{2,1,0:T(8,128)(2,1)}, u32[]{:S(2)}, u32[]{:S(2)}) collective-permute-start(bf16[4,176,256]{2,1,0:T(8,128)(2,1)S(1)} %collective-permute-done.4.refs_2_), channel_id=1, source_target_pairs={{0,1},{1,0},{2,3},{3,2},{4,5},{5,4},{6,7},{7,6},{8,9},{9,8},{10,11... | collective-permute-start | bytes 1081352 | tf_op jit(solution)/shard_map/ppermute | solution.py:200
  53.0 3.8 %collective-permute-start.7 = (bf16[4,176,256]{2,1,0:T(8,128)(2,1)S(1)}, bf16[4,176,256]{2,1,0:T(8,128)(2,1)}, u32[]{:S(2)}, u32[]{:S(2)}) collective-permute-start(bf16[4,176,256]{2,1,0:T(8,128)(2,1)S(1)} %collective-permute-done.3.refs_1_), channel_id=1, source_target_pairs={{0,1},{1,0},{2,3},{3,2},{4,5},{5,4},{6,7},{7,6},{8,9},{9,8},{10,11... | collective-permute-start | bytes 1081352 | tf_op jit(solution)/shard_map/ppermute | solution.py:200
  56.1 0.7 copy-start.1
  93.4 3.9 %collective-permute-start.11 = (bf16[16,32,256]{2,1,0:T(8,128)(2,1)S(1)}, bf16[16,32,256]{2,1,0:T(8,128)(2,1)S(1)}, u32[]{:S(2)}, u32[]{:S(2)}) collective-permute-start(bf16[16,32,256]{2,1,0:T(8,128)(2,1)S(1)} %get-tuple-element.18), channel_id=1, source_target_pairs={{0,1},{1,0},{2,3},{3,2},{4,5},{5,4},{6,7},{7,6},{8,9},{9,8},{10,11... | collective-permute-start | bytes 786440 | tf_op jit(solution)/shard_map/ppermute | solution.py:200
  95.3 7.8 %collective-permute-start.12 = (bf16[8,32,256]{2,1,0:T(8,128)(2,1)S(1)}, bf16[8,32,256]{2,1,0:T(8,128)(2,1)S(1)}, u32[]{:S(2)}, u32[]{:S(2)}) collective-permute-start(bf16[8,32,256]{2,1,0:T(8,128)(2,1)S(1)} %get-tuple-element.20), channel_id=1, source_target_pairs={{0,256},{32,288},{64,320},{96,352},{128,384},{160,416},{192,448},{... | collective-permute-start | bytes 393224 | tf_op jit(solution)/shard_map/ppermute | solution.py:200
  103.2 10.1 %collective-permute-start.13 = (bf16[4,32,256]{2,1,0:T(8,128)(2,1)S(1)}, bf16[4,32,256]{2,1,0:T(8,128)(2,1)S(1)}, u32[]{:S(2)}, u32[]{:S(2)}) collective-permute-start(bf16[4,32,256]{2,1,0:T(8,128)(2,1)S(1)} %slice.61), channel_id=1, source_target_pairs={{0,128},{32,160},{64,192},{96,224},{128,0},{160,32},{192,64},{224,... | collective-permute-start | bytes 196616 | tf_op jit(solution)/shard_map/ppermute | solution.py:200
  105.1 17.7 %all-to-all-start.1 = ((bf16[16,32,256]{2,1,0:T(8,128)(2,1)}), bf16[16,32,256]{2,1,0:T(8,128)(2,1)S(1)}, u32[]{:S(2)}, u32[]{:S(2)}) async-start(bf16[16,32,256]{2,1,0:T(8,128)(2,1)} %add_convert_fusion), calls=%async_computation.1 | async-start | bytes 524288 | tf_op jit(solution)/shard_map/all_to_all | solution.py:229
  113.3 7.6 %collective-permute-start.14 = (f32[2,32,256]{2,1,0:T(8,128)S(1)}, f32[2,32,256]{2,1,0:T(8,128)S(1)}, u32[]{:S(2)}, u32[]{:S(2)}) collective-permute-start(f32[2,32,256]{2,1,0:T(8,128)S(1)} %slice.38), channel_id=1, source_target_pairs={{0,64},{32,96},{64,0},{96,32},{128,192},{160,224},{192,128},{224,1... | collective-permute-start | bytes 196616 | tf_op jit(solution)/shard_map/ppermute | solution.py:200
  120.9 5.8 %collective-permute-start.15 = (f32[1,32,256]{2,1,0:T(8,128)S(1)}, f32[1,32,256]{2,1,0:T(8,128)S(1)}, u32[]{:S(2)}, u32[]{:S(2)}) collective-permute-start(f32[1,32,256]{2,1,0:T(8,128)S(1)} %slice.40), channel_id=1, source_target_pairs={{0,32},{32,0},{64,96},{96,64},{128,160},{160,128},{192,224},{224,1... | collective-permute-start | bytes 98312 | tf_op jit(solution)/shard_map/ppermute | solution.py:200

commit v5 on v4

--- a/solution.py
+++ b/solution.py
@@ -17,7 +17,7 @@
 LANES = 128
 AUG_GROUP = LANES // AUG
 VEC_GROUP = LANES // VECS
-UNROLL = 8
+UNROLL = 16
 
 COL_SIZES = (4, 4, 2)
 ROW_SIZES = (2, 8)
@@ -68,25 +68,10 @@
 
 def tiles_kernel(slots_ref, count_ref, *refs):
     rows_from, cols_from = refs[:ROW_PARTS], refs[ROW_PARTS : ROW_PARTS + COL_PARTS]
-    forward_ref, forward_other_ref, mirror_ref, mirror_other_ref = refs[ROW_PARTS + COL_PARTS :][:4]
-    rows_ref, cols_ref, cvecs_ref, left_ref, vecs_ref, fsum_ref, msum_ref, row_sems, col_sems, vec_sems = refs[ROW_PARTS + COL_PARTS + 4 :]
-    row_span = rows_ref.shape[0]
-    col_span = cols_ref.shape[0]
-
-    def copies(sources, target, sems, first, last):
-        size = target.shape[0] // len(sources)
-        return [
-            pltpu.make_async_copy(
-                source.at[:, pl.ds(first, last - first)], target.at[pl.ds(at * size, size), pl.ds(0, last - first)], sems.at[at]
-            )
-            for at, source in enumerate(sources)
-        ]
-
-    row_copies = copies(rows_from, rows_ref, row_sems, 0, PACK)
-    col_copies = copies(cols_from, cols_ref, col_sems, 0, DEPTH)
-    vec_copies = copies(cols_from, cvecs_ref, vec_sems, DEPTH, PACK)
-    for copy in row_copies + col_copies + vec_copies:
-        copy.start()
+    forward_ref, mirror_ref, mirror_other_ref = refs[ROW_PARTS + COL_PARTS :][:3]
+    left_ref, row_vecs_ref, right_ref, col_vecs_ref, turned_ref, fsum_ref, msum_ref = refs[ROW_PARTS + COL_PARTS + 3 :]
+    row_span = left_ref.shape[0]
+    col_span = right_ref.shape[0]
 
     fsum_ref[...] = jnp.zeros_like(fsum_ref)
     msum_ref[...] = jnp.zeros_like(msum_ref)
@@ -95,42 +80,45 @@
     def lanes_of(group, width):
         return jnp.where(lax.div(lane, width) == group, 1.0, 0.0).astype(jnp.bfloat16)
 
-    for copy in row_copies:
-        copy.wait()
-
-    @pl.loop(0, row_span)
-    def _(block):
-        left_ref[block, 0:DESC, 0:DESC] = rows_ref[block, 0:DESC, 0:DESC]
-        left_ref[block, DESC:TILE, 0:DESC] = rows_ref[block, 0:DESC, DESC:TILE]
-
-    @pl.loop(0, row_span // AUG_GROUP)
-    def _(group):
-        offsets = rows_ref[pl.ds(group * AUG_GROUP, AUG_GROUP), DESC:DEPTH, :].reshape(LANES, TILE).T
-        for at in range(AUG_GROUP):
-            left_ref[group * AUG_GROUP + at, :, DESC:FULL] = offsets * lanes_of(at, AUG)
-
-    for copy in col_copies + vec_copies:
-        copy.wait()
-
-    @pl.loop(0, col_span)
-    def _(block):
-        offsets = cols_ref[block, DESC:DEPTH, :]
-        for at in range(1, AUG_GROUP):
-            cols_ref[block, DESC + at * AUG : DESC + (at + 1) * AUG, :] = offsets
+    offset_rows = []
+    for at, part in enumerate(rows_from):
+        size = part.shape[0]
+        for own in range(size):
+            block = at * size + own
+            left_ref[block, 0:DESC, 0:DESC] = part[own, 0:DESC, 0:DESC]
+            left_ref[block, DESC:TILE, 0:DESC] = part[own, 0:DESC, DESC:TILE]
+            row_vecs_ref[block] = part[own, DEPTH:PACK, :]
+            offset_rows.append(part[own, DESC:DEPTH, :])
+            if len(offset_rows) == AUG_GROUP:
+                turned = jnp.concatenate(offset_rows, axis=0).T
+                for place in range(AUG_GROUP):
+                    left_ref[block - AUG_GROUP + 1 + place, :, DESC:FULL] = turned * lanes_of(place, AUG)
+                offset_rows = []
+
+    for at, part in enumerate(cols_from):
+        size = part.shape[0]
+
+        @pl.loop(0, size)
+        def _(own):
+            right_ref[at * size + own, 0:DESC, :] = part[own, 0:DESC, :]
+            offsets = part[own, DESC:DEPTH, :]
+            for place in range(AUG_GROUP):
+                right_ref[at * size + own, DESC + place * AUG : DESC + (place + 1) * AUG, :] = offsets
+            col_vecs_ref[at * size + own] = part[own, DEPTH:PACK, :]
 
     @pl.loop(0, col_span // VEC_GROUP)
     def _(group):
-        narrow = cvecs_ref[pl.ds(group * VEC_GROUP, VEC_GROUP)].reshape(LANES, TILE).T
+        narrow = col_vecs_ref[pl.ds(group * VEC_GROUP, VEC_GROUP)].reshape(LANES, TILE).T
         for at in range(VEC_GROUP):
-            vecs_ref[group * VEC_GROUP + at] = narrow * lanes_of(at, VECS)
+            turned_ref[group * VEC_GROUP + at] = narrow * lanes_of(at, VECS)
 
     def tile(slot):
         row_at = slots_ref[0, slot]
         col_at = slots_ref[1, slot]
-        score = jnp.dot(left_ref[row_at], cols_ref[col_at], preferred_element_type=jnp.float32)
+        score = jnp.dot(left_ref[row_at], right_ref[col_at], preferred_element_type=jnp.float32)
         block = jnp.exp2(score * POWER).astype(jnp.bfloat16)
-        forward = jnp.dot(block, vecs_ref[col_at], preferred_element_type=jnp.float32)
-        mirror = jnp.dot(rows_ref[row_at, DEPTH:PACK, :], block, preferred_element_type=jnp.float32)
+        forward = jnp.dot(block, turned_ref[col_at], preferred_element_type=jnp.float32)
+        mirror = jnp.dot(row_vecs_ref[row_at], block, preferred_element_type=jnp.float32)
         return slots_ref[2, slot], slots_ref[3, slot], forward, mirror
 
     @pl.loop(0, lax.div(count_ref[0, 0] + (UNROLL - 1), UNROLL))
@@ -140,16 +128,11 @@
             fsum_ref[forward_at] += forward
             msum_ref[mirror_at] += mirror
 
-    half = row_span // 2
-
-    def total(block):
+    @pl.loop(0, row_span)
+    def _(block):
         turned = fsum_ref[block].T
-        return sum(turned[at * VECS : (at + 1) * VECS] for at in range(VEC_GROUP))
-
-    @pl.loop(0, half)
-    def _(block):
-        forward_ref[block] = total(block)
-        forward_other_ref[block] = total(half + block).astype(jnp.bfloat16)
+        total = sum(turned[at * VECS : (at + 1) * VECS] for at in range(VEC_GROUP))
+        forward_ref[block] = total.astype(jnp.bfloat16)
 
     mirror_ref[...] = msum_ref[0 : col_span // 2]
     mirror_other_ref[...] = msum_ref[col_span // 2 : col_span].astype(jnp.bfloat16)
@@ -160,30 +143,25 @@
     col_span = sum(part.shape[0] for part in col_parts)
     smem = pl.BlockSpec(memory_space=pltpu.SMEM)
     vmem = pl.BlockSpec(memory_space=pltpu.VMEM)
-    anywhere = pl.BlockSpec(memory_space=pl.ANY)
     return pl.pallas_call(
         tiles_kernel,
         out_shape=(
-            jax.ShapeDtypeStruct((row_span // 2, VECS, TILE), jnp.float32),
-            jax.ShapeDtypeStruct((row_span // 2, VECS, TILE), jnp.bfloat16),
+            jax.ShapeDtypeStruct((row_span, VECS, TILE), jnp.bfloat16),
             jax.ShapeDtypeStruct((col_span // 2, VECS, TILE), jnp.float32),
             jax.ShapeDtypeStruct((col_span // 2, VECS, TILE), jnp.bfloat16),
         ),
-        in_specs=[smem, smem] + [anywhere] * (ROW_PARTS + COL_PARTS),
-        out_specs=(vmem, vmem, vmem, vmem),
+        in_specs=[smem, smem] + [vmem] * (ROW_PARTS + COL_PARTS),
+        out_specs=(vmem, vmem, vmem),
         scratch_shapes=[
-            pltpu.VMEM((row_span, PACK, TILE), jnp.bfloat16),
+            pltpu.VMEM((row_span, TILE, FULL), jnp.bfloat16),
+            pltpu.VMEM((row_span, VECS, TILE), jnp.bfloat16),
             pltpu.VMEM((col_span, FULL, TILE), jnp.bfloat16),
             pltpu.VMEM((col_span, VECS, TILE), jnp.bfloat16),
-            pltpu.VMEM((row_span, TILE, FULL), jnp.bfloat16),
             pltpu.VMEM((col_span, TILE, LANES), jnp.bfloat16),
             pltpu.VMEM((row_span + 1, TILE, LANES), jnp.float32),
             pltpu.VMEM((col_span + 1, VECS, TILE), jnp.float32),
-            pltpu.SemaphoreType.DMA((ROW_PARTS,)),
-            pltpu.SemaphoreType.DMA((COL_PARTS,)),
-            pltpu.SemaphoreType.DMA((COL_PARTS,)),
         ],
-        compiler_params=pltpu.CompilerParams(vmem_limit_bytes=48 * 1024 * 1024),
+        compiler_params=pltpu.CompilerParams(vmem_limit_bytes=36 * 1024 * 1024),
         name="tile_products",
     )(slots, tile_count, *row_parts, *col_parts)
 
@@ -234,16 +212,12 @@
     return [along_z, swapped(along_z, "row", ROW_SIZES, 0, 1)]
 
 
-def add_mirrors(mirror, for_neighbour, after):
-    received, _ = lax.optimization_barrier((swapped(for_neighbour, "row", ROW_SIZES, 0, 1), after))
-    mirror = mirror + received.astype(jnp.float32)
-    bit = ROW_SIZES[1] // 2
-    while bit:
-        sent = mirror[bit:].astype(jnp.bfloat16) if bit > 2 else mirror[bit:]
-        sent, _ = lax.optimization_barrier((sent, after))
-        mirror = mirror[:bit] + swapped(sent, "row", ROW_SIZES, 1, bit).astype(jnp.float32)
-        bit //= 2
-    return mirror[0]
+def add_mirrors(mirror, for_neighbour):
+    mirror = mirror + swapped(for_neighbour, "row", ROW_SIZES, 0, 1).astype(jnp.float32)
+    sent = mirror.astype(jnp.bfloat16)
+    received = [swapped(sent[bits : bits + 2], "row", ROW_SIZES, 1, bits) for bits in (2, 4, 6)]
+    mirror = mirror[0:2] + sum(part.astype(jnp.float32) for part in received)
+    return mirror[0] + swapped(mirror[1], "row", ROW_SIZES, 1, 1)
 
 
 def slot_places(tile_pairs, tile_count):
@@ -260,7 +234,7 @@
         [
             (core * 4 + x) * 4 + y_hi,
             (row_there[0] ^ row_here[0]) * (col_span // 2) + row_there[1],
-            jnp.where(live, core * (row_span // 2) + (local_row >> 1), row_span),
+            jnp.where(live, local_row, row_span),
             jnp.where(live & (i != j), local_col ^ lax.axis_index("row"), col_span),
         ]
     )
@@ -271,11 +245,9 @@
     col_parts = gather_cols(col_copies)
     row_parts = gather_rows(row_own)
     slots = slot_places(pattern[0, 0], counts[0, 0])
-    forward, for_other_core, mirror, for_neighbour = tile_products(slots, counts, row_parts, col_parts)
-    for_other_core = swapped(for_other_core, "col", COL_SIZES, 2, 1)
-    forward = (forward + for_other_core.astype(jnp.float32)).astype(jnp.bfloat16)
-    mirror = add_mirrors(mirror, for_neighbour, forward)
-    forward = grouped_all_to_all(forward, "col", COL_SIZES, lambda place: place[2])
+    forward, mirror, for_neighbour = tile_products(slots, counts, row_parts, col_parts)
+    mirror = add_mirrors(mirror, for_neighbour)
+    forward = lax.all_to_all(forward, "col", 0, 0, tiled=True)
     return jnp.sum(forward.astype(jnp.float32), axis=0) + mirror
 
 

time: 128 us -> 125 us (0.977)
  the two profiles are of different devices: /device:TPU:2 before, /device:TPU:6 now
where the time goes in v5:
time: 125 us; the launch traced here: 123 us
  starting transfers between devices  72.3 us (58%)
  Pallas kernels  34 us (27%)
  waiting for transfers between devices  14.3 us (11%)
    ppermute x16, starting transfers between devices, moved(): return lax.ppermute(value, axis, pairs)  54.4 us
    pallas_call x1, Pallas kernels, tile_products(): pl.pallas_call(tiles_kernel, out_shape=(jax.ShapeDtypeStruct((row_span, V...  32.1 us
    ppermute x16, waiting for transfers between devices, moved(): return lax.ppermute(value, axis, pairs)  14 us
    all_to_all x1, starting transfers between devices, grouped_all_to_all(): lax.all_to_all(value, axis, 0, 0, axis_index_groups=list(groups.values())...  10.4 us
    all_to_all x1, starting transfers between devices, body(): forward = lax.all_to_all(forward, 'col', 0, 0, tiled=True)  7.46 us
  transfers between devices with their start and end apart: 18, of which 7 were waited for; matrix products, arithmetic and copies ran while one was open for 0% of the time, Pallas kernels for 0%

profile of v5, /device:TPU:6, one launch (start us, length us, event | category | flops | bytes accessed | tf_op | source)
XLA Modules:
  0.0 123.0 jit_solution(17365092104467774026)
XLA Ops:
  0.0 1.9 %pack_blocks.1 = (bf16[176,256]{1,0:T(8,128)(2,1)}, bf16[8,176,256]{2,1,0:T(8,128)(2,1)}) custom-call(bf16[256,128]{1,0:T(8,128)(2,1)} %feat_ref.1, bf16[256]{0:T(256)(128)(2,1)} %scale_ref.1, f32[32,256]{1,0:T(8,128)} %vec_ref.1), custom_call_target="tpu_custom_call" | custom-call | tf_op jit(solution)/shard_map/pack_blocks/pallas_call | solution.py:64
  1.9 0.0 copy-start
  1.9 10.4 %all-to-all-start = ((bf16[8,176,256]{2,1,0:T(8,128)(2,1)}), bf16[8,176,256]{2,1,0:T(8,128)(2,1)S(1)}, u32[]{:S(2)}, u32[]{:S(2)}) async-start(bf16[8,176,256]{2,1,0:T(8,128)(2,1)} %get-tuple-element.11), calls=%async_computation | async-start | bytes 1441792 | tf_op jit(solution)/shard_map/all_to_all | solution.py:207
  12.3 0.0 copy-done
  12.3 6.2 %collective-permute-start.2 = (bf16[176,256]{1,0:T(8,128)(2,1)S(1)}, bf16[176,256]{1,0:T(8,128)(2,1)S(1)}, u32[]{:S(2)}, u32[]{:S(2)}) collective-permute-start(bf16[176,256]{1,0:T(8,128)(2,1)S(1)} %copy-done), channel_id=1, source_target_pairs={{0,24},{1,25},{2,26},{3,27},{4,28},{5,29},{6,30},{7,31},{8,0},{9,1... | collective-permute-start | bytes 270344 | tf_op jit(solution)/shard_map/ppermute | solution.py:178
  18.5 3.8 %collective-permute-start.1 = (bf16[176,256]{1,0:T(8,128)(2,1)S(1)}, bf16[176,256]{1,0:T(8,128)(2,1)S(1)}, u32[]{:S(2)}, u32[]{:S(2)}) collective-permute-start(bf16[176,256]{1,0:T(8,128)(2,1)S(1)} %copy-done), channel_id=1, source_target_pairs={{0,16},{1,17},{2,18},{3,19},{4,20},{5,21},{6,22},{7,23},{8,24},{9,... | collective-permute-start | bytes 270344 | tf_op jit(solution)/shard_map/ppermute | solution.py:178
  22.3 4.5 %collective-permute-start = (bf16[176,256]{1,0:T(8,128)(2,1)S(1)}, bf16[176,256]{1,0:T(8,128)(2,1)S(1)}, u32[]{:S(2)}, u32[]{:S(2)}) collective-permute-start(bf16[176,256]{1,0:T(8,128)(2,1)S(1)} %copy-done), channel_id=1, source_target_pairs={{0,8},{1,9},{2,10},{3,11},{4,12},{5,13},{6,14},{7,15},{8,16},{9,17... | collective-permute-start | bytes 270344 | tf_op jit(solution)/shard_map/ppermute | solution.py:178
  26.8 0.0 collective-permute-done.2
  26.9 4.6 %collective-permute-done.1 = bf16[176,256]{1,0:T(8,128)(2,1)S(1)} collective-permute-done((bf16[176,256]{1,0:T(8,128)(2,1)S(1)}, bf16[176,256]{1,0:T(8,128)(2,1)S(1)}, u32[]{:S(2)}, u32[]{:S(2)}) %collective-permute-start.1) | collective-permute-done | bytes 90144 | tf_op jit(solution)/shard_map/ppermute | solution.py:178
  31.5 0.0 collective-permute-done
  31.5 2.7 %collective-permute-start.5 = (bf16[4,176,256]{2,1,0:T(8,128)(2,1)S(1)}, bf16[4,176,256]{2,1,0:T(8,128)(2,1)S(1)}, u32[]{:S(2)}, u32[]{:S(2)}) collective-permute-start(bf16[4,176,256]{2,1,0:T(8,128)(2,1)S(1)} %pad_maximum_fusion.refs_0_), channel_id=1, source_target_pairs={{0,6},{1,7},{2,0},{3,1},{4,2},{5,3},{6,4},{7,5},{8,14},{9,15},{10,... | collective-permute-start | bytes 1081352 | tf_op jit(solution)/shard_map/ppermute | solution.py:178
  34.3 3.0 %collective-permute-start.4 = (bf16[4,176,256]{2,1,0:T(8,128)(2,1)S(1)}, bf16[4,176,256]{2,1,0:T(8,128)(2,1)S(1)}, u32[]{:S(2)}, u32[]{:S(2)}) collective-permute-start(bf16[4,176,256]{2,1,0:T(8,128)(2,1)S(1)} %pad_maximum_fusion.refs_0_), channel_id=1, source_target_pairs={{0,4},{1,5},{2,6},{3,7},{4,0},{5,1},{6,2},{7,3},{8,12},{9,13},{10,... | collective-permute-start | bytes 1081352 | tf_op jit(solution)/shard_map/ppermute | solution.py:178
  37.3 4.0 %collective-permute-start.3 = (bf16[4,176,256]{2,1,0:T(8,128)(2,1)S(1)}, bf16[4,176,256]{2,1,0:T(8,128)(2,1)S(1)}, u32[]{:S(2)}, u32[]{:S(2)}) collective-permute-start(bf16[4,176,256]{2,1,0:T(8,128)(2,1)S(1)} %pad_maximum_fusion.refs_0_), channel_id=1, source_target_pairs={{0,2},{1,3},{2,4},{3,5},{4,6},{5,7},{6,0},{7,1},{8,10},{9,11},{10,... | collective-permute-start | bytes 1081352 | tf_op jit(solution)/shard_map/ppermute | solution.py:178
  41.3 0.0 all-to-all-done.refs_8_
  41.3 4.7 %collective-permute-start.10 = (bf16[8,176,256]{2,1,0:T(8,128)(2,1)S(1)}, bf16[8,176,256]{2,1,0:T(8,128)(2,1)S(1)}, u32[]{:S(2)}, u32[]{:S(2)}) collective-permute-start(bf16[8,176,256]{2,1,0:T(8,128)(2,1)S(1)} %all-to-all-done.refs_8_), channel_id=1, source_target_pairs={{0,256},{32,288},{64,320},{96,352},{128,384},{160,416},{192,448},{... | collective-permute-start | bytes 2162696 | tf_op jit(solution)/shard_map/ppermute | solution.py:178
  46.0 1.9 %collective-permute-start.6 = (bf16[4,176,256]{2,1,0:T(8,128)(2,1)S(1)}, bf16[4,176,256]{2,1,0:T(8,128)(2,1)S(1)}, u32[]{:S(2)}, u32[]{:S(2)}) collective-permute-start(bf16[4,176,256]{2,1,0:T(8,128)(2,1)S(1)} %pad_maximum_fusion.refs_0_), channel_id=1, source_target_pairs={{0,1},{1,0},{2,3},{3,2},{4,5},{5,4},{6,7},{7,6},{8,9},{9,8},{10,11... | collective-permute-start | bytes 1081352 | tf_op jit(solution)/shard_map/ppermute | solution.py:178
  47.9 2.5 %collective-permute-done.5.refs_3_ = bf16[4,176,256]{2,1,0:T(8,128)(2,1)S(1)} collective-permute-done((bf16[4,176,256]{2,1,0:T(8,128)(2,1)S(1)}, bf16[4,176,256]{2,1,0:T(8,128)(2,1)S(1)}, u32[]{:S(2)}, u32[]{:S(2)}) %collective-permute-start.5) | collective-permute-done | bytes 360480 | tf_op jit(solution)/shard_map/ppermute | solution.py:178
  50.5 1.9 %collective-permute-start.9 = (bf16[4,176,256]{2,1,0:T(8,128)(2,1)S(1)}, bf16[4,176,256]{2,1,0:T(8,128)(2,1)}, u32[]{:S(2)}, u32[]{:S(2)}) collective-permute-start(bf16[4,176,256]{2,1,0:T(8,128)(2,1)S(1)} %collective-permute-done.5.refs_3_), channel_id=1, source_target_pairs={{0,1},{1,0},{2,3},{3,2},{4,5},{5,4},{6,7},{7,6},{8,9},{9,8},{10,11... | collective-permute-start | bytes 1081352 | tf_op jit(solution)/shard_map/ppermute | solution.py:178
  52.4 0.0 collective-permute-done.4.refs_2_
  52.4 2.4 %collective-permute-start.8 = (bf16[4,176,256]{2,1,0:T(8,128)(2,1)S(1)}, bf16[4,176,256]{2,1,0:T(8,128)(2,1)}, u32[]{:S(2)}, u32[]{:S(2)}) collective-permute-start(bf16[4,176,256]{2,1,0:T(8,128)(2,1)S(1)} %collective-permute-done.4.refs_2_), channel_id=1, source_target_pairs={{0,1},{1,0},{2,3},{3,2},{4,5},{5,4},{6,7},{7,6},{8,9},{9,8},{10,11... | collective-permute-start | bytes 1081352 | tf_op jit(solution)/shard_map/ppermute | solution.py:178
  54.8 0.0 collective-permute-done.3.refs_1_
  54.8 1.9 %collective-permute-start.7 = (bf16[4,176,256]{2,1,0:T(8,128)(2,1)S(1)}, bf16[4,176,256]{2,1,0:T(8,128)(2,1)}, u32[]{:S(2)}, u32[]{:S(2)}) collective-permute-start(bf16[4,176,256]{2,1,0:T(8,128)(2,1)S(1)} %collective-permute-done.3.refs_1_), channel_id=1, source_target_pairs={{0,1},{1,0},{2,3},{3,2},{4,5},{5,4},{6,7},{7,6},{8,9},{9,8},{10,11... | collective-permute-start | bytes 1081352 | tf_op jit(solution)/shard_map/ppermute | solution.py:178
  57.4 0.0 copy-start.1
  57.4 0.7 copy-done.1
  58.1 0.0 collective-permute-done.6.refs_4_
  58.1 0.0 collective-permute-done.9.refs_7_
  58.1 0.0 collective-permute-done.8.refs_6_
  58.1 0.4 collective-permute-done.7.refs_5_
  58.5 2.3 %collective-permute-done.10.refs_9_ = bf16[8,176,256]{2,1,0:T(8,128)(2,1)S(1)} collective-permute-done((bf16[8,176,256]{2,1,0:T(8,128)(2,1)S(1)}, bf16[8,176,256]{2,1,0:T(8,128)(2,1)S(1)}, u32[]{:S(2)}, u32[]{:S(2)}) %collective-permute-start.10) | collective-permute-done | bytes 720928 | tf_op jit(solution)/shard_map/ppermute | solution.py:178
  60.8 32.1 %tile_products.1 = (bf16[32,32,256]{2,1,0:T(8,128)(2,1)}, f32[8,32,256]{2,1,0:T(8,128)S(1)}, bf16[8,32,256]{2,1,0:T(8,128)(2,1)}) custom-call(s32[4,128]{1,0:T(4,128)S(1)} %pad_add_fusion.slots_ref, s32[1,1]{1,0:T(1,128)} %copy.6.count_ref, bf16[4,176,256]{2,1,0:T(8,128)(2,1)S(1)} %pad_maximum_fusion.refs_0_, ...), custom_call_target="tpu_custom_call" | custom-call | tf_op jit(solution)/shard_map/tile_products/pallas_call | solution.py:146
  92.9 1.9 %collective-permute-start.11 = (bf16[8,32,256]{2,1,0:T(8,128)(2,1)}, bf16[8,32,256]{2,1,0:T(8,128)(2,1)S(1)}, u32[]{:S(2)}, u32[]{:S(2)}) collective-permute-start(bf16[8,32,256]{2,1,0:T(8,128)(2,1)} %get-tuple-element.14), channel_id=1, source_target_pairs={{0,256},{32,288},{64,320},{96,352},{128,384},{160,416},{192,448},{... | collective-permute-start | bytes 393224 | tf_op jit(solution)/shard_map/ppermute | solution.py:178
  94.8 7.5 %all-to-all-start.1 = ((bf16[32,32,256]{2,1,0:T(8,128)(2,1)}), bf16[32,32,256]{2,1,0:T(8,128)(2,1)S(1)}, u32[]{:S(2)}, u32[]{:S(2)}) async-start(bf16[32,32,256]{2,1,0:T(8,128)(2,1)} %get-tuple-element.12), calls=%async_computation.1 | async-start | bytes 1048576 | tf_op jit(solution)/shard_map/all_to_all | solution.py:250
  102.3 0.0 collective-permute-done.11
  102.4 1.9 %collective-permute-start.12 = (bf16[2,32,256]{2,1,0:T(8,128)(2,1)S(1)}, bf16[2,32,256]{2,1,0:T(8,128)(2,1)S(1)}, u32[]{:S(2)}, u32[]{:S(2)}) collective-permute-start(bf16[2,32,256]{2,1,0:T(8,128)(2,1)S(1)} %get-tuple-element.17), channel_id=1, source_target_pairs={{0,64},{32,96},{64,0},{96,32},{128,192},{160,224},{192,128},{224,1... | collective-permute-start | bytes 98312 | tf_op jit(solution)/shard_map/ppermute | solution.py:178
  104.3 2.3 %collective-permute-start.14 = (bf16[2,32,256]{2,1,0:T(8,128)(2,1)S(1)}, bf16[2,32,256]{2,1,0:T(8,128)(2,1)S(1)}, u32[]{:S(2)}, u32[]{:S(2)}) collective-permute-start(bf16[2,32,256]{2,1,0:T(8,128)(2,1)S(1)} %get-tuple-element.18), channel_id=1, source_target_pairs={{0,192},{32,224},{64,128},{96,160},{128,64},{160,96},{192,0},{224,... | collective-permute-start | bytes 98312 | tf_op jit(solution)/shard_map/ppermute | solution.py:178
  106.6 8.0 %collective-permute-start.13 = (bf16[2,32,256]{2,1,0:T(8,128)(2,1)S(1)}, bf16[2,32,256]{2,1,0:T(8,128)(2,1)S(1)}, u32[]{:S(2)}, u32[]{:S(2)}) collective-permute-start(bf16[2,32,256]{2,1,0:T(8,128)(2,1)S(1)} %get-tuple-element.19), channel_id=1, source_target_pairs={{0,128},{32,160},{64,192},{96,224},{128,0},{160,32},{192,64},{224,... | collective-permute-start | bytes 98312 | tf_op jit(solution)/shard_map/ppermute | solution.py:178
  114.6 0.0 collective-permute-done.12
  114.6 0.0 collective-permute-done.14
  114.6 1.9 %collective-permute-done.13 = bf16[2,32,256]{2,1,0:T(8,128)(2,1)S(1)} collective-permute-done((bf16[2,32,256]{2,1,0:T(8,128)(2,1)S(1)}, bf16[2,32,256]{2,1,0:T(8,128)(2,1)S(1)}, u32[]{:S(2)}, u32[]{:S(2)}) %collective-permute-start.13) | collective-permute-done | bytes 32800 | tf_op jit(solution)/shard_map/ppermute | solution.py:178
  116.6 3.2 %collective-permute-start.15 = (f32[32,256]{1,0:T(8,128)S(1)}, f32[32,256]{1,0:T(8,128)S(1)}, u32[]{:S(2)}, u32[]{:S(2)}) collective-permute-start(f32[32,256]{1,0:T(8,128)S(1)} %slice_bitcast_fusion), channel_id=1, source_target_pairs={{0,32},{32,0},{64,96},{96,64},{128,160},{160,128},{192,224},{224,1... | collective-permute-start | bytes 98312 | tf_op jit(solution)/shard_map/ppermute | solution.py:178
  119.8 0.3 all-to-all-done.1
  120.0 0.1 convert_reduce_fusion
  120.1 2.3 %collective-permute-done.15 = f32[32,256]{1,0:T(8,128)S(1)} collective-permute-done((f32[32,256]{1,0:T(8,128)S(1)}, f32[32,256]{1,0:T(8,128)S(1)}, u32[]{:S(2)}, u32[]{:S(2)}) %collective-permute-start.15) | collective-permute-done | bytes 32800 | tf_op jit(solution)/shard_map/ppermute | solution.py:178
  122.4 0.6 fusion.1
  (7 shorter events, 0.1 us)
Async XLA Ops:
  1.9 10.5 %copy-start = (bf16[176,256]{1,0:T(8,128)(2,1)S(1)}, bf16[176,256]{1,0:T(8,128)(2,1)}, u32[]{:S(2)}) copy-start(bf16[176,256]{1,0:T(8,128)(2,1)} %get-tuple-element.10) | copy-start | bytes 270340
  1.9 39.4 %all-to-all-start = ((bf16[8,176,256]{2,1,0:T(8,128)(2,1)}), bf16[8,176,256]{2,1,0:T(8,128)(2,1)S(1)}, u32[]{:S(2)}, u32[]{:S(2)}) async-start(bf16[8,176,256]{2,1,0:T(8,128)(2,1)} %get-tuple-element.11), calls=%async_computation | async-start | bytes 1441792 | tf_op jit(solution)/shard_map/all_to_all | solution.py:207
  12.3 14.5 %collective-permute-start.2 = (bf16[176,256]{1,0:T(8,128)(2,1)S(1)}, bf16[176,256]{1,0:T(8,128)(2,1)S(1)}, u32[]{:S(2)}, u32[]{:S(2)}) collective-permute-start(bf16[176,256]{1,0:T(8,128)(2,1)S(1)} %copy-done), channel_id=1, source_target_pairs={{0,24},{1,25},{2,26},{3,27},{4,28},{5,29},{6,30},{7,31},{8,0},{9,1... | collective-permute-start | bytes 270344 | tf_op jit(solution)/shard_map/ppermute | solution.py:178
  18.5 12.9 %collective-permute-start.1 = (bf16[176,256]{1,0:T(8,128)(2,1)S(1)}, bf16[176,256]{1,0:T(8,128)(2,1)S(1)}, u32[]{:S(2)}, u32[]{:S(2)}) collective-permute-start(bf16[176,256]{1,0:T(8,128)(2,1)S(1)} %copy-done), channel_id=1, source_target_pairs={{0,16},{1,17},{2,18},{3,19},{4,20},{5,21},{6,22},{7,23},{8,24},{9,... | collective-permute-start | bytes 270344 | tf_op jit(solution)/shard_map/ppermute | solution.py:178
  22.3 9.1 %collective-permute-start = (bf16[176,256]{1,0:T(8,128)(2,1)S(1)}, bf16[176,256]{1,0:T(8,128)(2,1)S(1)}, u32[]{:S(2)}, u32[]{:S(2)}) collective-permute-start(bf16[176,256]{1,0:T(8,128)(2,1)S(1)} %copy-done), channel_id=1, source_target_pairs={{0,8},{1,9},{2,10},{3,11},{4,12},{5,13},{6,14},{7,15},{8,16},{9,17... | collective-permute-start | bytes 270344 | tf_op jit(solution)/shard_map/ppermute | solution.py:178
  31.5 18.9 %collective-permute-start.5 = (bf16[4,176,256]{2,1,0:T(8,128)(2,1)S(1)}, bf16[4,176,256]{2,1,0:T(8,128)(2,1)S(1)}, u32[]{:S(2)}, u32[]{:S(2)}) collective-permute-start(bf16[4,176,256]{2,1,0:T(8,128)(2,1)S(1)} %pad_maximum_fusion.refs_0_), channel_id=1, source_target_pairs={{0,6},{1,7},{2,0},{3,1},{4,2},{5,3},{6,4},{7,5},{8,14},{9,15},{10,... | collective-permute-start | bytes 1081352 | tf_op jit(solution)/shard_map/ppermute | solution.py:178
  34.3 18.1 %collective-permute-start.4 = (bf16[4,176,256]{2,1,0:T(8,128)(2,1)S(1)}, bf16[4,176,256]{2,1,0:T(8,128)(2,1)S(1)}, u32[]{:S(2)}, u32[]{:S(2)}) collective-permute-start(bf16[4,176,256]{2,1,0:T(8,128)(2,1)S(1)} %pad_maximum_fusion.refs_0_), channel_id=1, source_target_pairs={{0,4},{1,5},{2,6},{3,7},{4,0},{5,1},{6,2},{7,3},{8,12},{9,13},{10,... | collective-permute-start | bytes 1081352 | tf_op jit(solution)/shard_map/ppermute | solution.py:178
  37.3 17.5 %collective-permute-start.3 = (bf16[4,176,256]{2,1,0:T(8,128)(2,1)S(1)}, bf16[4,176,256]{2,1,0:T(8,128)(2,1)S(1)}, u32[]{:S(2)}, u32[]{:S(2)}) collective-permute-start(bf16[4,176,256]{2,1,0:T(8,128)(2,1)S(1)} %pad_maximum_fusion.refs_0_), channel_id=1, source_target_pairs={{0,2},{1,3},{2,4},{3,5},{4,6},{5,7},{6,0},{7,1},{8,10},{9,11},{10,... | collective-permute-start | bytes 1081352 | tf_op jit(solution)/shard_map/ppermute | solution.py:178
  41.3 19.5 %collective-permute-start.10 = (bf16[8,176,256]{2,1,0:T(8,128)(2,1)S(1)}, bf16[8,176,256]{2,1,0:T(8,128)(2,1)S(1)}, u32[]{:S(2)}, u32[]{:S(2)}) collective-permute-start(bf16[8,176,256]{2,1,0:T(8,128)(2,1)S(1)} %all-to-all-done.refs_8_), channel_id=1, source_target_pairs={{0,256},{32,288},{64,320},{96,352},{128,384},{160,416},{192,448},{... | collective-permute-start | bytes 2162696 | tf_op jit(solution)/shard_map/ppermute | solution.py:178
  46.0 12.1 %collective-permute-start.6 = (bf16[4,176,256]{2,1,0:T(8,128)(2,1)S(1)}, bf16[4,176,256]{2,1,0:T(8,128)(2,1)S(1)}, u32[]{:S(2)}, u32[]{:S(2)}) collective-permute-start(bf16[4,176,256]{2,1,0:T(8,128)(2,1)S(1)} %pad_maximum_fusion.refs_0_), channel_id=1, source_target_pairs={{0,1},{1,0},{2,3},{3,2},{4,5},{5,4},{6,7},{7,6},{8,9},{9,8},{10,11... | collective-permute-start | bytes 1081352 | tf_op jit(solution)/shard_map/ppermute | solution.py:178
  50.5 7.7 %collective-permute-start.9 = (bf16[4,176,256]{2,1,0:T(8,128)(2,1)S(1)}, bf16[4,176,256]{2,1,0:T(8,128)(2,1)}, u32[]{:S(2)}, u32[]{:S(2)}) collective-permute-start(bf16[4,176,256]{2,1,0:T(8,128)(2,1)S(1)} %collective-permute-done.5.refs_3_), channel_id=1, source_target_pairs={{0,1},{1,0},{2,3},{3,2},{4,5},{5,4},{6,7},{7,6},{8,9},{9,8},{10,11... | collective-permute-start | bytes 1081352 | tf_op jit(solution)/shard_map/ppermute | solution.py:178
  52.4 5.8 %collective-permute-start.8 = (bf16[4,176,256]{2,1,0:T(8,128)(2,1)S(1)}, bf16[4,176,256]{2,1,0:T(8,128)(2,1)}, u32[]{:S(2)}, u32[]{:S(2)}) collective-permute-start(bf16[4,176,256]{2,1,0:T(8,128)(2,1)S(1)} %collective-permute-done.4.refs_2_), channel_id=1, source_target_pairs={{0,1},{1,0},{2,3},{3,2},{4,5},{5,4},{6,7},{7,6},{8,9},{9,8},{10,11... | collective-permute-start | bytes 1081352 | tf_op jit(solution)/shard_map/ppermute | solution.py:178
  54.8 3.7 %collective-permute-start.7 = (bf16[4,176,256]{2,1,0:T(8,128)(2,1)S(1)}, bf16[4,176,256]{2,1,0:T(8,128)(2,1)}, u32[]{:S(2)}, u32[]{:S(2)}) collective-permute-start(bf16[4,176,256]{2,1,0:T(8,128)(2,1)S(1)} %collective-permute-done.3.refs_1_), channel_id=1, source_target_pairs={{0,1},{1,0},{2,3},{3,2},{4,5},{5,4},{6,7},{7,6},{8,9},{9,8},{10,11... | collective-permute-start | bytes 1081352 | tf_op jit(solution)/shard_map/ppermute | solution.py:178
  57.4 0.7 copy-start.1
  92.9 9.4 %collective-permute-start.11 = (bf16[8,32,256]{2,1,0:T(8,128)(2,1)}, bf16[8,32,256]{2,1,0:T(8,128)(2,1)S(1)}, u32[]{:S(2)}, u32[]{:S(2)}) collective-permute-start(bf16[8,32,256]{2,1,0:T(8,128)(2,1)} %get-tuple-element.14), channel_id=1, source_target_pairs={{0,256},{32,288},{64,320},{96,352},{128,384},{160,416},{192,448},{... | collective-permute-start | bytes 393224 | tf_op jit(solution)/shard_map/ppermute | solution.py:178
  94.8 25.2 %all-to-all-start.1 = ((bf16[32,32,256]{2,1,0:T(8,128)(2,1)}), bf16[32,32,256]{2,1,0:T(8,128)(2,1)S(1)}, u32[]{:S(2)}, u32[]{:S(2)}) async-start(bf16[32,32,256]{2,1,0:T(8,128)(2,1)} %get-tuple-element.12), calls=%async_computation.1 | async-start | bytes 1048576 | tf_op jit(solution)/shard_map/all_to_all | solution.py:250
  102.4 12.2 %collective-permute-start.12 = (bf16[2,32,256]{2,1,0:T(8,128)(2,1)S(1)}, bf16[2,32,256]{2,1,0:T(8,128)(2,1)S(1)}, u32[]{:S(2)}, u32[]{:S(2)}) collective-permute-start(bf16[2,32,256]{2,1,0:T(8,128)(2,1)S(1)} %get-tuple-element.17), channel_id=1, source_target_pairs={{0,64},{32,96},{64,0},{96,32},{128,192},{160,224},{192,128},{224,1... | collective-permute-start | bytes 98312 | tf_op jit(solution)/shard_map/ppermute | solution.py:178
  104.3 10.3 %collective-permute-start.14 = (bf16[2,32,256]{2,1,0:T(8,128)(2,1)S(1)}, bf16[2,32,256]{2,1,0:T(8,128)(2,1)S(1)}, u32[]{:S(2)}, u32[]{:S(2)}) collective-permute-start(bf16[2,32,256]{2,1,0:T(8,128)(2,1)S(1)} %get-tuple-element.18), channel_id=1, source_target_pairs={{0,192},{32,224},{64,128},{96,160},{128,64},{160,96},{192,0},{224,... | collective-permute-start | bytes 98312 | tf_op jit(solution)/shard_map/ppermute | solution.py:178
  106.6 9.9 %collective-permute-start.13 = (bf16[2,32,256]{2,1,0:T(8,128)(2,1)S(1)}, bf16[2,32,256]{2,1,0:T(8,128)(2,1)S(1)}, u32[]{:S(2)}, u32[]{:S(2)}) collective-permute-start(bf16[2,32,256]{2,1,0:T(8,128)(2,1)S(1)} %get-tuple-element.19), channel_id=1, source_target_pairs={{0,128},{32,160},{64,192},{96,224},{128,0},{160,32},{192,64},{224,... | collective-permute-start | bytes 98312 | tf_op jit(solution)/shard_map/ppermute | solution.py:178
  116.6 5.8 %collective-permute-start.15 = (f32[32,256]{1,0:T(8,128)S(1)}, f32[32,256]{1,0:T(8,128)S(1)}, u32[]{:S(2)}, u32[]{:S(2)}) collective-permute-start(f32[32,256]{1,0:T(8,128)S(1)} %slice_bitcast_fusion), channel_id=1, source_target_pairs={{0,32},{32,0},{64,96},{96,64},{128,160},{160,128},{192,224},{224,1... | collective-permute-start | bytes 98312 | tf_op jit(solution)/shard_map/ppermute | solution.py:178

commit v6 on v5

--- a/solution.py
+++ b/solution.py
@@ -17,7 +17,7 @@
 LANES = 128
 AUG_GROUP = LANES // AUG
 VEC_GROUP = LANES // VECS
-UNROLL = 16
+UNROLL = 8
 
 COL_SIZES = (4, 4, 2)
 ROW_SIZES = (2, 8)
@@ -112,27 +112,45 @@
         for at in range(VEC_GROUP):
             turned_ref[group * VEC_GROUP + at] = narrow * lanes_of(at, VECS)
 
-    def tile(slot):
-        row_at = slots_ref[0, slot]
-        col_at = slots_ref[1, slot]
-        score = jnp.dot(left_ref[row_at], right_ref[col_at], preferred_element_type=jnp.float32)
+    def scores(slot):
+        left, right = left_ref[slots_ref[0, slot]], right_ref[slots_ref[1, slot]]
+        return jnp.dot(left, right, preferred_element_type=jnp.float32)
+
+    def products(slot, score):
         block = jnp.exp2(score * POWER).astype(jnp.bfloat16)
-        forward = jnp.dot(block, turned_ref[col_at], preferred_element_type=jnp.float32)
-        mirror = jnp.dot(row_vecs_ref[row_at], block, preferred_element_type=jnp.float32)
+        forward = jnp.dot(block, turned_ref[slots_ref[1, slot]], preferred_element_type=jnp.float32)
+        mirror = jnp.dot(row_vecs_ref[slots_ref[0, slot]], block, preferred_element_type=jnp.float32)
         return slots_ref[2, slot], slots_ref[3, slot], forward, mirror
 
     @pl.loop(0, lax.div(count_ref[0, 0] + (UNROLL - 1), UNROLL))
     def _(group):
-        done = [tile(group * UNROLL + step) for step in range(UNROLL)]
+        done = []
+        score = scores(group * UNROLL)
+        for step in range(UNROLL):
+            slot = group * UNROLL + step
+            following = scores(slot + 1) if step + 1 < UNROLL else None
+            done.append(products(slot, score))
+            score = following
         for forward_at, mirror_at, forward, mirror in done:
             fsum_ref[forward_at] += forward
             msum_ref[mirror_at] += mirror
 
-    @pl.loop(0, row_span)
-    def _(block):
-        turned = fsum_ref[block].T
-        total = sum(turned[at * VECS : (at + 1) * VECS] for at in range(VEC_GROUP))
-        forward_ref[block] = total.astype(jnp.bfloat16)
+    lane_group = lax.div(lane, VECS)
+
+    @pl.loop(0, row_span // VEC_GROUP)
+    def _(group):
+        sums = [fsum_ref[group * VEC_GROUP + at] for at in range(VEC_GROUP)]
+        merged = None
+        for shift in range(VEC_GROUP):
+            chosen = sums[shift]
+            for at in range(1, VEC_GROUP):
+                chosen = jnp.where(lane_group == at, sums[(at + shift) % VEC_GROUP], chosen)
+            if shift:
+                chosen = pltpu.roll(chosen, shift * VECS, 1)
+            merged = chosen if merged is None else merged + chosen
+        turned = merged.T.astype(jnp.bfloat16)
+        for at in range(VEC_GROUP):
+            forward_ref[group * VEC_GROUP + at] = turned[at * VECS : (at + 1) * VECS]
 
     mirror_ref[...] = msum_ref[0 : col_span // 2]
     mirror_other_ref[...] = msum_ref[col_span // 2 : col_span].astype(jnp.bfloat16)

time: 125 us -> 116 us (0.928)
  Pallas kernels: 34 us -> 24.7 us
  waiting for transfers between devices: 14.3 us -> 16.1 us
    pallas_call x1, Pallas kernels: 32.1 us -> 22.8 us  [tile_products(): pl.pallas_call(tiles_kernel, out_shape=(jax.ShapeDtypeStruct((row_span, V...]
    ppermute x16, waiting for transfers between devices: 14 us -> 15.5 us  [moved(): return lax.ppermute(value, axis, pairs)]
where the time goes in v6:
time: 116 us; the launch traced here: 114 us
  starting transfers between devices  71.2 us (61%)
  Pallas kernels  24.7 us (21%)
  waiting for transfers between devices  16.1 us (14%)
    ppermute x16, starting transfers between devices, moved(): return lax.ppermute(value, axis, pairs)  53.2 us
    pallas_call x1, Pallas kernels, tile_products(): pl.pallas_call(tiles_kernel, out_shape=(jax.ShapeDtypeStruct((row_span, V...  22.8 us
    ppermute x16, waiting for transfers between devices, moved(): return lax.ppermute(value, axis, pairs)  15.5 us
    all_to_all x1, starting transfers between devices, grouped_all_to_all(): lax.all_to_all(value, axis, 0, 0, axis_index_groups=list(groups.values())...  10.4 us
    all_to_all x1, starting transfers between devices, body(): forward = lax.all_to_all(forward, 'col', 0, 0, tiled=True)  7.46 us
  transfers between devices with their start and end apart: 18, of which 7 were waited for; matrix products, arithmetic and copies ran while one was open for 0% of the time, Pallas kernels for 0%

profile of v6, /device:TPU:6, one launch (start us, length us, event | category | flops | bytes accessed | tf_op | source)
XLA Modules:
  0.0 114.4 jit_solution(4672837749120845083)
XLA Ops:
  0.0 1.9 %pack_blocks.1 = (bf16[176,256]{1,0:T(8,128)(2,1)}, bf16[8,176,256]{2,1,0:T(8,128)(2,1)}) custom-call(bf16[256,128]{1,0:T(8,128)(2,1)} %feat_ref.1, bf16[256]{0:T(256)(128)(2,1)} %scale_ref.1, f32[32,256]{1,0:T(8,128)} %vec_ref.1), custom_call_target="tpu_custom_call" | custom-call | tf_op jit(solution)/shard_map/pack_blocks/pallas_call | solution.py:64
  1.9 0.0 copy-start
  1.9 10.4 %all-to-all-start = ((bf16[8,176,256]{2,1,0:T(8,128)(2,1)}), bf16[8,176,256]{2,1,0:T(8,128)(2,1)S(1)}, u32[]{:S(2)}, u32[]{:S(2)}) async-start(bf16[8,176,256]{2,1,0:T(8,128)(2,1)} %get-tuple-element.11), calls=%async_computation | async-start | bytes 1441792 | tf_op jit(solution)/shard_map/all_to_all | solution.py:225
  12.3 0.0 copy-done
  12.3 6.2 %collective-permute-start.2 = (bf16[176,256]{1,0:T(8,128)(2,1)S(1)}, bf16[176,256]{1,0:T(8,128)(2,1)S(1)}, u32[]{:S(2)}, u32[]{:S(2)}) collective-permute-start(bf16[176,256]{1,0:T(8,128)(2,1)S(1)} %copy-done), channel_id=1, source_target_pairs={{0,24},{1,25},{2,26},{3,27},{4,28},{5,29},{6,30},{7,31},{8,0},{9,1... | collective-permute-start | bytes 270344 | tf_op jit(solution)/shard_map/ppermute | solution.py:196
  18.5 3.8 %collective-permute-start.1 = (bf16[176,256]{1,0:T(8,128)(2,1)S(1)}, bf16[176,256]{1,0:T(8,128)(2,1)S(1)}, u32[]{:S(2)}, u32[]{:S(2)}) collective-permute-start(bf16[176,256]{1,0:T(8,128)(2,1)S(1)} %copy-done), channel_id=1, source_target_pairs={{0,16},{1,17},{2,18},{3,19},{4,20},{5,21},{6,22},{7,23},{8,24},{9,... | collective-permute-start | bytes 270344 | tf_op jit(solution)/shard_map/ppermute | solution.py:196
  22.3 4.5 %collective-permute-start = (bf16[176,256]{1,0:T(8,128)(2,1)S(1)}, bf16[176,256]{1,0:T(8,128)(2,1)S(1)}, u32[]{:S(2)}, u32[]{:S(2)}) collective-permute-start(bf16[176,256]{1,0:T(8,128)(2,1)S(1)} %copy-done), channel_id=1, source_target_pairs={{0,8},{1,9},{2,10},{3,11},{4,12},{5,13},{6,14},{7,15},{8,16},{9,17... | collective-permute-start | bytes 270344 | tf_op jit(solution)/shard_map/ppermute | solution.py:196
  26.8 0.0 collective-permute-done.2
  26.9 4.6 %collective-permute-done.1 = bf16[176,256]{1,0:T(8,128)(2,1)S(1)} collective-permute-done((bf16[176,256]{1,0:T(8,128)(2,1)S(1)}, bf16[176,256]{1,0:T(8,128)(2,1)S(1)}, u32[]{:S(2)}, u32[]{:S(2)}) %collective-permute-start.1) | collective-permute-done | bytes 90144 | tf_op jit(solution)/shard_map/ppermute | solution.py:196
  31.5 0.0 collective-permute-done
  31.5 2.7 %collective-permute-start.5 = (bf16[4,176,256]{2,1,0:T(8,128)(2,1)S(1)}, bf16[4,176,256]{2,1,0:T(8,128)(2,1)S(1)}, u32[]{:S(2)}, u32[]{:S(2)}) collective-permute-start(bf16[4,176,256]{2,1,0:T(8,128)(2,1)S(1)} %pad_maximum_fusion.refs_0_), channel_id=1, source_target_pairs={{0,6},{1,7},{2,0},{3,1},{4,2},{5,3},{6,4},{7,5},{8,14},{9,15},{10,... | collective-permute-start | bytes 1081352 | tf_op jit(solution)/shard_map/ppermute | solution.py:196
  34.3 3.0 %collective-permute-start.4 = (bf16[4,176,256]{2,1,0:T(8,128)(2,1)S(1)}, bf16[4,176,256]{2,1,0:T(8,128)(2,1)S(1)}, u32[]{:S(2)}, u32[]{:S(2)}) collective-permute-start(bf16[4,176,256]{2,1,0:T(8,128)(2,1)S(1)} %pad_maximum_fusion.refs_0_), channel_id=1, source_target_pairs={{0,4},{1,5},{2,6},{3,7},{4,0},{5,1},{6,2},{7,3},{8,12},{9,13},{10,... | collective-permute-start | bytes 1081352 | tf_op jit(solution)/shard_map/ppermute | solution.py:196
  37.3 4.0 %collective-permute-start.3 = (bf16[4,176,256]{2,1,0:T(8,128)(2,1)S(1)}, bf16[4,176,256]{2,1,0:T(8,128)(2,1)S(1)}, u32[]{:S(2)}, u32[]{:S(2)}) collective-permute-start(bf16[4,176,256]{2,1,0:T(8,128)(2,1)S(1)} %pad_maximum_fusion.refs_0_), channel_id=1, source_target_pairs={{0,2},{1,3},{2,4},{3,5},{4,6},{5,7},{6,0},{7,1},{8,10},{9,11},{10,... | collective-permute-start | bytes 1081352 | tf_op jit(solution)/shard_map/ppermute | solution.py:196
  41.3 0.0 all-to-all-done.refs_8_
  41.3 4.7 %collective-permute-start.10 = (bf16[8,176,256]{2,1,0:T(8,128)(2,1)S(1)}, bf16[8,176,256]{2,1,0:T(8,128)(2,1)S(1)}, u32[]{:S(2)}, u32[]{:S(2)}) collective-permute-start(bf16[8,176,256]{2,1,0:T(8,128)(2,1)S(1)} %all-to-all-done.refs_8_), channel_id=1, source_target_pairs={{0,256},{32,288},{64,320},{96,352},{128,384},{160,416},{192,448},{... | collective-permute-start | bytes 2162696 | tf_op jit(solution)/shard_map/ppermute | solution.py:196
  46.0 1.9 %collective-permute-start.6 = (bf16[4,176,256]{2,1,0:T(8,128)(2,1)S(1)}, bf16[4,176,256]{2,1,0:T(8,128)(2,1)S(1)}, u32[]{:S(2)}, u32[]{:S(2)}) collective-permute-start(bf16[4,176,256]{2,1,0:T(8,128)(2,1)S(1)} %pad_maximum_fusion.refs_0_), channel_id=1, source_target_pairs={{0,1},{1,0},{2,3},{3,2},{4,5},{5,4},{6,7},{7,6},{8,9},{9,8},{10,11... | collective-permute-start | bytes 1081352 | tf_op jit(solution)/shard_map/ppermute | solution.py:196
  47.9 2.5 %collective-permute-done.5.refs_3_ = bf16[4,176,256]{2,1,0:T(8,128)(2,1)S(1)} collective-permute-done((bf16[4,176,256]{2,1,0:T(8,128)(2,1)S(1)}, bf16[4,176,256]{2,1,0:T(8,128)(2,1)S(1)}, u32[]{:S(2)}, u32[]{:S(2)}) %collective-permute-start.5) | collective-permute-done | bytes 360480 | tf_op jit(solution)/shard_map/ppermute | solution.py:196
  50.5 1.9 %collective-permute-start.9 = (bf16[4,176,256]{2,1,0:T(8,128)(2,1)S(1)}, bf16[4,176,256]{2,1,0:T(8,128)(2,1)}, u32[]{:S(2)}, u32[]{:S(2)}) collective-permute-start(bf16[4,176,256]{2,1,0:T(8,128)(2,1)S(1)} %collective-permute-done.5.refs_3_), channel_id=1, source_target_pairs={{0,1},{1,0},{2,3},{3,2},{4,5},{5,4},{6,7},{7,6},{8,9},{9,8},{10,11... | collective-permute-start | bytes 1081352 | tf_op jit(solution)/shard_map/ppermute | solution.py:196
  52.4 0.0 collective-permute-done.4.refs_2_
  52.4 2.4 %collective-permute-start.8 = (bf16[4,176,256]{2,1,0:T(8,128)(2,1)S(1)}, bf16[4,176,256]{2,1,0:T(8,128)(2,1)}, u32[]{:S(2)}, u32[]{:S(2)}) collective-permute-start(bf16[4,176,256]{2,1,0:T(8,128)(2,1)S(1)} %collective-permute-done.4.refs_2_), channel_id=1, source_target_pairs={{0,1},{1,0},{2,3},{3,2},{4,5},{5,4},{6,7},{7,6},{8,9},{9,8},{10,11... | collective-permute-start | bytes 1081352 | tf_op jit(solution)/shard_map/ppermute | solution.py:196
  54.8 0.0 collective-permute-done.3.refs_1_
  54.8 1.9 %collective-permute-start.7 = (bf16[4,176,256]{2,1,0:T(8,128)(2,1)S(1)}, bf16[4,176,256]{2,1,0:T(8,128)(2,1)}, u32[]{:S(2)}, u32[]{:S(2)}) collective-permute-start(bf16[4,176,256]{2,1,0:T(8,128)(2,1)S(1)} %collective-permute-done.3.refs_1_), channel_id=1, source_target_pairs={{0,1},{1,0},{2,3},{3,2},{4,5},{5,4},{6,7},{7,6},{8,9},{9,8},{10,11... | collective-permute-start | bytes 1081352 | tf_op jit(solution)/shard_map/ppermute | solution.py:196
  57.4 0.0 copy-start.1
  57.4 0.7 copy-done.1
  58.1 0.0 collective-permute-done.6.refs_4_
  58.1 0.0 collective-permute-done.9.refs_7_
  58.1 0.0 collective-permute-done.8.refs_6_
  58.1 0.4 collective-permute-done.7.refs_5_
  58.5 2.3 %collective-permute-done.10.refs_9_ = bf16[8,176,256]{2,1,0:T(8,128)(2,1)S(1)} collective-permute-done((bf16[8,176,256]{2,1,0:T(8,128)(2,1)S(1)}, bf16[8,176,256]{2,1,0:T(8,128)(2,1)S(1)}, u32[]{:S(2)}, u32[]{:S(2)}) %collective-permute-start.10) | collective-permute-done | bytes 720928 | tf_op jit(solution)/shard_map/ppermute | solution.py:196
  60.8 22.8 %tile_products.1 = (bf16[32,32,256]{2,1,0:T(8,128)(2,1)}, f32[8,32,256]{2,1,0:T(8,128)S(1)}, bf16[8,32,256]{2,1,0:T(8,128)(2,1)}) custom-call(s32[4,128]{1,0:T(4,128)S(1)} %pad_add_fusion.slots_ref, s32[1,1]{1,0:T(1,128)} %copy.6.count_ref, bf16[4,176,256]{2,1,0:T(8,128)(2,1)S(1)} %pad_maximum_fusion.refs_0_, ...), custom_call_target="tpu_custom_call" | custom-call | tf_op jit(solution)/shard_map/tile_products/pallas_call | solution.py:164
  83.6 1.9 %collective-permute-start.11 = (bf16[8,32,256]{2,1,0:T(8,128)(2,1)}, bf16[8,32,256]{2,1,0:T(8,128)(2,1)S(1)}, u32[]{:S(2)}, u32[]{:S(2)}) collective-permute-start(bf16[8,32,256]{2,1,0:T(8,128)(2,1)} %get-tuple-element.14), channel_id=1, source_target_pairs={{0,256},{32,288},{64,320},{96,352},{128,384},{160,416},{192,448},{... | collective-permute-start | bytes 393224 | tf_op jit(solution)/shard_map/ppermute | solution.py:196
  85.5 7.5 %all-to-all-start.1 = ((bf16[32,32,256]{2,1,0:T(8,128)(2,1)}), bf16[32,32,256]{2,1,0:T(8,128)(2,1)S(1)}, u32[]{:S(2)}, u32[]{:S(2)}) async-start(bf16[32,32,256]{2,1,0:T(8,128)(2,1)} %get-tuple-element.12), calls=%async_computation.1 | async-start | bytes 1048576 | tf_op jit(solution)/shard_map/all_to_all | solution.py:268
  93.0 0.0 collective-permute-done.11
  93.1 2.9 %collective-permute-start.12 = (bf16[2,32,256]{2,1,0:T(8,128)(2,1)S(1)}, bf16[2,32,256]{2,1,0:T(8,128)(2,1)S(1)}, u32[]{:S(2)}, u32[]{:S(2)}) collective-permute-start(bf16[2,32,256]{2,1,0:T(8,128)(2,1)S(1)} %get-tuple-element.17), channel_id=1, source_target_pairs={{0,64},{32,96},{64,0},{96,32},{128,192},{160,224},{192,128},{224,1... | collective-permute-start | bytes 98312 | tf_op jit(solution)/shard_map/ppermute | solution.py:196
  96.0 2.3 %collective-permute-start.14 = (bf16[2,32,256]{2,1,0:T(8,128)(2,1)S(1)}, bf16[2,32,256]{2,1,0:T(8,128)(2,1)S(1)}, u32[]{:S(2)}, u32[]{:S(2)}) collective-permute-start(bf16[2,32,256]{2,1,0:T(8,128)(2,1)S(1)} %get-tuple-element.18), channel_id=1, source_target_pairs={{0,192},{32,224},{64,128},{96,160},{128,64},{160,96},{192,0},{224,... | collective-permute-start | bytes 98312 | tf_op jit(solution)/shard_map/ppermute | solution.py:196
  98.2 7.1 %collective-permute-start.13 = (bf16[2,32,256]{2,1,0:T(8,128)(2,1)S(1)}, bf16[2,32,256]{2,1,0:T(8,128)(2,1)S(1)}, u32[]{:S(2)}, u32[]{:S(2)}) collective-permute-start(bf16[2,32,256]{2,1,0:T(8,128)(2,1)S(1)} %get-tuple-element.19), channel_id=1, source_target_pairs={{0,128},{32,160},{64,192},{96,224},{128,0},{160,32},{192,64},{224,... | collective-permute-start | bytes 98312 | tf_op jit(solution)/shard_map/ppermute | solution.py:196
  105.3 0.0 collective-permute-done.12
  105.3 0.0 collective-permute-done.14
  105.3 2.6 %collective-permute-done.13 = bf16[2,32,256]{2,1,0:T(8,128)(2,1)S(1)} collective-permute-done((bf16[2,32,256]{2,1,0:T(8,128)(2,1)S(1)}, bf16[2,32,256]{2,1,0:T(8,128)(2,1)S(1)}, u32[]{:S(2)}, u32[]{:S(2)}) %collective-permute-start.13) | collective-permute-done | bytes 32800 | tf_op jit(solution)/shard_map/ppermute | solution.py:196
  108.0 2.1 %collective-permute-start.15 = (f32[32,256]{1,0:T(8,128)S(1)}, f32[32,256]{1,0:T(8,128)S(1)}, u32[]{:S(2)}, u32[]{:S(2)}) collective-permute-start(f32[32,256]{1,0:T(8,128)S(1)} %slice_bitcast_fusion), channel_id=1, source_target_pairs={{0,32},{32,0},{64,96},{96,64},{128,160},{160,128},{192,224},{224,1... | collective-permute-start | bytes 98312 | tf_op jit(solution)/shard_map/ppermute | solution.py:196
  110.0 0.7 all-to-all-done.1
  110.7 0.1 convert_reduce_fusion
  110.8 3.0 %collective-permute-done.15 = f32[32,256]{1,0:T(8,128)S(1)} collective-permute-done((f32[32,256]{1,0:T(8,128)S(1)}, f32[32,256]{1,0:T(8,128)S(1)}, u32[]{:S(2)}, u32[]{:S(2)}) %collective-permute-start.15) | collective-permute-done | bytes 32800 | tf_op jit(solution)/shard_map/ppermute | solution.py:196
  113.8 0.6 fusion.1
  (7 shorter events, 0.1 us)
Async XLA Ops:
  1.9 10.5 %copy-start = (bf16[176,256]{1,0:T(8,128)(2,1)S(1)}, bf16[176,256]{1,0:T(8,128)(2,1)}, u32[]{:S(2)}) copy-start(bf16[176,256]{1,0:T(8,128)(2,1)} %get-tuple-element.10) | copy-start | bytes 270340
  1.9 39.4 %all-to-all-start = ((bf16[8,176,256]{2,1,0:T(8,128)(2,1)}), bf16[8,176,256]{2,1,0:T(8,128)(2,1)S(1)}, u32[]{:S(2)}, u32[]{:S(2)}) async-start(bf16[8,176,256]{2,1,0:T(8,128)(2,1)} %get-tuple-element.11), calls=%async_computation | async-start | bytes 1441792 | tf_op jit(solution)/shard_map/all_to_all | solution.py:225
  12.3 14.5 %collective-permute-start.2 = (bf16[176,256]{1,0:T(8,128)(2,1)S(1)}, bf16[176,256]{1,0:T(8,128)(2,1)S(1)}, u32[]{:S(2)}, u32[]{:S(2)}) collective-permute-start(bf16[176,256]{1,0:T(8,128)(2,1)S(1)} %copy-done), channel_id=1, source_target_pairs={{0,24},{1,25},{2,26},{3,27},{4,28},{5,29},{6,30},{7,31},{8,0},{9,1... | collective-permute-start | bytes 270344 | tf_op jit(solution)/shard_map/ppermute | solution.py:196
  18.5 12.9 %collective-permute-start.1 = (bf16[176,256]{1,0:T(8,128)(2,1)S(1)}, bf16[176,256]{1,0:T(8,128)(2,1)S(1)}, u32[]{:S(2)}, u32[]{:S(2)}) collective-permute-start(bf16[176,256]{1,0:T(8,128)(2,1)S(1)} %copy-done), channel_id=1, source_target_pairs={{0,16},{1,17},{2,18},{3,19},{4,20},{5,21},{6,22},{7,23},{8,24},{9,... | collective-permute-start | bytes 270344 | tf_op jit(solution)/shard_map/ppermute | solution.py:196
  22.3 9.1 %collective-permute-start = (bf16[176,256]{1,0:T(8,128)(2,1)S(1)}, bf16[176,256]{1,0:T(8,128)(2,1)S(1)}, u32[]{:S(2)}, u32[]{:S(2)}) collective-permute-start(bf16[176,256]{1,0:T(8,128)(2,1)S(1)} %copy-done), channel_id=1, source_target_pairs={{0,8},{1,9},{2,10},{3,11},{4,12},{5,13},{6,14},{7,15},{8,16},{9,17... | collective-permute-start | bytes 270344 | tf_op jit(solution)/shard_map/ppermute | solution.py:196
  31.5 18.9 %collective-permute-start.5 = (bf16[4,176,256]{2,1,0:T(8,128)(2,1)S(1)}, bf16[4,176,256]{2,1,0:T(8,128)(2,1)S(1)}, u32[]{:S(2)}, u32[]{:S(2)}) collective-permute-start(bf16[4,176,256]{2,1,0:T(8,128)(2,1)S(1)} %pad_maximum_fusion.refs_0_), channel_id=1, source_target_pairs={{0,6},{1,7},{2,0},{3,1},{4,2},{5,3},{6,4},{7,5},{8,14},{9,15},{10,... | collective-permute-start | bytes 1081352 | tf_op jit(solution)/shard_map/ppermute | solution.py:196
  34.3 18.1 %collective-permute-start.4 = (bf16[4,176,256]{2,1,0:T(8,128)(2,1)S(1)}, bf16[4,176,256]{2,1,0:T(8,128)(2,1)S(1)}, u32[]{:S(2)}, u32[]{:S(2)}) collective-permute-start(bf16[4,176,256]{2,1,0:T(8,128)(2,1)S(1)} %pad_maximum_fusion.refs_0_), channel_id=1, source_target_pairs={{0,4},{1,5},{2,6},{3,7},{4,0},{5,1},{6,2},{7,3},{8,12},{9,13},{10,... | collective-permute-start | bytes 1081352 | tf_op jit(solution)/shard_map/ppermute | solution.py:196
  37.3 17.5 %collective-permute-start.3 = (bf16[4,176,256]{2,1,0:T(8,128)(2,1)S(1)}, bf16[4,176,256]{2,1,0:T(8,128)(2,1)S(1)}, u32[]{:S(2)}, u32[]{:S(2)}) collective-permute-start(bf16[4,176,256]{2,1,0:T(8,128)(2,1)S(1)} %pad_maximum_fusion.refs_0_), channel_id=1, source_target_pairs={{0,2},{1,3},{2,4},{3,5},{4,6},{5,7},{6,0},{7,1},{8,10},{9,11},{10,... | collective-permute-start | bytes 1081352 | tf_op jit(solution)/shard_map/ppermute | solution.py:196
  41.3 19.5 %collective-permute-start.10 = (bf16[8,176,256]{2,1,0:T(8,128)(2,1)S(1)}, bf16[8,176,256]{2,1,0:T(8,128)(2,1)S(1)}, u32[]{:S(2)}, u32[]{:S(2)}) collective-permute-start(bf16[8,176,256]{2,1,0:T(8,128)(2,1)S(1)} %all-to-all-done.refs_8_), channel_id=1, source_target_pairs={{0,256},{32,288},{64,320},{96,352},{128,384},{160,416},{192,448},{... | collective-permute-start | bytes 2162696 | tf_op jit(solution)/shard_map/ppermute | solution.py:196
  46.0 12.1 %collective-permute-start.6 = (bf16[4,176,256]{2,1,0:T(8,128)(2,1)S(1)}, bf16[4,176,256]{2,1,0:T(8,128)(2,1)S(1)}, u32[]{:S(2)}, u32[]{:S(2)}) collective-permute-start(bf16[4,176,256]{2,1,0:T(8,128)(2,1)S(1)} %pad_maximum_fusion.refs_0_), channel_id=1, source_target_pairs={{0,1},{1,0},{2,3},{3,2},{4,5},{5,4},{6,7},{7,6},{8,9},{9,8},{10,11... | collective-permute-start | bytes 1081352 | tf_op jit(solution)/shard_map/ppermute | solution.py:196
  50.5 7.7 %collective-permute-start.9 = (bf16[4,176,256]{2,1,0:T(8,128)(2,1)S(1)}, bf16[4,176,256]{2,1,0:T(8,128)(2,1)}, u32[]{:S(2)}, u32[]{:S(2)}) collective-permute-start(bf16[4,176,256]{2,1,0:T(8,128)(2,1)S(1)} %collective-permute-done.5.refs_3_), channel_id=1, source_target_pairs={{0,1},{1,0},{2,3},{3,2},{4,5},{5,4},{6,7},{7,6},{8,9},{9,8},{10,11... | collective-permute-start | bytes 1081352 | tf_op jit(solution)/shard_map/ppermute | solution.py:196
  52.4 5.8 %collective-permute-start.8 = (bf16[4,176,256]{2,1,0:T(8,128)(2,1)S(1)}, bf16[4,176,256]{2,1,0:T(8,128)(2,1)}, u32[]{:S(2)}, u32[]{:S(2)}) collective-permute-start(bf16[4,176,256]{2,1,0:T(8,128)(2,1)S(1)} %collective-permute-done.4.refs_2_), channel_id=1, source_target_pairs={{0,1},{1,0},{2,3},{3,2},{4,5},{5,4},{6,7},{7,6},{8,9},{9,8},{10,11... | collective-permute-start | bytes 1081352 | tf_op jit(solution)/shard_map/ppermute | solution.py:196
  54.8 3.7 %collective-permute-start.7 = (bf16[4,176,256]{2,1,0:T(8,128)(2,1)S(1)}, bf16[4,176,256]{2,1,0:T(8,128)(2,1)}, u32[]{:S(2)}, u32[]{:S(2)}) collective-permute-start(bf16[4,176,256]{2,1,0:T(8,128)(2,1)S(1)} %collective-permute-done.3.refs_1_), channel_id=1, source_target_pairs={{0,1},{1,0},{2,3},{3,2},{4,5},{5,4},{6,7},{7,6},{8,9},{9,8},{10,11... | collective-permute-start | bytes 1081352 | tf_op jit(solution)/shard_map/ppermute | solution.py:196
  57.4 0.7 copy-start.1
  83.6 9.4 %collective-permute-start.11 = (bf16[8,32,256]{2,1,0:T(8,128)(2,1)}, bf16[8,32,256]{2,1,0:T(8,128)(2,1)S(1)}, u32[]{:S(2)}, u32[]{:S(2)}) collective-permute-start(bf16[8,32,256]{2,1,0:T(8,128)(2,1)} %get-tuple-element.14), channel_id=1, source_target_pairs={{0,256},{32,288},{64,320},{96,352},{128,384},{160,416},{192,448},{... | collective-permute-start | bytes 393224 | tf_op jit(solution)/shard_map/ppermute | solution.py:196
  85.5 25.2 %all-to-all-start.1 = ((bf16[32,32,256]{2,1,0:T(8,128)(2,1)}), bf16[32,32,256]{2,1,0:T(8,128)(2,1)S(1)}, u32[]{:S(2)}, u32[]{:S(2)}) async-start(bf16[32,32,256]{2,1,0:T(8,128)(2,1)} %get-tuple-element.12), calls=%async_computation.1 | async-start | bytes 1048576 | tf_op jit(solution)/shard_map/all_to_all | solution.py:268
  93.1 12.2 %collective-permute-start.12 = (bf16[2,32,256]{2,1,0:T(8,128)(2,1)S(1)}, bf16[2,32,256]{2,1,0:T(8,128)(2,1)S(1)}, u32[]{:S(2)}, u32[]{:S(2)}) collective-permute-start(bf16[2,32,256]{2,1,0:T(8,128)(2,1)S(1)} %get-tuple-element.17), channel_id=1, source_target_pairs={{0,64},{32,96},{64,0},{96,32},{128,192},{160,224},{192,128},{224,1... | collective-permute-start | bytes 98312 | tf_op jit(solution)/shard_map/ppermute | solution.py:196
  96.0 9.4 %collective-permute-start.14 = (bf16[2,32,256]{2,1,0:T(8,128)(2,1)S(1)}, bf16[2,32,256]{2,1,0:T(8,128)(2,1)S(1)}, u32[]{:S(2)}, u32[]{:S(2)}) collective-permute-start(bf16[2,32,256]{2,1,0:T(8,128)(2,1)S(1)} %get-tuple-element.18), channel_id=1, source_target_pairs={{0,192},{32,224},{64,128},{96,160},{128,64},{160,96},{192,0},{224,... | collective-permute-start | bytes 98312 | tf_op jit(solution)/shard_map/ppermute | solution.py:196
  98.2 9.7 %collective-permute-start.13 = (bf16[2,32,256]{2,1,0:T(8,128)(2,1)S(1)}, bf16[2,32,256]{2,1,0:T(8,128)(2,1)S(1)}, u32[]{:S(2)}, u32[]{:S(2)}) collective-permute-start(bf16[2,32,256]{2,1,0:T(8,128)(2,1)S(1)} %get-tuple-element.19), channel_id=1, source_target_pairs={{0,128},{32,160},{64,192},{96,224},{128,0},{160,32},{192,64},{224,... | collective-permute-start | bytes 98312 | tf_op jit(solution)/shard_map/ppermute | solution.py:196
  108.0 5.8 %collective-permute-start.15 = (f32[32,256]{1,0:T(8,128)S(1)}, f32[32,256]{1,0:T(8,128)S(1)}, u32[]{:S(2)}, u32[]{:S(2)}) collective-permute-start(f32[32,256]{1,0:T(8,128)S(1)} %slice_bitcast_fusion), channel_id=1, source_target_pairs={{0,32},{32,0},{64,96},{96,64},{128,160},{160,128},{192,224},{224,1... | collective-permute-start | bytes 98312 | tf_op jit(solution)/shard_map/ppermute | solution.py:196

commit v7 on v6

--- a/solution.py
+++ b/solution.py
@@ -116,24 +116,25 @@
         left, right = left_ref[slots_ref[0, slot]], right_ref[slots_ref[1, slot]]
         return jnp.dot(left, right, preferred_element_type=jnp.float32)
 
-    def products(slot, score):
-        block = jnp.exp2(score * POWER).astype(jnp.bfloat16)
+    def weights(score):
+        return jnp.exp2(score * POWER).astype(jnp.bfloat16)
+
+    def add_products(slot, block):
         forward = jnp.dot(block, turned_ref[slots_ref[1, slot]], preferred_element_type=jnp.float32)
         mirror = jnp.dot(row_vecs_ref[slots_ref[0, slot]], block, preferred_element_type=jnp.float32)
-        return slots_ref[2, slot], slots_ref[3, slot], forward, mirror
+        fsum_ref[slots_ref[2, slot]] += forward
+        msum_ref[slots_ref[3, slot]] += mirror
 
     @pl.loop(0, lax.div(count_ref[0, 0] + (UNROLL - 1), UNROLL))
     def _(group):
-        done = []
-        score = scores(group * UNROLL)
-        for step in range(UNROLL):
-            slot = group * UNROLL + step
-            following = scores(slot + 1) if step + 1 < UNROLL else None
-            done.append(products(slot, score))
-            score = following
-        for forward_at, mirror_at, forward, mirror in done:
-            fsum_ref[forward_at] += forward
-            msum_ref[mirror_at] += mirror
+        first = group * UNROLL
+        score, block = scores(first), None
+        for step in range(1, UNROLL + 2):
+            following = scores(first + step) if step < UNROLL else None
+            ready = weights(score) if score is not None else None
+            if block is not None:
+                add_products(first + step - 2, block)
+            score, block = following, ready
 
     lane_group = lax.div(lane, VECS)
 

time: 116 us -> 114 us (0.983)
  Pallas kernels: 24.7 us -> 21.5 us
    pallas_call x1, Pallas kernels: 22.8 us -> 19.6 us  [tile_products(): pl.pallas_call(tiles_kernel, out_shape=(jax.ShapeDtypeStruct((row_span, V...]
    ppermute x16, waiting for transfers between devices: 15.5 us -> 16.7 us  [moved(): return lax.ppermute(value, axis, pairs)]
where the time goes in v7:
time: 114 us; the launch traced here: 112 us
  starting transfers between devices  71.3 us (63%)
  Pallas kernels  21.5 us (19%)
  waiting for transfers between devices  16.7 us (15%)
    ppermute x16, starting transfers between devices, moved(): return lax.ppermute(value, axis, pairs)  53.9 us
    pallas_call x1, Pallas kernels, tile_products(): pl.pallas_call(tiles_kernel, out_shape=(jax.ShapeDtypeStruct((row_span, V...  19.6 us
    ppermute x16, waiting for transfers between devices, moved(): return lax.ppermute(value, axis, pairs)  16.7 us
    all_to_all x1, starting transfers between devices, grouped_all_to_all(): lax.all_to_all(value, axis, 0, 0, axis_index_groups=list(groups.values())...  10.4 us
    all_to_all x1, starting transfers between devices, body(): forward = lax.all_to_all(forward, 'col', 0, 0, tiled=True)  6.93 us
  transfers between devices with their start and end apart: 18, of which 7 were waited for; matrix products, arithmetic and copies ran while one was open for 0% of the time, Pallas kernels for 0%

profile of v7, /device:TPU:6, one launch (start us, length us, event | category | flops | bytes accessed | tf_op | source)
XLA Modules:
  0.0 112.0 jit_solution(13306905731513662566)
XLA Ops:
  0.0 1.9 %pack_blocks.1 = (bf16[176,256]{1,0:T(8,128)(2,1)}, bf16[8,176,256]{2,1,0:T(8,128)(2,1)}) custom-call(bf16[256,128]{1,0:T(8,128)(2,1)} %feat_ref.1, bf16[256]{0:T(256)(128)(2,1)} %scale_ref.1, f32[32,256]{1,0:T(8,128)} %vec_ref.1), custom_call_target="tpu_custom_call" | custom-call | tf_op jit(solution)/shard_map/pack_blocks/pallas_call | solution.py:64
  1.9 0.0 copy-start
  1.9 10.4 %all-to-all-start = ((bf16[8,176,256]{2,1,0:T(8,128)(2,1)}), bf16[8,176,256]{2,1,0:T(8,128)(2,1)S(1)}, u32[]{:S(2)}, u32[]{:S(2)}) async-start(bf16[8,176,256]{2,1,0:T(8,128)(2,1)} %get-tuple-element.11), calls=%async_computation | async-start | bytes 1441792 | tf_op jit(solution)/shard_map/all_to_all | solution.py:226
  12.3 0.0 copy-done
  12.3 6.2 %collective-permute-start.2 = (bf16[176,256]{1,0:T(8,128)(2,1)S(1)}, bf16[176,256]{1,0:T(8,128)(2,1)S(1)}, u32[]{:S(2)}, u32[]{:S(2)}) collective-permute-start(bf16[176,256]{1,0:T(8,128)(2,1)S(1)} %copy-done), channel_id=1, source_target_pairs={{0,24},{1,25},{2,26},{3,27},{4,28},{5,29},{6,30},{7,31},{8,0},{9,1... | collective-permute-start | bytes 270344 | tf_op jit(solution)/shard_map/ppermute | solution.py:197
  18.5 3.8 %collective-permute-start.1 = (bf16[176,256]{1,0:T(8,128)(2,1)S(1)}, bf16[176,256]{1,0:T(8,128)(2,1)S(1)}, u32[]{:S(2)}, u32[]{:S(2)}) collective-permute-start(bf16[176,256]{1,0:T(8,128)(2,1)S(1)} %copy-done), channel_id=1, source_target_pairs={{0,16},{1,17},{2,18},{3,19},{4,20},{5,21},{6,22},{7,23},{8,24},{9,... | collective-permute-start | bytes 270344 | tf_op jit(solution)/shard_map/ppermute | solution.py:197
  22.3 4.5 %collective-permute-start = (bf16[176,256]{1,0:T(8,128)(2,1)S(1)}, bf16[176,256]{1,0:T(8,128)(2,1)S(1)}, u32[]{:S(2)}, u32[]{:S(2)}) collective-permute-start(bf16[176,256]{1,0:T(8,128)(2,1)S(1)} %copy-done), channel_id=1, source_target_pairs={{0,8},{1,9},{2,10},{3,11},{4,12},{5,13},{6,14},{7,15},{8,16},{9,17... | collective-permute-start | bytes 270344 | tf_op jit(solution)/shard_map/ppermute | solution.py:197
  26.8 0.0 collective-permute-done.2
  26.9 4.6 %collective-permute-done.1 = bf16[176,256]{1,0:T(8,128)(2,1)S(1)} collective-permute-done((bf16[176,256]{1,0:T(8,128)(2,1)S(1)}, bf16[176,256]{1,0:T(8,128)(2,1)S(1)}, u32[]{:S(2)}, u32[]{:S(2)}) %collective-permute-start.1) | collective-permute-done | bytes 90144 | tf_op jit(solution)/shard_map/ppermute | solution.py:197
  31.5 0.0 collective-permute-done
  31.5 2.7 %collective-permute-start.5 = (bf16[4,176,256]{2,1,0:T(8,128)(2,1)S(1)}, bf16[4,176,256]{2,1,0:T(8,128)(2,1)S(1)}, u32[]{:S(2)}, u32[]{:S(2)}) collective-permute-start(bf16[4,176,256]{2,1,0:T(8,128)(2,1)S(1)} %pad_maximum_fusion.refs_0_), channel_id=1, source_target_pairs={{0,6},{1,7},{2,0},{3,1},{4,2},{5,3},{6,4},{7,5},{8,14},{9,15},{10,... | collective-permute-start | bytes 1081352 | tf_op jit(solution)/shard_map/ppermute | solution.py:197
  34.3 3.0 %collective-permute-start.4 = (bf16[4,176,256]{2,1,0:T(8,128)(2,1)S(1)}, bf16[4,176,256]{2,1,0:T(8,128)(2,1)S(1)}, u32[]{:S(2)}, u32[]{:S(2)}) collective-permute-start(bf16[4,176,256]{2,1,0:T(8,128)(2,1)S(1)} %pad_maximum_fusion.refs_0_), channel_id=1, source_target_pairs={{0,4},{1,5},{2,6},{3,7},{4,0},{5,1},{6,2},{7,3},{8,12},{9,13},{10,... | collective-permute-start | bytes 1081352 | tf_op jit(solution)/shard_map/ppermute | solution.py:197
  37.3 4.0 %collective-permute-start.3 = (bf16[4,176,256]{2,1,0:T(8,128)(2,1)S(1)}, bf16[4,176,256]{2,1,0:T(8,128)(2,1)S(1)}, u32[]{:S(2)}, u32[]{:S(2)}) collective-permute-start(bf16[4,176,256]{2,1,0:T(8,128)(2,1)S(1)} %pad_maximum_fusion.refs_0_), channel_id=1, source_target_pairs={{0,2},{1,3},{2,4},{3,5},{4,6},{5,7},{6,0},{7,1},{8,10},{9,11},{10,... | collective-permute-start | bytes 1081352 | tf_op jit(solution)/shard_map/ppermute | solution.py:197
  41.3 0.0 all-to-all-done.refs_8_
  41.3 4.7 %collective-permute-start.10 = (bf16[8,176,256]{2,1,0:T(8,128)(2,1)S(1)}, bf16[8,176,256]{2,1,0:T(8,128)(2,1)S(1)}, u32[]{:S(2)}, u32[]{:S(2)}) collective-permute-start(bf16[8,176,256]{2,1,0:T(8,128)(2,1)S(1)} %all-to-all-done.refs_8_), channel_id=1, source_target_pairs={{0,256},{32,288},{64,320},{96,352},{128,384},{160,416},{192,448},{... | collective-permute-start | bytes 2162696 | tf_op jit(solution)/shard_map/ppermute | solution.py:197
  46.0 1.9 %collective-permute-start.6 = (bf16[4,176,256]{2,1,0:T(8,128)(2,1)S(1)}, bf16[4,176,256]{2,1,0:T(8,128)(2,1)S(1)}, u32[]{:S(2)}, u32[]{:S(2)}) collective-permute-start(bf16[4,176,256]{2,1,0:T(8,128)(2,1)S(1)} %pad_maximum_fusion.refs_0_), channel_id=1, source_target_pairs={{0,1},{1,0},{2,3},{3,2},{4,5},{5,4},{6,7},{7,6},{8,9},{9,8},{10,11... | collective-permute-start | bytes 1081352 | tf_op jit(solution)/shard_map/ppermute | solution.py:197
  47.9 2.5 %collective-permute-done.5.refs_3_ = bf16[4,176,256]{2,1,0:T(8,128)(2,1)S(1)} collective-permute-done((bf16[4,176,256]{2,1,0:T(8,128)(2,1)S(1)}, bf16[4,176,256]{2,1,0:T(8,128)(2,1)S(1)}, u32[]{:S(2)}, u32[]{:S(2)}) %collective-permute-start.5) | collective-permute-done | bytes 360480 | tf_op jit(solution)/shard_map/ppermute | solution.py:197
  50.5 1.9 %collective-permute-start.9 = (bf16[4,176,256]{2,1,0:T(8,128)(2,1)S(1)}, bf16[4,176,256]{2,1,0:T(8,128)(2,1)}, u32[]{:S(2)}, u32[]{:S(2)}) collective-permute-start(bf16[4,176,256]{2,1,0:T(8,128)(2,1)S(1)} %collective-permute-done.5.refs_3_), channel_id=1, source_target_pairs={{0,1},{1,0},{2,3},{3,2},{4,5},{5,4},{6,7},{7,6},{8,9},{9,8},{10,11... | collective-permute-start | bytes 1081352 | tf_op jit(solution)/shard_map/ppermute | solution.py:197
  52.4 0.0 collective-permute-done.4.refs_2_
  52.4 2.4 %collective-permute-start.8 = (bf16[4,176,256]{2,1,0:T(8,128)(2,1)S(1)}, bf16[4,176,256]{2,1,0:T(8,128)(2,1)}, u32[]{:S(2)}, u32[]{:S(2)}) collective-permute-start(bf16[4,176,256]{2,1,0:T(8,128)(2,1)S(1)} %collective-permute-done.4.refs_2_), channel_id=1, source_target_pairs={{0,1},{1,0},{2,3},{3,2},{4,5},{5,4},{6,7},{7,6},{8,9},{9,8},{10,11... | collective-permute-start | bytes 1081352 | tf_op jit(solution)/shard_map/ppermute | solution.py:197
  54.8 0.0 collective-permute-done.3.refs_1_
  54.8 1.9 %collective-permute-start.7 = (bf16[4,176,256]{2,1,0:T(8,128)(2,1)S(1)}, bf16[4,176,256]{2,1,0:T(8,128)(2,1)}, u32[]{:S(2)}, u32[]{:S(2)}) collective-permute-start(bf16[4,176,256]{2,1,0:T(8,128)(2,1)S(1)} %collective-permute-done.3.refs_1_), channel_id=1, source_target_pairs={{0,1},{1,0},{2,3},{3,2},{4,5},{5,4},{6,7},{7,6},{8,9},{9,8},{10,11... | collective-permute-start | bytes 1081352 | tf_op jit(solution)/shard_map/ppermute | solution.py:197
  57.4 0.0 copy-start.1
  57.4 0.7 copy-done.1
  58.1 0.0 collective-permute-done.6.refs_4_
  58.1 0.0 collective-permute-done.9.refs_7_
  58.1 0.0 collective-permute-done.8.refs_6_
  58.1 0.4 collective-permute-done.7.refs_5_
  58.5 2.3 %collective-permute-done.10.refs_9_ = bf16[8,176,256]{2,1,0:T(8,128)(2,1)S(1)} collective-permute-done((bf16[8,176,256]{2,1,0:T(8,128)(2,1)S(1)}, bf16[8,176,256]{2,1,0:T(8,128)(2,1)S(1)}, u32[]{:S(2)}, u32[]{:S(2)}) %collective-permute-start.10) | collective-permute-done | bytes 720928 | tf_op jit(solution)/shard_map/ppermute | solution.py:197
  60.8 19.6 %tile_products.1 = (bf16[32,32,256]{2,1,0:T(8,128)(2,1)}, f32[8,32,256]{2,1,0:T(8,128)S(1)}, bf16[8,32,256]{2,1,0:T(8,128)(2,1)}) custom-call(s32[4,128]{1,0:T(4,128)S(1)} %pad_add_fusion.slots_ref, s32[1,1]{1,0:T(1,128)} %copy.6.count_ref, bf16[4,176,256]{2,1,0:T(8,128)(2,1)S(1)} %pad_maximum_fusion.refs_0_, ...), custom_call_target="tpu_custom_call" | custom-call | tf_op jit(solution)/shard_map/tile_products/pallas_call | solution.py:165
  80.5 1.9 %collective-permute-start.11 = (bf16[8,32,256]{2,1,0:T(8,128)(2,1)}, bf16[8,32,256]{2,1,0:T(8,128)(2,1)S(1)}, u32[]{:S(2)}, u32[]{:S(2)}) collective-permute-start(bf16[8,32,256]{2,1,0:T(8,128)(2,1)} %get-tuple-element.14), channel_id=1, source_target_pairs={{0,256},{32,288},{64,320},{96,352},{128,384},{160,416},{192,448},{... | collective-permute-start | bytes 393224 | tf_op jit(solution)/shard_map/ppermute | solution.py:197
  82.4 6.9 %all-to-all-start.1 = ((bf16[32,32,256]{2,1,0:T(8,128)(2,1)}), bf16[32,32,256]{2,1,0:T(8,128)(2,1)S(1)}, u32[]{:S(2)}, u32[]{:S(2)}) async-start(bf16[32,32,256]{2,1,0:T(8,128)(2,1)} %get-tuple-element.12), calls=%async_computation.1 | async-start | bytes 1048576 | tf_op jit(solution)/shard_map/all_to_all | solution.py:269
  89.3 0.0 collective-permute-done.11
  89.4 4.4 %collective-permute-start.12 = (bf16[2,32,256]{2,1,0:T(8,128)(2,1)S(1)}, bf16[2,32,256]{2,1,0:T(8,128)(2,1)S(1)}, u32[]{:S(2)}, u32[]{:S(2)}) collective-permute-start(bf16[2,32,256]{2,1,0:T(8,128)(2,1)S(1)} %get-tuple-element.17), channel_id=1, source_target_pairs={{0,64},{32,96},{64,0},{96,32},{128,192},{160,224},{192,128},{224,1... | collective-permute-start | bytes 98312 | tf_op jit(solution)/shard_map/ppermute | solution.py:197
  93.9 1.9 %collective-permute-start.14 = (bf16[2,32,256]{2,1,0:T(8,128)(2,1)S(1)}, bf16[2,32,256]{2,1,0:T(8,128)(2,1)S(1)}, u32[]{:S(2)}, u32[]{:S(2)}) collective-permute-start(bf16[2,32,256]{2,1,0:T(8,128)(2,1)S(1)} %get-tuple-element.18), channel_id=1, source_target_pairs={{0,192},{32,224},{64,128},{96,160},{128,64},{160,96},{192,0},{224,... | collective-permute-start | bytes 98312 | tf_op jit(solution)/shard_map/ppermute | solution.py:197
  95.8 5.9 %collective-permute-start.13 = (bf16[2,32,256]{2,1,0:T(8,128)(2,1)S(1)}, bf16[2,32,256]{2,1,0:T(8,128)(2,1)S(1)}, u32[]{:S(2)}, u32[]{:S(2)}) collective-permute-start(bf16[2,32,256]{2,1,0:T(8,128)(2,1)S(1)} %get-tuple-element.19), channel_id=1, source_target_pairs={{0,128},{32,160},{64,192},{96,224},{128,0},{160,32},{192,64},{224,... | collective-permute-start | bytes 98312 | tf_op jit(solution)/shard_map/ppermute | solution.py:197
  101.7 0.0 collective-permute-done.12
  101.7 0.1 collective-permute-done.14
  101.8 3.7 %collective-permute-done.13 = bf16[2,32,256]{2,1,0:T(8,128)(2,1)S(1)} collective-permute-done((bf16[2,32,256]{2,1,0:T(8,128)(2,1)S(1)}, bf16[2,32,256]{2,1,0:T(8,128)(2,1)S(1)}, u32[]{:S(2)}, u32[]{:S(2)}) %collective-permute-start.13) | collective-permute-done | bytes 32800 | tf_op jit(solution)/shard_map/ppermute | solution.py:197
  105.5 2.7 %collective-permute-start.15 = (f32[32,256]{1,0:T(8,128)S(1)}, f32[32,256]{1,0:T(8,128)S(1)}, u32[]{:S(2)}, u32[]{:S(2)}) collective-permute-start(f32[32,256]{1,0:T(8,128)S(1)} %slice_bitcast_fusion), channel_id=1, source_target_pairs={{0,32},{32,0},{64,96},{96,64},{128,160},{160,128},{192,224},{224,1... | collective-permute-start | bytes 98312 | tf_op jit(solution)/shard_map/ppermute | solution.py:197
  108.3 0.0 all-to-all-done.1
  108.3 0.1 convert_reduce_fusion
  108.4 3.0 %collective-permute-done.15 = f32[32,256]{1,0:T(8,128)S(1)} collective-permute-done((f32[32,256]{1,0:T(8,128)S(1)}, f32[32,256]{1,0:T(8,128)S(1)}, u32[]{:S(2)}, u32[]{:S(2)}) %collective-permute-start.15) | collective-permute-done | bytes 32800 | tf_op jit(solution)/shard_map/ppermute | solution.py:197
  111.4 0.6 fusion.1
  (7 shorter events, 0.1 us)
Async XLA Ops:
  1.9 10.5 %copy-start = (bf16[176,256]{1,0:T(8,128)(2,1)S(1)}, bf16[176,256]{1,0:T(8,128)(2,1)}, u32[]{:S(2)}) copy-start(bf16[176,256]{1,0:T(8,128)(2,1)} %get-tuple-element.10) | copy-start | bytes 270340
  1.9 39.4 %all-to-all-start = ((bf16[8,176,256]{2,1,0:T(8,128)(2,1)}), bf16[8,176,256]{2,1,0:T(8,128)(2,1)S(1)}, u32[]{:S(2)}, u32[]{:S(2)}) async-start(bf16[8,176,256]{2,1,0:T(8,128)(2,1)} %get-tuple-element.11), calls=%async_computation | async-start | bytes 1441792 | tf_op jit(solution)/shard_map/all_to_all | solution.py:226
  12.3 14.5 %collective-permute-start.2 = (bf16[176,256]{1,0:T(8,128)(2,1)S(1)}, bf16[176,256]{1,0:T(8,128)(2,1)S(1)}, u32[]{:S(2)}, u32[]{:S(2)}) collective-permute-start(bf16[176,256]{1,0:T(8,128)(2,1)S(1)} %copy-done), channel_id=1, source_target_pairs={{0,24},{1,25},{2,26},{3,27},{4,28},{5,29},{6,30},{7,31},{8,0},{9,1... | collective-permute-start | bytes 270344 | tf_op jit(solution)/shard_map/ppermute | solution.py:197
  18.5 12.9 %collective-permute-start.1 = (bf16[176,256]{1,0:T(8,128)(2,1)S(1)}, bf16[176,256]{1,0:T(8,128)(2,1)S(1)}, u32[]{:S(2)}, u32[]{:S(2)}) collective-permute-start(bf16[176,256]{1,0:T(8,128)(2,1)S(1)} %copy-done), channel_id=1, source_target_pairs={{0,16},{1,17},{2,18},{3,19},{4,20},{5,21},{6,22},{7,23},{8,24},{9,... | collective-permute-start | bytes 270344 | tf_op jit(solution)/shard_map/ppermute | solution.py:197
  22.3 9.1 %collective-permute-start = (bf16[176,256]{1,0:T(8,128)(2,1)S(1)}, bf16[176,256]{1,0:T(8,128)(2,1)S(1)}, u32[]{:S(2)}, u32[]{:S(2)}) collective-permute-start(bf16[176,256]{1,0:T(8,128)(2,1)S(1)} %copy-done), channel_id=1, source_target_pairs={{0,8},{1,9},{2,10},{3,11},{4,12},{5,13},{6,14},{7,15},{8,16},{9,17... | collective-permute-start | bytes 270344 | tf_op jit(solution)/shard_map/ppermute | solution.py:197
  31.5 18.9 %collective-permute-start.5 = (bf16[4,176,256]{2,1,0:T(8,128)(2,1)S(1)}, bf16[4,176,256]{2,1,0:T(8,128)(2,1)S(1)}, u32[]{:S(2)}, u32[]{:S(2)}) collective-permute-start(bf16[4,176,256]{2,1,0:T(8,128)(2,1)S(1)} %pad_maximum_fusion.refs_0_), channel_id=1, source_target_pairs={{0,6},{1,7},{2,0},{3,1},{4,2},{5,3},{6,4},{7,5},{8,14},{9,15},{10,... | collective-permute-start | bytes 1081352 | tf_op jit(solution)/shard_map/ppermute | solution.py:197
  34.3 18.1 %collective-permute-start.4 = (bf16[4,176,256]{2,1,0:T(8,128)(2,1)S(1)}, bf16[4,176,256]{2,1,0:T(8,128)(2,1)S(1)}, u32[]{:S(2)}, u32[]{:S(2)}) collective-permute-start(bf16[4,176,256]{2,1,0:T(8,128)(2,1)S(1)} %pad_maximum_fusion.refs_0_), channel_id=1, source_target_pairs={{0,4},{1,5},{2,6},{3,7},{4,0},{5,1},{6,2},{7,3},{8,12},{9,13},{10,... | collective-permute-start | bytes 1081352 | tf_op jit(solution)/shard_map/ppermute | solution.py:197
  37.3 17.5 %collective-permute-start.3 = (bf16[4,176,256]{2,1,0:T(8,128)(2,1)S(1)}, bf16[4,176,256]{2,1,0:T(8,128)(2,1)S(1)}, u32[]{:S(2)}, u32[]{:S(2)}) collective-permute-start(bf16[4,176,256]{2,1,0:T(8,128)(2,1)S(1)} %pad_maximum_fusion.refs_0_), channel_id=1, source_target_pairs={{0,2},{1,3},{2,4},{3,5},{4,6},{5,7},{6,0},{7,1},{8,10},{9,11},{10,... | collective-permute-start | bytes 1081352 | tf_op jit(solution)/shard_map/ppermute | solution.py:197
  41.3 19.5 %collective-permute-start.10 = (bf16[8,176,256]{2,1,0:T(8,128)(2,1)S(1)}, bf16[8,176,256]{2,1,0:T(8,128)(2,1)S(1)}, u32[]{:S(2)}, u32[]{:S(2)}) collective-permute-start(bf16[8,176,256]{2,1,0:T(8,128)(2,1)S(1)} %all-to-all-done.refs_8_), channel_id=1, source_target_pairs={{0,256},{32,288},{64,320},{96,352},{128,384},{160,416},{192,448},{... | collective-permute-start | bytes 2162696 | tf_op jit(solution)/shard_map/ppermute | solution.py:197
  46.0 12.1 %collective-permute-start.6 = (bf16[4,176,256]{2,1,0:T(8,128)(2,1)S(1)}, bf16[4,176,256]{2,1,0:T(8,128)(2,1)S(1)}, u32[]{:S(2)}, u32[]{:S(2)}) collective-permute-start(bf16[4,176,256]{2,1,0:T(8,128)(2,1)S(1)} %pad_maximum_fusion.refs_0_), channel_id=1, source_target_pairs={{0,1},{1,0},{2,3},{3,2},{4,5},{5,4},{6,7},{7,6},{8,9},{9,8},{10,11... | collective-permute-start | bytes 1081352 | tf_op jit(solution)/shard_map/ppermute | solution.py:197
  50.5 7.7 %collective-permute-start.9 = (bf16[4,176,256]{2,1,0:T(8,128)(2,1)S(1)}, bf16[4,176,256]{2,1,0:T(8,128)(2,1)}, u32[]{:S(2)}, u32[]{:S(2)}) collective-permute-start(bf16[4,176,256]{2,1,0:T(8,128)(2,1)S(1)} %collective-permute-done.5.refs_3_), channel_id=1, source_target_pairs={{0,1},{1,0},{2,3},{3,2},{4,5},{5,4},{6,7},{7,6},{8,9},{9,8},{10,11... | collective-permute-start | bytes 1081352 | tf_op jit(solution)/shard_map/ppermute | solution.py:197
  52.4 5.8 %collective-permute-start.8 = (bf16[4,176,256]{2,1,0:T(8,128)(2,1)S(1)}, bf16[4,176,256]{2,1,0:T(8,128)(2,1)}, u32[]{:S(2)}, u32[]{:S(2)}) collective-permute-start(bf16[4,176,256]{2,1,0:T(8,128)(2,1)S(1)} %collective-permute-done.4.refs_2_), channel_id=1, source_target_pairs={{0,1},{1,0},{2,3},{3,2},{4,5},{5,4},{6,7},{7,6},{8,9},{9,8},{10,11... | collective-permute-start | bytes 1081352 | tf_op jit(solution)/shard_map/ppermute | solution.py:197
  54.8 3.7 %collective-permute-start.7 = (bf16[4,176,256]{2,1,0:T(8,128)(2,1)S(1)}, bf16[4,176,256]{2,1,0:T(8,128)(2,1)}, u32[]{:S(2)}, u32[]{:S(2)}) collective-permute-start(bf16[4,176,256]{2,1,0:T(8,128)(2,1)S(1)} %collective-permute-done.3.refs_1_), channel_id=1, source_target_pairs={{0,1},{1,0},{2,3},{3,2},{4,5},{5,4},{6,7},{7,6},{8,9},{9,8},{10,11... | collective-permute-start | bytes 1081352 | tf_op jit(solution)/shard_map/ppermute | solution.py:197
  57.4 0.7 copy-start.1
  80.5 8.9 %collective-permute-start.11 = (bf16[8,32,256]{2,1,0:T(8,128)(2,1)}, bf16[8,32,256]{2,1,0:T(8,128)(2,1)S(1)}, u32[]{:S(2)}, u32[]{:S(2)}) collective-permute-start(bf16[8,32,256]{2,1,0:T(8,128)(2,1)} %get-tuple-element.14), channel_id=1, source_target_pairs={{0,256},{32,288},{64,320},{96,352},{128,384},{160,416},{192,448},{... | collective-permute-start | bytes 393224 | tf_op jit(solution)/shard_map/ppermute | solution.py:197
  82.4 25.9 %all-to-all-start.1 = ((bf16[32,32,256]{2,1,0:T(8,128)(2,1)}), bf16[32,32,256]{2,1,0:T(8,128)(2,1)S(1)}, u32[]{:S(2)}, u32[]{:S(2)}) async-start(bf16[32,32,256]{2,1,0:T(8,128)(2,1)} %get-tuple-element.12), calls=%async_computation.1 | async-start | bytes 1048576 | tf_op jit(solution)/shard_map/all_to_all | solution.py:269
  89.4 12.2 %collective-permute-start.12 = (bf16[2,32,256]{2,1,0:T(8,128)(2,1)S(1)}, bf16[2,32,256]{2,1,0:T(8,128)(2,1)S(1)}, u32[]{:S(2)}, u32[]{:S(2)}) collective-permute-start(bf16[2,32,256]{2,1,0:T(8,128)(2,1)S(1)} %get-tuple-element.17), channel_id=1, source_target_pairs={{0,64},{32,96},{64,0},{96,32},{128,192},{160,224},{192,128},{224,1... | collective-permute-start | bytes 98312 | tf_op jit(solution)/shard_map/ppermute | solution.py:197
  93.9 7.9 %collective-permute-start.14 = (bf16[2,32,256]{2,1,0:T(8,128)(2,1)S(1)}, bf16[2,32,256]{2,1,0:T(8,128)(2,1)S(1)}, u32[]{:S(2)}, u32[]{:S(2)}) collective-permute-start(bf16[2,32,256]{2,1,0:T(8,128)(2,1)S(1)} %get-tuple-element.18), channel_id=1, source_target_pairs={{0,192},{32,224},{64,128},{96,160},{128,64},{160,96},{192,0},{224,... | collective-permute-start | bytes 98312 | tf_op jit(solution)/shard_map/ppermute | solution.py:197
  95.8 9.7 %collective-permute-start.13 = (bf16[2,32,256]{2,1,0:T(8,128)(2,1)S(1)}, bf16[2,32,256]{2,1,0:T(8,128)(2,1)S(1)}, u32[]{:S(2)}, u32[]{:S(2)}) collective-permute-start(bf16[2,32,256]{2,1,0:T(8,128)(2,1)S(1)} %get-tuple-element.19), channel_id=1, source_target_pairs={{0,128},{32,160},{64,192},{96,224},{128,0},{160,32},{192,64},{224,... | collective-permute-start | bytes 98312 | tf_op jit(solution)/shard_map/ppermute | solution.py:197
  105.5 5.8 %collective-permute-start.15 = (f32[32,256]{1,0:T(8,128)S(1)}, f32[32,256]{1,0:T(8,128)S(1)}, u32[]{:S(2)}, u32[]{:S(2)}) collective-permute-start(f32[32,256]{1,0:T(8,128)S(1)} %slice_bitcast_fusion), channel_id=1, source_target_pairs={{0,32},{32,0},{64,96},{96,64},{128,160},{160,128},{192,224},{224,1... | collective-permute-start | bytes 98312 | tf_op jit(solution)/shard_map/ppermute | solution.py:197
